TPU v7x, 32 devices: a whole 2x2x4 slice. The times are simulated.
32 devices in a mesh: wide: 8 (over z, core), narrow: 4 (over y, x).
Axes of the slice: x: 2, y: 2, z: 4, core: 2. Of those that a mesh axis runs over, the one named last changes fastest.
Arguments:
- density: float32 [128, 2, 512, 512], P(('wide', 'narrow')), may hold values from -6 to 6
- hamiltonian: bfloat16 [2, 512, 512], replicated, may hold values from -0.1875 to 0.1875
- left_operators: bfloat16 [7, 2, 512, 512], replicated, may hold values from -0.25 to 0.25
- right_operators: bfloat16 [7, 2, 512, 512], replicated, may hold values from -0.25 to 0.25
- block_mask: int32 [7, 2, 8, 8], replicated, may hold values 0 or 1
- operator_slot: int32 [7], replicated, may hold values from 0 to 6, each once
- flip_sign: int32 [7], replicated, may hold values from 0 to 1
- damping_rate: float32 [7], replicated, may hold values from 0.2 to 2
- lower_weight: float32 [7], replicated, may hold values from 0.5 to 2
Outputs:
- derivative: float32 [128, 2, 512, 512], P(('wide', 'narrow'))
Inputs may be any that keep to these rules, and one draw needn't show every extreme that they name: `operator_slot`: each of the 7 slots is used by exactly one mode.
All inputs are finite; a program needn't handle non-finite values.
Results may differ from a plain program's by a relative error of at most 0.0023.
Values may be sent and summed in bfloat16 or wider, within the bound.
No kernel may reach another device: no remote copies, remote signals or barrier semaphores. Data moves between devices by JAX's collectives and lax.ppermute only.
A program may use at most 256 MiB of HBM per device.

v0:
```python
import functools

import jax
import jax.numpy as jnp
from jax import lax
from jax.experimental import pallas as pl
from jax.experimental.pallas import tpu as pltpu
from jax.sharding import PartitionSpec as P

VMEM_LIMIT = 56 * 2**20
COST = 1.0
SMEM = pl.BlockSpec(memory_space=pltpu.SMEM)


def params(flops, moved):
    return dict(
        compiler_params=pltpu.CompilerParams(
            vmem_limit_bytes=VMEM_LIMIT, dimension_semantics=("arbitrary",)
        ),
        cost_estimate=pl.CostEstimate(
            flops=int(COST * flops), bytes_accessed=int(COST * moved), transcendentals=0
        ),
    )


def dot(a, b):
    return jnp.dot(a, b, preferred_element_type=jnp.float32)


def round_kernel(groups, density_ref, _, *out_refs):
    step = pl.program_id(0)
    first_seen = min(first for first, _, _ in groups)
    for (first, span, part), out_ref in zip(groups, out_refs):

        @pl.when((step + first_seen >= first) & (step + first_seen < first + span))
        def _(part=part, out_ref=out_ref):
            if part is None:
                out_ref[...] = density_ref[...].astype(jnp.bfloat16)
            else:
                out_ref[0, 0] = density_ref[0, part].astype(jnp.bfloat16)


def round_groups(density, groups, after):
    n = density.shape[-1]
    low = min(first for first, _, _ in groups)
    high = max(first + span for first, span, _ in groups)

    def out_spec(first, span, part):
        return pl.BlockSpec(
            (1, 2 if part is None else 1, n, n),
            lambda g: (jnp.clip(g + low - first, 0, span - 1), 0, 0, 0),
        )

    return pl.pallas_call(
        functools.partial(round_kernel, groups),
        grid=(high - low,),
        in_specs=[
            pl.BlockSpec((1, 2, n, n), lambda g: (g + low, 0, 0, 0)),
            pl.BlockSpec(memory_space=pl.ANY),
        ],
        out_specs=[out_spec(*group) for group in groups],
        out_shape=[
            jax.ShapeDtypeStruct((span, 2 if part is None else 1, n, n), jnp.bfloat16)
            for _, span, part in groups
        ],
        **params(0, 8 * n * n * (high - low) + sum(4 * n * n * span for _, span, _ in groups)),
    )(density, after)


def operator_kernel(slot_ref, mask_ref, left_ref, right_ref, ham_ref, lout_ref, rout_ref):
    step = pl.program_id(0)
    last = pl.num_programs(0) - 1
    blocks = mask_ref.shape[2]
    n = left_ref.shape[2]
    size = n // blocks

    @pl.when(step < last)
    def _():
        lane = lax.broadcasted_iota(jnp.int32, (blocks, n), 1)
        row = lax.broadcasted_iota(jnp.int32, (blocks, n), 0)
        spread = jnp.where((lane >= row * size) & (lane < (row + 1) * size), 1.0, 0.0)
        for side, (src, dst) in enumerate(((left_ref, lout_ref), (right_ref, rout_ref))):
            wide = dot(mask_ref[0, side].astype(jnp.float32), spread).astype(jnp.bfloat16)
            for i in range(blocks):
                rows = slice(i * size, (i + 1) * size)
                for part in range(2):
                    dst[0, part, rows, :] = src[0, part, rows, :] * wide[i : i + 1, :]

    @pl.when(step == last)
    def _():
        lout_ref[0, 0] = ham_ref[1]
        lout_ref[0, 1] = -ham_ref[0]
        rout_ref[0, 0] = -ham_ref[1]
        rout_ref[0, 1] = ham_ref[0]


def make_operators(left_operators, right_operators, block_mask, operator_slot, hamiltonian):
    modes, _, n, _ = left_operators.shape
    block = (1, 2, n, n)

    def slot_of(g, slot):
        return (slot[jnp.minimum(g, modes - 1)], 0, 0, 0)

    operator = pl.BlockSpec(block, slot_of)
    out = pl.BlockSpec(block, lambda g, slot: (g, 0, 0, 0))
    shape = jax.ShapeDtypeStruct((modes + 1, 2, n, n), jnp.bfloat16)
    return pl.pallas_call(
        operator_kernel,
        grid_spec=pltpu.PrefetchScalarGridSpec(
            num_scalar_prefetch=1,
            grid=(modes + 1,),
            in_specs=[
                pl.BlockSpec((1,) + block_mask.shape[1:], slot_of),
                operator,
                operator,
                pl.BlockSpec((2, n, n), lambda g, slot: (0, 0, 0)),
            ],
            out_specs=[out, out],
        ),
        out_shape=[shape, shape],
        **params(0, 16 * (modes + 1) * n * n),
    )(operator_slot, block_mask, left_operators, right_operators, hamiltonian)


def term_kernel(first, terms, fresh, coef_ref, base_ref, *refs):
    out_ref = refs[-1]
    index = first + pl.program_id(0)
    if fresh:
        rate = -coef_ref[index, coef_ref.shape[1] - 1]
        real, imag = rate * base_ref[0, 0], rate * base_ref[0, 1]
    else:
        real, imag = base_ref[0, 0], base_ref[0, 1]
    for t, (mode, part) in enumerate(terms):
        rho, left, right = refs[3 * t : 3 * t + 3]
        coef = coef_ref[index, mode]
        lr, li, rr, ri = left[0, 0], left[0, 1], right[0, 0], right[0, 1]
        if part is None:
            a, b = rho[0, 0], rho[0, 1]
            real += coef * (dot(lr, a) - dot(li, b) + dot(a, rr) - dot(b, ri))
            imag += coef * (dot(lr, b) + dot(li, a) + dot(a, ri) + dot(b, rr))
        elif part == 0:
            a = rho[0, 0]
            real += coef * (dot(lr, a) + dot(a, rr))
            imag += coef * (dot(li, a) + dot(a, ri))
        else:
            b = rho[0, 0]
            real -= coef * (dot(li, b) + dot(b, ri))
            imag += coef * (dot(lr, b) + dot(b, rr))
    out_ref[0, 0] = real
    out_ref[0, 1] = imag


def add_terms(base, coef, operators, first, span, terms, fresh=False):
    n = base.shape[-1]
    lefts, rights = operators
    specs, args = [], []
    for mode, part, array, place in terms:
        specs.append(
            pl.BlockSpec((1, 2 if part is None else 1, n, n), lambda g, place=place: (place(g), 0, 0, 0))
        )
        operator = pl.BlockSpec((1, 2, n, n), lambda g, mode=mode: (mode, 0, 0, 0))
        specs += [operator, operator]
        args += [array, lefts, rights]
    block = pl.BlockSpec((1, 2, n, n), lambda g: (first + g, 0, 0, 0))
    return pl.pallas_call(
        functools.partial(term_kernel, first, [t[:2] for t in terms], fresh),
        grid=(span,),
        in_specs=[SMEM, block] + specs,
        out_specs=block,
        out_shape=jax.ShapeDtypeStruct(base.shape, jnp.float32),
        input_output_aliases={} if fresh else {1: 0},
        **params(
            16 * n**3 * span * sum(1 if t[1] is None else 0.5 for t in terms),
            n * n * span * (16 + 4 * len(terms)) + 8 * n * n * len(terms),
        ),
    )(coef, base, *args)


def flip(value, axis, bit):
    pairs = [(source, source ^ (1 << bit)) for source in range(lax.axis_size(axis))]
    return lax.ppermute(value, axis, pairs)


def coefficients(count, modes, flip_sign, damping_rate, lower_weight):
    first = (lax.axis_index("wide") * lax.axis_size("narrow") + lax.axis_index("narrow")) * count
    indices = first + jnp.arange(count, dtype=jnp.int32)
    bits = indices[:, None] >> jnp.arange(modes, dtype=jnp.int32)[None, :] & 1
    parity = 1 - 2 * ((jnp.cumsum(bits, axis=1) - bits) % 2)
    sign = parity * (1 - 2 * flip_sign)[None, :]
    coef = sign.astype(jnp.float32) * jnp.where(bits > 0, lower_weight[None, :], jnp.float32(1.0))
    rates = jnp.sum(bits.astype(jnp.float32) * damping_rate[None, :], axis=1)
    return jnp.concatenate([coef, jnp.ones((count, 1), jnp.float32), rates[:, None]], axis=1)


def body(
    density,
    hamiltonian,
    left_operators,
    right_operators,
    block_mask,
    operator_slot,
    flip_sign,
    damping_rate,
    lower_weight,
):
    count = density.shape[0]
    modes = left_operators.shape[0]
    local_bits = count.bit_length() - 1
    narrow_bits = lax.axis_size("narrow").bit_length() - 1
    last = count - 1

    def axis_of(mode):
        if mode < local_bits + narrow_bits:
            return "narrow", mode - local_bits
        return "wide", mode - local_bits - narrow_bits

    remote = list(range(local_bits, modes))
    slow = remote[-2:][::-1]
    near = [m for m in remote[:-2] if axis_of(m) == ("wide", 0)]
    middle = [m for m in remote[:-2] if m not in near]

    half = count // 2
    pieces = [(0, half), (half, last - half)] if half else [(0, last)]
    pieces = [(first, span, None) for first, span in pieces if span > 0]
    plan = [(near, 0, count, None)]
    plan += [([m], 0, last or count, None) for m in middle[:1]]
    for place, piece in enumerate(pieces):
        plan.append((slow,) + piece)
        if place == 0:
            plan += [([m], 0, count, None) for m in middle[1:]]
            middle = middle[:1]
    plan += [([m], last, 1, None) for m in middle[:1] if last]
    plan += [([m], 0, count, None) for m in middle[1:]]
    plan += [(slow, last, 1, 0), (slow, last, 1, 1)]
    plan = [step for step in plan if step[0]]

    groups = list(dict.fromkeys([(0, count, None)] + [step[1:] for step in plan]))
    early = [step[1:] for step in plan if step[0] == slow][:1]
    late = [group for group in groups if group not in early]
    rounded = dict(zip(early, round_groups(density, early, damping_rate)))
    rounded.update(zip(late, round_groups(density, late, rounded[early[0]])))

    sent = [[flip(rounded[step[1:]], *axis_of(m)) for m in step[0]] for step in plan]
    coef = coefficients(count, modes, flip_sign, damping_rate, lower_weight)
    operators = make_operators(
        left_operators, right_operators, block_mask, operator_slot, hamiltonian
    )
    whole = rounded[(0, count, None)]

    terms = [(modes, None, whole, lambda g: g)]
    for mode in range(local_bits):
        terms.append((mode, None, whole, lambda g, mode=mode: g ^ (1 << mode)))
    if near:
        terms += [(m, None, array, lambda g: g) for m, array in zip(near, sent[0])]
        plan, sent = plan[1:], sent[1:]
    result = add_terms(density, coef, operators, 0, count, terms, fresh=True)
    for (step_modes, first, span, part), arrays in zip(plan, sent):
        terms = [(m, part, array, lambda g: g) for m, array in zip(step_modes, arrays)]
        result = add_terms(result, coef, operators, first, span, terms)
    return result


def solution(mesh):
    placed = (P(("wide", "narrow"), None, None, None), P(), P(), P(), P(), P(), P(), P(), P())
    return jax.shard_map(
        body,
        mesh=mesh,
        in_specs=placed,
        out_specs=P(("wide", "narrow"), None, None, None),
        check_vma=False,
    )
```

profile of v0, /device:TPU:0, one launch (start us, length us, event | category | flops | bytes accessed | tf_op | source)
XLA Modules:
  0.0 205.5 jit_solution(636742527406352173)
XLA Ops:
  0.0 0.0 copy-start.8
  0.0 0.0 copy-start.12
  0.0 3.3 %shard_map.91._ = bf16[2,2,512,512]{3,2,1,0:T(8,128)(2,1)} custom-call(f32[4,2,512,512]{3,2,1,0:T(8,128)} %base_ref.1, f32[7]{0:T(128)} %_.1), custom_call_target="tpu_custom_call" | custom-call | bytes 6291456 | tf_op jit(solution)/shard_map/pallas_call | solution.py:54
  3.3 0.0 copy-start
  3.3 8.4 %shard_map.92 = (bf16[4,2,512,512]{3,2,1,0:T(8,128)(2,1)}, bf16[3,2,512,512]{3,2,1,0:T(8,128)(2,1)}, bf16[1,2,512,512]{3,2,1,0:T(8,128)(2,1)}, bf16[1,2,512,512]...) custom-call(f32[4,2,512,512]{3,2,1,0:T(8,128)} %base_ref.1, ...), custom_call_target="tpu_custom_call" | custom-call | bytes 19922944 | tf_op jit(solution)/shard_map/pallas_call | solution.py:54
  11.7 0.5 collective-permute-start
  12.1 0.0 copy-done
  12.1 3.7 %collective-permute-start.2 = (bf16[2,2,512,512]{3,2,1,0:T(8,128)(2,1)S(1)}, bf16[2,2,512,512]{3,2,1,0:T(8,128)(2,1)}, u32[]{:S(2)}, u32[]{:S(2)}) collective-permute-start(bf16[2,2,512,512]{3,2,1,0:T(8,128)(2,1)S(1)} %copy-done), channel_id=1, source_target_pairs={{0,16},{4,20},{8,24},{12,28},{16,0},{20,4},{24,8},{28,12},{1,17},{... | collective-permute-start | bytes 6291464 | tf_op jit(solution)/shard_map/ppermute | solution.py:181
  15.8 1.6 collective-permute-start.3
  17.4 1.5 collective-permute-start.4
  18.9 1.5 collective-permute-start.1
  20.4 0.1 shift-right-arithmetic_and_fusion
  20.5 0.2 reduce_window_sum.11
  20.6 0.0 copy-done.12
  20.7 0.0 copy-done.8
  20.7 0.0 copy-done.9
  20.7 0.2 fusion.5
  20.9 0.1 copy.17
  20.9 0.1 pad.1.clone
  21.0 15.4 %shard_map.93 = (bf16[8,2,512,512]{3,2,1,0:T(8,128)(2,1)}, bf16[8,2,512,512]{3,2,1,0:T(8,128)(2,1)}) custom-call(s32[7]{0:T(128)} %slot_ref.1, s32[7,2,8,8]{3,2,1,0:T(8,128)} %mask_ref.1, bf16[7,2,512,512]{3,2,1,0:T(8,128)(2,1)} %left_ref.1, bf16[7,2,512,512]{3,2,1,0:T(8,128)(2,1)} %right_ref.1, bf16[2,512,512]{2,1,0:T(8,128)(2,1)} %ham_ref.1), custom_call_target="tpu_custom_call" | custom-call | bytes 33554432 | tf_op jit(solution)/shard_map/pallas_call | solution.py:107
  36.4 0.7 pad_maximum_fusion.coef_ref
  37.0 0.0 collective-permute-done.refs_9_
  37.0 0.3 collective-permute-start.5
  37.4 43.5 %shard_map.94.base_ref = f32[4,2,512,512]{3,2,1,0:T(8,128)} custom-call(f32[4,9]{1,0:T(4,128)} %pad_maximum_fusion.coef_ref, f32[4,2,512,512]{3,2,1,0:T(8,128)} %base_ref.1, bf16[4,2,512,512]{3,2,1,0:T(8,128)(2,1)} %get-tuple-element.13.refs_0_.refs_3_.refs_6_, bf16[8,2,512,512]{3,2,1,0:T(8,128)(2,1)} %get-tuple-element.14.refs_1_.refs_4_.refs_7_.refs_10_, ...), custom_call_target="tpu_custom_call" | custom-call | flops 34359738368 | bytes 41943040 | tf_op jit(solution)/shard_map/pallas_call | solution.py:165
  80.9 7.9 %collective-permute-done.1.refs_0_ = bf16[3,2,512,512]{3,2,1,0:T(8,128)(2,1)} collective-permute-done((bf16[3,2,512,512]{3,2,1,0:T(8,128)(2,1)}, bf16[3,2,512,512]{3,2,1,0:T(8,128)(2,1)}, u32[]{:S(2)}, u32[]{:S(2)}) %collective-permute-start.1) | collective-permute-done | bytes 3145760 | tf_op jit(solution)/shard_map/ppermute | solution.py:181
  88.8 0.4 collective-permute-start.6
  89.3 11.2 %shard_map.95.base_ref = f32[4,2,512,512]{3,2,1,0:T(8,128)} custom-call(f32[4,9]{1,0:T(4,128)} %pad_maximum_fusion.coef_ref, f32[4,2,512,512]{3,2,1,0:T(8,128)} %shard_map.94.base_ref, bf16[3,2,512,512]{3,2,1,0:T(8,128)(2,1)} %collective-permute-done.1.refs_0_, ...), custom_call_target="tpu_custom_call", output_to_operand_aliasing={{}: (1, {})} | custom-call | flops 6442450944 | bytes 17825792 | tf_op jit(solution)/shard_map/pallas_call | solution.py:165
  100.4 7.0 %collective-permute-done.2.refs_0_ = bf16[2,2,512,512]{3,2,1,0:T(8,128)(2,1)} collective-permute-done((bf16[2,2,512,512]{3,2,1,0:T(8,128)(2,1)S(1)}, bf16[2,2,512,512]{3,2,1,0:T(8,128)(2,1)}, u32[]{:S(2)}, u32[]{:S(2)}) %collective-permute-start.2) | collective-permute-done | bytes 2097184 | tf_op jit(solution)/shard_map/ppermute | solution.py:181
  107.4 0.0 copy-start.10
  107.4 0.0 collective-permute-start.8
  107.4 1.0 collective-permute-done.3.refs_3_
  108.5 3.3 %collective-permute-start.9 = (bf16[1,1,512,512]{3,2,1,0:T(8,128)(2,1)}, bf16[1,1,512,512]{3,2,1,0:T(8,128)(2,1)S(1)}, u32[]{:S(2)}, u32[]{:S(2)}) collective-permute-start(bf16[1,1,512,512]{3,2,1,0:T(8,128)(2,1)} %get-tuple-element.19), channel_id=1, source_target_pairs={{0,8},{4,12},{8,0},{12,4},{16,24},{20,28},{24,16},{28,20},{1,9},{5... | collective-permute-start | bytes 1572872 | tf_op jit(solution)/shard_map/ppermute | solution.py:181
  111.7 14.3 %shard_map.96.base_ref = f32[4,2,512,512]{3,2,1,0:T(8,128)} custom-call(f32[4,9]{1,0:T(4,128)} %pad_maximum_fusion.coef_ref, f32[4,2,512,512]{3,2,1,0:T(8,128)} %shard_map.95.base_ref, bf16[2,2,512,512]{3,2,1,0:T(8,128)(2,1)} %collective-permute-done.2.refs_0_, ...), custom_call_target="tpu_custom_call", output_to_operand_aliasing={{}: (1, {})} | custom-call | flops 8589934592 | bytes 16777216 | tf_op jit(solution)/shard_map/pallas_call | solution.py:165
  126.1 0.0 collective-permute-done.4.refs_0_
  126.1 0.0 copy-done.10
  126.1 0.0 copy-start.11
  126.1 1.6 collective-permute-start.7
  127.6 13.6 %shard_map.97.base_ref = f32[4,2,512,512]{3,2,1,0:T(8,128)} custom-call(f32[4,9]{1,0:T(4,128)} %pad_maximum_fusion.coef_ref, f32[4,2,512,512]{3,2,1,0:T(8,128)} %shard_map.96.base_ref, bf16[4,2,512,512]{3,2,1,0:T(8,128)(2,1)} %collective-permute-done.4.refs_0_, ...), custom_call_target="tpu_custom_call", output_to_operand_aliasing={{}: (1, {})} | custom-call | flops 8589934592 | bytes 23068672 | tf_op jit(solution)/shard_map/pallas_call | solution.py:165
  141.2 11.1 %collective-permute-done.5.refs_0_ = bf16[1,2,512,512]{3,2,1,0:T(8,128)(2,1)S(1)} collective-permute-done((bf16[1,2,512,512]{3,2,1,0:T(8,128)(2,1)}, bf16[1,2,512,512]{3,2,1,0:T(8,128)(2,1)S(1)}, u32[]{:S(2)}, u32[]{:S(2)}) %collective-permute-start.5) | collective-permute-done | bytes 1048608 | tf_op jit(solution)/shard_map/ppermute | solution.py:181
  152.3 0.0 copy-start.1
  152.3 0.0 copy-done.11
  152.3 0.0 collective-permute-start.10
  152.3 0.9 collective-permute-done.6.refs_3_
  153.3 0.0 copy-start.2
  153.3 3.4 %collective-permute-start.11 = (bf16[1,1,512,512]{3,2,1,0:T(8,128)(2,1)S(1)}, bf16[1,1,512,512]{3,2,1,0:T(8,128)(2,1)S(1)}, u32[]{:S(2)}, u32[]{:S(2)}) collective-permute-start(bf16[1,1,512,512]{3,2,1,0:T(8,128)(2,1)S(1)} %copy-done.11), channel_id=1, source_target_pairs={{0,8},{4,12},{8,0},{12,4},{16,24},{20,28},{24,16},{28,20},{1,9},{5... | collective-permute-start | bytes 1572872 | tf_op jit(solution)/shard_map/ppermute | solution.py:181
  156.6 0.0 copy-done.1
  156.6 0.0 copy-done.2
  156.6 9.3 %shard_map.98.base_ref = f32[4,2,512,512]{3,2,1,0:T(8,128)} custom-call(f32[4,9]{1,0:T(4,128)} %pad_maximum_fusion.coef_ref, f32[4,2,512,512]{3,2,1,0:T(8,128)} %shard_map.97.base_ref, bf16[1,2,512,512]{3,2,1,0:T(8,128)(2,1)} %copy-done.1, ...), custom_call_target="tpu_custom_call", output_to_operand_aliasing={{}: (1, {})} | custom-call | flops 4294967296 | bytes 10485760 | tf_op jit(solution)/shard_map/pallas_call | solution.py:165
  166.0 0.0 collective-permute-done.7.refs_0_
  166.0 0.0 copy-start.3
  166.0 1.0 copy-done.3
  167.0 6.2 %shard_map.99.base_ref = f32[4,2,512,512]{3,2,1,0:T(8,128)} custom-call(f32[4,9]{1,0:T(4,128)} %pad_maximum_fusion.coef_ref, f32[4,2,512,512]{3,2,1,0:T(8,128)} %shard_map.98.base_ref, bf16[1,2,512,512]{3,2,1,0:T(8,128)(2,1)} %copy-done.3, ...), custom_call_target="tpu_custom_call", output_to_operand_aliasing={{}: (1, {})} | custom-call | flops 2147483648 | bytes 7340032 | tf_op jit(solution)/shard_map/pallas_call | solution.py:165
  173.2 1.7 collective-permute-done.8.refs_0_
  174.8 0.0 copy-start.4
  174.8 0.9 collective-permute-done.9.refs_3_
  175.7 0.0 copy-done.4
  175.7 0.0 copy-start.5
  175.7 0.8 copy-done.5
  176.5 6.8 %shard_map.100.base_ref = f32[4,2,512,512]{3,2,1,0:T(8,128)} custom-call(f32[4,9]{1,0:T(4,128)} %pad_maximum_fusion.coef_ref, f32[4,2,512,512]{3,2,1,0:T(8,128)} %shard_map.99.base_ref, bf16[1,1,512,512]{3,2,1,0:T(8,128)(2,1)} %copy-done.4, ...), custom_call_target="tpu_custom_call", output_to_operand_aliasing={{}: (1, {})} | custom-call | flops 2147483648 | bytes 10485760 | tf_op jit(solution)/shard_map/pallas_call | solution.py:165
  183.3 13.8 %collective-permute-done.10.refs_0_ = bf16[1,1,512,512]{3,2,1,0:T(8,128)(2,1)S(1)} collective-permute-done((bf16[1,1,512,512]{3,2,1,0:T(8,128)(2,1)S(1)}, bf16[1,1,512,512]{3,2,1,0:T(8,128)(2,1)S(1)}, u32[]{:S(2)}, u32[]{:S(2)}) %collective-permute-start.10) | collective-permute-done | bytes 524320 | tf_op jit(solution)/shard_map/ppermute | solution.py:181
  197.1 0.1 collective-permute-done.11.refs_3_
  197.1 0.8 copy-done.6
  197.9 0.8 copy-done.7
  198.7 6.8 %shard_map.101 = f32[4,2,512,512]{3,2,1,0:T(8,128)} custom-call(f32[4,9]{1,0:T(4,128)} %pad_maximum_fusion.coef_ref, f32[4,2,512,512]{3,2,1,0:T(8,128)} %shard_map.100.base_ref, bf16[1,1,512,512]{3,2,1,0:T(8,128)(2,1)} %copy-done.6, bf16[8,2,512,512]{3,2,1,0:T(8,128)(2,1)} %get-tuple-element.14.refs_1_.refs_4_.refs_7_.refs_10_, ...), custom_call_target="tpu_custom_call", output_to_operand_aliasing={{}: (1, {})} | custom-call | flops 2147483648 | bytes 10485760 | tf_op jit(solution)/shard_map/pallas_call | solution.py:165
  (5 shorter events, 0.0 us)
Async XLA Ops:
  0.0 20.7 %copy-start.8 = (f32[7]{0:T(128)S(1)}, f32[7]{0:T(128)}, u32[]{:S(2)}) copy-start(f32[7]{0:T(128)} %_.1) | copy-start | bytes 88
  0.0 20.6 %copy-start.12 = (s32[7]{0:T(128)S(1)}, s32[7]{0:T(128)}, u32[]{:S(2)}) copy-start(s32[7]{0:T(128)} %param.15) | copy-start | bytes 88
  0.0 20.7 %copy-start.9 = (f32[7]{0:T(128)S(1)}, f32[7]{0:T(128)}, u32[]{:S(2)}) copy-start(f32[7]{0:T(128)} %param.17) | copy-start | bytes 88
  3.3 8.8 %copy-start = (bf16[2,2,512,512]{3,2,1,0:T(8,128)(2,1)S(1)}, bf16[2,2,512,512]{3,2,1,0:T(8,128)(2,1)}, u32[]{:S(2)}) copy-start(bf16[2,2,512,512]{3,2,1,0:T(8,128)(2,1)} %shard_map.91._) | copy-start | bytes 6291460
  11.7 25.4 %collective-permute-start = (bf16[4,2,512,512]{3,2,1,0:T(8,128)(2,1)}, bf16[4,2,512,512]{3,2,1,0:T(8,128)(2,1)}, u32[]{:S(2)}, u32[]{:S(2)}) collective-permute-start(bf16[4,2,512,512]{3,2,1,0:T(8,128)(2,1)} %get-tuple-element.13.refs_0_.refs_3_.refs_6_), channel_id=1, source_target_pairs={{0,4},{4,0},{8,12},{12,8},{16,20},{20,16},{24,28},{28,24},{1,5},{5... | collective-permute-start | bytes 12582920 | tf_op jit(solution)/shard_map/ppermute | solution.py:181
  12.1 95.3 %collective-permute-start.2 = (bf16[2,2,512,512]{3,2,1,0:T(8,128)(2,1)S(1)}, bf16[2,2,512,512]{3,2,1,0:T(8,128)(2,1)}, u32[]{:S(2)}, u32[]{:S(2)}) collective-permute-start(bf16[2,2,512,512]{3,2,1,0:T(8,128)(2,1)S(1)} %copy-done), channel_id=1, source_target_pairs={{0,16},{4,20},{8,24},{12,28},{16,0},{20,4},{24,8},{28,12},{1,17},{... | collective-permute-start | bytes 6291464 | tf_op jit(solution)/shard_map/ppermute | solution.py:181
  15.8 92.7 %collective-permute-start.3 = (bf16[2,2,512,512]{3,2,1,0:T(8,128)(2,1)S(1)}, bf16[2,2,512,512]{3,2,1,0:T(8,128)(2,1)}, u32[]{:S(2)}, u32[]{:S(2)}) collective-permute-start(bf16[2,2,512,512]{3,2,1,0:T(8,128)(2,1)S(1)} %copy-done), channel_id=1, source_target_pairs={{0,8},{4,12},{8,0},{12,4},{16,24},{20,28},{24,16},{28,20},{1,9},{5... | collective-permute-start | bytes 6291464 | tf_op jit(solution)/shard_map/ppermute | solution.py:181
  17.4 108.7 %collective-permute-start.4 = (bf16[4,2,512,512]{3,2,1,0:T(8,128)(2,1)}, bf16[4,2,512,512]{3,2,1,0:T(8,128)(2,1)}, u32[]{:S(2)}, u32[]{:S(2)}) collective-permute-start(bf16[4,2,512,512]{3,2,1,0:T(8,128)(2,1)} %get-tuple-element.13.refs_0_.refs_3_.refs_6_), channel_id=1, source_target_pairs={{0,2},{1,3},{2,0},{3,1},{4,6},{5,7},{6,4},{7,5},{8,10},{9,11},{10,... | collective-permute-start | bytes 12582920 | tf_op jit(solution)/shard_map/ppermute | solution.py:181
  18.9 69.9 %collective-permute-start.1 = (bf16[3,2,512,512]{3,2,1,0:T(8,128)(2,1)}, bf16[3,2,512,512]{3,2,1,0:T(8,128)(2,1)}, u32[]{:S(2)}, u32[]{:S(2)}) collective-permute-start(bf16[3,2,512,512]{3,2,1,0:T(8,128)(2,1)} %get-tuple-element.16), channel_id=1, source_target_pairs={{0,1},{1,0},{2,3},{3,2},{4,5},{5,4},{6,7},{7,6},{8,9},{9,8},{10,11... | collective-permute-start | bytes 9437192 | tf_op jit(solution)/shard_map/ppermute | solution.py:181
  37.0 115.3 %collective-permute-start.5 = (bf16[1,2,512,512]{3,2,1,0:T(8,128)(2,1)}, bf16[1,2,512,512]{3,2,1,0:T(8,128)(2,1)S(1)}, u32[]{:S(2)}, u32[]{:S(2)}) collective-permute-start(bf16[1,2,512,512]{3,2,1,0:T(8,128)(2,1)} %get-tuple-element.17), channel_id=1, source_target_pairs={{0,16},{4,20},{8,24},{12,28},{16,0},{20,4},{24,8},{28,12},{1,17},{... | collective-permute-start | bytes 3145736 | tf_op jit(solution)/shard_map/ppermute | solution.py:181
  88.8 64.4 %collective-permute-start.6 = (bf16[1,2,512,512]{3,2,1,0:T(8,128)(2,1)}, bf16[1,2,512,512]{3,2,1,0:T(8,128)(2,1)S(1)}, u32[]{:S(2)}, u32[]{:S(2)}) collective-permute-start(bf16[1,2,512,512]{3,2,1,0:T(8,128)(2,1)} %get-tuple-element.17), channel_id=1, source_target_pairs={{0,8},{4,12},{8,0},{12,4},{16,24},{20,28},{24,16},{28,20},{1,9},{5... | collective-permute-start | bytes 3145736 | tf_op jit(solution)/shard_map/ppermute | solution.py:181
  107.4 18.6 %copy-start.10 = (bf16[1,2,512,512]{3,2,1,0:T(8,128)(2,1)S(1)}, bf16[1,2,512,512]{3,2,1,0:T(8,128)(2,1)}, u32[]{:S(2)}) copy-start(bf16[1,2,512,512]{3,2,1,0:T(8,128)(2,1)} %get-tuple-element.18) | copy-start | bytes 3145732
  107.4 67.4 %collective-permute-start.8 = (bf16[1,1,512,512]{3,2,1,0:T(8,128)(2,1)}, bf16[1,1,512,512]{3,2,1,0:T(8,128)(2,1)S(1)}, u32[]{:S(2)}, u32[]{:S(2)}) collective-permute-start(bf16[1,1,512,512]{3,2,1,0:T(8,128)(2,1)} %get-tuple-element.19), channel_id=1, source_target_pairs={{0,16},{4,20},{8,24},{12,28},{16,0},{20,4},{24,8},{28,12},{1,17},{... | collective-permute-start | bytes 1572872 | tf_op jit(solution)/shard_map/ppermute | solution.py:181
  108.5 67.2 %collective-permute-start.9 = (bf16[1,1,512,512]{3,2,1,0:T(8,128)(2,1)}, bf16[1,1,512,512]{3,2,1,0:T(8,128)(2,1)S(1)}, u32[]{:S(2)}, u32[]{:S(2)}) collective-permute-start(bf16[1,1,512,512]{3,2,1,0:T(8,128)(2,1)} %get-tuple-element.19), channel_id=1, source_target_pairs={{0,8},{4,12},{8,0},{12,4},{16,24},{20,28},{24,16},{28,20},{1,9},{5... | collective-permute-start | bytes 1572872 | tf_op jit(solution)/shard_map/ppermute | solution.py:181
  126.1 26.3 %copy-start.11 = (bf16[1,1,512,512]{3,2,1,0:T(8,128)(2,1)S(1)}, bf16[1,1,512,512]{3,2,1,0:T(8,128)(2,1)}, u32[]{:S(2)}) copy-start(bf16[1,1,512,512]{3,2,1,0:T(8,128)(2,1)} %get-tuple-element.20) | copy-start | bytes 1572868
  126.1 39.9 %collective-permute-start.7 = (bf16[1,2,512,512]{3,2,1,0:T(8,128)(2,1)S(1)}, bf16[1,2,512,512]{3,2,1,0:T(8,128)(2,1)S(1)}, u32[]{:S(2)}, u32[]{:S(2)}) collective-permute-start(bf16[1,2,512,512]{3,2,1,0:T(8,128)(2,1)S(1)} %copy-done.10), channel_id=1, source_target_pairs={{0,1},{1,0},{2,3},{3,2},{4,5},{5,4},{6,7},{7,6},{8,9},{9,8},{10,11... | collective-permute-start | bytes 3145736 | tf_op jit(solution)/shard_map/ppermute | solution.py:181
  152.3 4.3 %copy-start.1 = (bf16[1,2,512,512]{3,2,1,0:T(8,128)(2,1)}, bf16[1,2,512,512]{3,2,1,0:T(8,128)(2,1)S(1)}, u32[]{:S(2)}) copy-start(bf16[1,2,512,512]{3,2,1,0:T(8,128)(2,1)S(1)} %collective-permute-done.5.refs_0_) | copy-start | bytes 3145732
  152.3 44.8 %collective-permute-start.10 = (bf16[1,1,512,512]{3,2,1,0:T(8,128)(2,1)S(1)}, bf16[1,1,512,512]{3,2,1,0:T(8,128)(2,1)S(1)}, u32[]{:S(2)}, u32[]{:S(2)}) collective-permute-start(bf16[1,1,512,512]{3,2,1,0:T(8,128)(2,1)S(1)} %copy-done.11), channel_id=1, source_target_pairs={{0,16},{4,20},{8,24},{12,28},{16,0},{20,4},{24,8},{28,12},{1,17},{... | collective-permute-start | bytes 1572872 | tf_op jit(solution)/shard_map/ppermute | solution.py:181
  153.3 3.4 %copy-start.2 = (bf16[1,2,512,512]{3,2,1,0:T(8,128)(2,1)}, bf16[1,2,512,512]{3,2,1,0:T(8,128)(2,1)S(1)}, u32[]{:S(2)}) copy-start(bf16[1,2,512,512]{3,2,1,0:T(8,128)(2,1)S(1)} %collective-permute-done.6.refs_3_) | copy-start | bytes 3145732
  153.3 43.9 %collective-permute-start.11 = (bf16[1,1,512,512]{3,2,1,0:T(8,128)(2,1)S(1)}, bf16[1,1,512,512]{3,2,1,0:T(8,128)(2,1)S(1)}, u32[]{:S(2)}, u32[]{:S(2)}) collective-permute-start(bf16[1,1,512,512]{3,2,1,0:T(8,128)(2,1)S(1)} %copy-done.11), channel_id=1, source_target_pairs={{0,8},{4,12},{8,0},{12,4},{16,24},{20,28},{24,16},{28,20},{1,9},{5... | collective-permute-start | bytes 1572872 | tf_op jit(solution)/shard_map/ppermute | solution.py:181
  166.0 1.0 copy-start.3
  174.8 0.9 copy-start.4
  175.7 0.8 copy-start.5
  197.1 0.8 copy-start.6
  197.9 0.8 copy-start.7
where the time goes:
time: 206 us
  Pallas kernels  139 us (67%)
  waiting for transfers between devices  44.4 us (22%)
  starting transfers between devices  17.7 us (9%)
  local copies, waits for them, and re-layouts  3.54 us (2%)
    pallas_call x8, Pallas kernels, add_terms(): pl.pallas_call(functools.partial(term_kernel, first, [t[:2] for t in term...  112 us
    ppermute x12, waiting for transfers between devices, flip(): return lax.ppermute(value, axis, pairs)  44.4 us
    ppermute x12, starting transfers between devices, flip(): return lax.ppermute(value, axis, pairs)  17.7 us
    pallas_call x1, Pallas kernels, make_operators(): pl.pallas_call(operator_kernel, grid_spec=pltpu.PrefetchScalarGridSpec(nu...  15.4 us
    pallas_call x2, Pallas kernels, round_groups(): pl.pallas_call(functools.partial(round_kernel, groups), grid=(high - low,...  11.7 us
  transfers between devices with their start and end apart: 12, of which 9 were waited for; matrix products, arithmetic and copies ran while one was open for 1% of the time, Pallas kernels for 59%

commit v1 on v0

--- a/solution.py
+++ b/solution.py
@@ -8,7 +8,7 @@
 from jax.sharding import PartitionSpec as P
 
 VMEM_LIMIT = 56 * 2**20
-COST = 1.0
+LAST_VMEM_LIMIT = 24 * 2**20
 SMEM = pl.BlockSpec(memory_space=pltpu.SMEM)
 
 
@@ -18,7 +18,7 @@
             vmem_limit_bytes=VMEM_LIMIT, dimension_semantics=("arbitrary",)
         ),
         cost_estimate=pl.CostEstimate(
-            flops=int(COST * flops), bytes_accessed=int(COST * moved), transcendentals=0
+            flops=flops, bytes_accessed=moved, transcendentals=0
         ),
     )
 
@@ -27,43 +27,54 @@
     return jnp.dot(a, b, preferred_element_type=jnp.float32)
 
 
-def round_kernel(groups, density_ref, _, *out_refs):
-    step = pl.program_id(0)
-    first_seen = min(first for first, _, _ in groups)
-    for (first, span, part), out_ref in zip(groups, out_refs):
-
-        @pl.when((step + first_seen >= first) & (step + first_seen < first + span))
-        def _(part=part, out_ref=out_ref):
-            if part is None:
-                out_ref[...] = density_ref[...].astype(jnp.bfloat16)
-            else:
-                out_ref[0, 0] = density_ref[0, part].astype(jnp.bfloat16)
+def round_kernel(groups, low, high, density_ref, _, *refs):
+    outs, (source, loads, stores, *rounded) = refs[: len(groups)], refs[len(groups) :]
+    pairs = [(index, part) for index in range(low, high) for part in range(2)]
+    reads = {
+        pair: pltpu.make_async_copy(density_ref.at[pair], source.at[place], loads.at[place])
+        for place, pair in enumerate(pairs)
+    }
+    for pair in pairs:
+        reads[pair].start()
+    writes = []
+    for place, (index, part) in enumerate(pairs):
+        reads[index, part].wait()
+        kept = rounded[0].at[place]
+        kept[...] = source[place].astype(jnp.bfloat16)
+        for (first, span, only), out_ref in zip(groups, outs):
+            if first <= index < first + span and only in (None, part):
+                target = out_ref.at[index - first, part if only is None else 0]
+                writes.append(pltpu.make_async_copy(kept, target, stores.at[len(writes)]))
+                writes[-1].start()
+    for write in writes:
+        write.wait()
 
 
 def round_groups(density, groups, after):
     n = density.shape[-1]
     low = min(first for first, _, _ in groups)
     high = max(first + span for first, span, _ in groups)
-
-    def out_spec(first, span, part):
-        return pl.BlockSpec(
-            (1, 2 if part is None else 1, n, n),
-            lambda g: (jnp.clip(g + low - first, 0, span - 1), 0, 0, 0),
-        )
-
-    return pl.pallas_call(
-        functools.partial(round_kernel, groups),
-        grid=(high - low,),
-        in_specs=[
-            pl.BlockSpec((1, 2, n, n), lambda g: (g + low, 0, 0, 0)),
-            pl.BlockSpec(memory_space=pl.ANY),
-        ],
-        out_specs=[out_spec(*group) for group in groups],
+    parts = 2 * (high - low)
+    writes = sum(span * (2 if part is None else 1) for _, span, part in groups)
+    anywhere = pl.BlockSpec(memory_space=pl.ANY)
+    return pl.pallas_call(
+        functools.partial(round_kernel, groups, low, high),
+        in_specs=[anywhere, anywhere],
+        out_specs=[anywhere] * len(groups),
         out_shape=[
             jax.ShapeDtypeStruct((span, 2 if part is None else 1, n, n), jnp.bfloat16)
             for _, span, part in groups
         ],
-        **params(0, 8 * n * n * (high - low) + sum(4 * n * n * span for _, span, _ in groups)),
+        scratch_shapes=[
+            pltpu.VMEM((parts, n, n), jnp.float32),
+            pltpu.SemaphoreType.DMA((parts,)),
+            pltpu.SemaphoreType.DMA((writes,)),
+            pltpu.VMEM((parts, n, n), jnp.bfloat16),
+        ],
+        compiler_params=pltpu.CompilerParams(vmem_limit_bytes=VMEM_LIMIT),
+        cost_estimate=pl.CostEstimate(
+            flops=0, bytes_accessed=n * n * (4 * parts + 2 * writes), transcendentals=0
+        ),
     )(density, after)
 
 
@@ -122,7 +133,7 @@
     )(operator_slot, block_mask, left_operators, right_operators, hamiltonian)
 
 
-def term_kernel(first, terms, fresh, coef_ref, base_ref, *refs):
+def term_kernel(first, terms, fresh, coef_ref, base_ref, _, *refs):
     out_ref = refs[-1]
     index = first + pl.program_id(0)
     if fresh:
@@ -150,7 +161,10 @@
     out_ref[0, 1] = imag
 
 
-def add_terms(base, coef, operators, first, span, terms, fresh=False):
+def add_terms(base, into, coef, operators, first, span, terms):
+    fresh = into is not base
+    alias = {1: 0} if not fresh else {2: 0} if into is not None else {}
+    into = into if fresh and into is not None else coef
     n = base.shape[-1]
     lefts, rights = operators
     specs, args = [], []
@@ -165,15 +179,111 @@
     return pl.pallas_call(
         functools.partial(term_kernel, first, [t[:2] for t in terms], fresh),
         grid=(span,),
-        in_specs=[SMEM, block] + specs,
+        in_specs=[SMEM, block, pl.BlockSpec(memory_space=pl.ANY)] + specs,
         out_specs=block,
         out_shape=jax.ShapeDtypeStruct(base.shape, jnp.float32),
-        input_output_aliases={} if fresh else {1: 0},
+        input_output_aliases=alias,
         **params(
             16 * n**3 * span * sum(1 if t[1] is None else 0.5 for t in terms),
             n * n * span * (16 + 4 * len(terms)) + 8 * n * n * len(terms),
         ),
-    )(coef, base, *args)
+    )(coef, base, into, *args)
+
+
+def part_terms(index, out, terms, coef_ref, arrays, left, right):
+    change = None
+    for t, (mode, part) in enumerate(terms):
+        use = part if out == 0 else 1 - part
+        coef = coef_ref[index, mode]
+        if out == 0 and part == 1:
+            coef = -coef
+        value = arrays[t][0, 0]
+        term = coef * (dot(left[t, use], value) + dot(value, right[t, use]))
+        change = term if change is None else change + term
+    return change
+
+
+def stage_kernel(index, terms, coef_ref, base_ref, left_ref, right_ref, *refs):
+    count = len(terms)
+    arrays, (total, left, right, loads) = refs[:count], refs[count:]
+    copies = [pltpu.make_async_copy(base_ref.at[index], total, loads.at[0])]
+    for t, (mode, _) in enumerate(terms):
+        for source, target in ((left_ref, left), (right_ref, right)):
+            copies.append(
+                pltpu.make_async_copy(source.at[mode], target.at[t], loads.at[len(copies)])
+            )
+    for copy in copies:
+        copy.start()
+    for copy in copies:
+        copy.wait()
+    for out in range(2):
+        total[out] += part_terms(index, out, terms, coef_ref, arrays, left, right)
+
+
+def finish_kernel(index, terms, coef_ref, _, total, left, right, *refs):
+    count = len(terms)
+    arrays, (out_ref, result, stores) = refs[:count], refs[count:]
+    writes = []
+    for out in range(2):
+        result[out] = total[out] + part_terms(index, out, terms, coef_ref, arrays, left, right)
+        writes.append(
+            pltpu.make_async_copy(result.at[out], out_ref.at[index, out], stores.at[out])
+        )
+        writes[-1].start()
+    for write in writes:
+        write.wait()
+
+
+def in_vmem(array):
+    return pltpu.with_memory_space_constraint(array, pltpu.VMEM)
+
+
+def in_hbm(array):
+    return pltpu.with_memory_space_constraint(array, pltpu.HBM)
+
+
+def last_params(n, count):
+    return dict(
+        compiler_params=pltpu.CompilerParams(vmem_limit_bytes=LAST_VMEM_LIMIT),
+        cost_estimate=pl.CostEstimate(
+            flops=8 * n**3 * count, bytes_accessed=n * n * (8 + 8 * count), transcendentals=0
+        ),
+    )
+
+
+ANYWHERE = pl.BlockSpec(memory_space=pl.ANY)
+WHOLE = pl.BlockSpec(memory_space=pltpu.VMEM)
+
+
+def stage_last(base, coef, operators, index, terms):
+    n = base.shape[-1]
+    count = len(terms)
+    return pl.pallas_call(
+        functools.partial(stage_kernel, index, [t[:2] for t in terms]),
+        in_specs=[SMEM] + [ANYWHERE] * 3 + [WHOLE] * count,
+        out_specs=[WHOLE] * 3,
+        out_shape=[
+            pltpu.VMEM((2, n, n), jnp.float32),
+            pltpu.VMEM((count, 2, n, n), jnp.bfloat16),
+            pltpu.VMEM((count, 2, n, n), jnp.bfloat16),
+        ],
+        scratch_shapes=[pltpu.SemaphoreType.DMA((1 + 2 * count,))],
+        **last_params(n, count),
+    )(coef, *[in_hbm(array) for array in (base, *operators)], *[in_vmem(t[2]) for t in terms])
+
+
+def finish_last(base, coef, staged, index, terms):
+    n = base.shape[-1]
+    count = len(terms)
+    return pl.pallas_call(
+        functools.partial(finish_kernel, index, [t[:2] for t in terms]),
+        in_specs=[SMEM, ANYWHERE] + [WHOLE] * (3 + count),
+        out_specs=ANYWHERE,
+        out_shape=jax.ShapeDtypeStruct(base.shape, jnp.float32),
+        scratch_shapes=[pltpu.VMEM((2, n, n), jnp.float32), pltpu.SemaphoreType.DMA((2,))],
+        input_output_aliases={1: 0},
+        **last_params(n, count),
+    )(coef, base, *[in_vmem(part) for part in staged], *[in_vmem(t[2]) for t in terms])
 
 
 def flip(value, axis, bit):
@@ -220,22 +330,21 @@
     middle = [m for m in remote[:-2] if m not in near]
 
     half = count // 2
-    pieces = [(0, half), (half, last - half)] if half else [(0, last)]
-    pieces = [(first, span, None) for first, span in pieces if span > 0]
-    plan = [(near, 0, count, None)]
-    plan += [([m], 0, last or count, None) for m in middle[:1]]
-    for place, piece in enumerate(pieces):
-        plan.append((slow,) + piece)
-        if place == 0:
-            plan += [([m], 0, count, None) for m in middle[1:]]
-            middle = middle[:1]
-    plan += [([m], last, 1, None) for m in middle[:1] if last]
-    plan += [([m], 0, count, None) for m in middle[1:]]
-    plan += [(slow, last, 1, 0), (slow, last, 1, 1)]
-    plan = [step for step in plan if step[0]]
-
-    groups = list(dict.fromkeys([(0, count, None)] + [step[1:] for step in plan]))
-    early = [step[1:] for step in plan if step[0] == slow][:1]
+    spans = [(0, half), (half, half)] if half else [(0, count)]
+    pieces = [piece for piece in ((0, half), (half, last - half)) if piece[1]]
+    plan = [(near,) + span + (None,) for span in spans]
+    plan.append((middle[:1], 0, last or count, None))
+    plan += [(slow,) + piece + (None,) for piece in pieces[:1]]
+    plan.append((middle[1:], 0, count, None))
+    plan += [(slow,) + piece + (None,) for piece in pieces[1:]]
+    if last:
+        plan.append((middle[:1], last, 1, None))
+    plan += [(slow, last, 1, part) for part in range(2)]
+
+    plan = [step for place, step in enumerate(plan) if step[0] or place < len(spans)]
+
+    groups = list(dict.fromkeys([step[1:] for step in plan]))
+    early = [step[1:] for step in plan if step[0] is slow][:1]
     late = [group for group in groups if group not in early]
     rounded = dict(zip(early, round_groups(density, early, damping_rate)))
     rounded.update(zip(late, round_groups(density, late, rounded[early[0]])))
@@ -245,18 +354,30 @@
     operators = make_operators(
         left_operators, right_operators, block_mask, operator_slot, hamiltonian
     )
-    whole = rounded[(0, count, None)]
-
-    terms = [(modes, None, whole, lambda g: g)]
-    for mode in range(local_bits):
-        terms.append((mode, None, whole, lambda g, mode=mode: g ^ (1 << mode)))
-    if near:
-        terms += [(m, None, array, lambda g: g) for m, array in zip(near, sent[0])]
-        plan, sent = plan[1:], sent[1:]
-    result = add_terms(density, coef, operators, 0, count, terms, fresh=True)
-    for (step_modes, first, span, part), arrays in zip(plan, sent):
+
+    def local_terms(span):
+        own, other = rounded[span + (None,)], rounded[(half - span[0],) + span[1:] + (None,)]
+        terms = [(modes, None, own, lambda g: g)]
+        for mode in range(local_bits):
+            step = 1 << mode
+            if step < span[1]:
+                terms.append((mode, None, own, lambda g, step=step: g ^ step))
+            else:
+                terms.append((mode, None, other, lambda g: g))
+        return terms
+
+    result, staged = None, None
+    for place, ((step_modes, first, span, part), arrays) in enumerate(zip(plan, sent)):
         terms = [(m, part, array, lambda g: g) for m, array in zip(step_modes, arrays)]
-        result = add_terms(result, coef, operators, first, span, terms)
+        if place < len(spans):
+            terms = local_terms(spans[place]) + terms
+            result = add_terms(density, result, coef, operators, first, span, terms)
+        elif part is None:
+            result = add_terms(result, result, coef, operators, first, span, terms)
+        elif part == 0:
+            staged = stage_last(result, coef, operators, first, terms)
+        else:
+            result = finish_last(result, coef, staged, first, terms)
     return result
 
 

time: 206 us -> 193 us (0.937)
  waiting for transfers between devices: 44.4 us -> 33.1 us
  starting transfers between devices: 17.7 us -> 14.5 us
    ppermute x12 -> x13, waiting for transfers between devices: 44.4 us -> 33.1 us  [flip(): return lax.ppermute(value, axis, pairs)]
    pallas_call x2 -> x4, Pallas kernels: 11.7 us -> 20.8 us  [the longest x2 11.2 us: round_groups(): pl.pallas_call(functools.partial(round_kernel, groups, low, high), in_spe...]
    pallas_call x8 -> x7, Pallas kernels: 112 us -> 105 us  [add_terms(): pl.pallas_call(functools.partial(term_kernel, first, [t[:2] for t in term...]
    ppermute x12 -> x13, starting transfers between devices: 17.7 us -> 14.5 us  [flip(): return lax.ppermute(value, axis, pairs)]
  transfers between devices with their start and end apart: 12 -> 13, of which waited for: 9 -> 6; matrix products, arithmetic and copies ran while one was open for 1% -> 1% of each run, Pallas kernels for 59% -> 70%
where the time goes in v1:
time: 193 us
  Pallas kernels  141 us (73%)
  waiting for transfers between devices  33.1 us (17%)
  starting transfers between devices  14.5 us (8%)
  local copies, waits for them, and re-layouts  2.59 us (1%)
    pallas_call x7, Pallas kernels, add_terms(): pl.pallas_call(functools.partial(term_kernel, first, [t[:2] for t in term...  105 us
    ppermute x13, waiting for transfers between devices, flip(): return lax.ppermute(value, axis, pairs)  33.1 us
    pallas_call x1, Pallas kernels, make_operators(): pl.pallas_call(operator_kernel, grid_spec=pltpu.PrefetchScalarGridSpec(nu...  15.4 us
    ppermute x13, starting transfers between devices, flip(): return lax.ppermute(value, axis, pairs)  14.5 us
    pallas_call x2, Pallas kernels, round_groups(): pl.pallas_call(functools.partial(round_kernel, groups, low, high), in_spe...  11.2 us
    pallas_call x1, Pallas kernels, stage_last(): pl.pallas_call(functools.partial(stage_kernel, index, [t[:2] for t in ter...  5.76 us
    pallas_call x1, Pallas kernels, finish_last(): pl.pallas_call(functools.partial(finish_kernel, index, [t[:2] for t in te...  3.91 us
  transfers between devices with their start and end apart: 13, of which 6 were waited for; matrix products, arithmetic and copies ran while one was open for 1% of the time, Pallas kernels for 70%

profile of v1, /device:TPU:0, one launch (start us, length us, event | category | flops | bytes accessed | tf_op | source)
XLA Modules:
  0.0 193.0 jit_solution(2865005943244316312)
XLA Ops:
  0.0 3.1 %shard_map.91._.refs_0_.refs_3_.refs_6_ = bf16[2,2,512,512]{3,2,1,0:T(8,128)(2,1)} custom-call(f32[4,2,512,512]{3,2,1,0:T(8,128)} %base_ref.3, f32[7]{0:T(128)} %_.1), custom_call_target="tpu_custom_call" | custom-call | bytes 6291456 | tf_op jit(solution)/shard_map/pallas_call | solution.py:60
  3.1 0.0 copy-start.8
  3.1 0.0 copy-start.4
  3.1 0.0 copy-start.5
  3.1 0.5 collective-permute-start
  3.7 3.7 %collective-permute-start.3 = (bf16[2,2,512,512]{3,2,1,0:T(8,128)(2,1)}, bf16[2,2,512,512]{3,2,1,0:T(8,128)(2,1)S(1)}, u32[]{:S(2)}, u32[]{:S(2)}) collective-permute-start(bf16[2,2,512,512]{3,2,1,0:T(8,128)(2,1)} %shard_map.91._.refs_0_.refs_3_.refs_6_), channel_id=1, source_target_pairs={{0,16},{4,20},{8,24},{12,28},{16,0},{20,4},{24,8},{28,12},{1,17},{... | collective-permute-start | bytes 6291464 | tf_op jit(solution)/shard_map/ppermute | solution.py:291
  7.3 1.6 collective-permute-start.4
  8.9 8.0 %shard_map.93 = (bf16[2,2,512,512]{3,2,1,0:T(8,128)(2,1)}, bf16[3,2,512,512]{3,2,1,0:T(8,128)(2,1)}, bf16[4,2,512,512]{3,2,1,0:T(8,128)(2,1)}, bf16[1,2,512,512]...) custom-call(f32[4,2,512,512]{3,2,1,0:T(8,128)} %base_ref.3, ...), custom_call_target="tpu_custom_call" | custom-call | bytes 20971520 | tf_op jit(solution)/shard_map/pallas_call | solution.py:60
  17.0 0.1 collective-permute-start.1
  17.0 1.6 collective-permute-start.2
  18.6 0.1 shift-right-arithmetic_and_fusion
  18.7 0.0 copy-done.8
  18.7 0.2 reduce_window_sum.11
  18.9 0.0 copy-done.4
  18.9 0.0 copy-done.5
  18.9 0.2 fusion.5
  19.1 0.1 copy.17
  19.2 0.1 pad.1.clone
  19.2 15.4 %shard_map.92 = (bf16[8,2,512,512]{3,2,1,0:T(8,128)(2,1)}, bf16[8,2,512,512]{3,2,1,0:T(8,128)(2,1)}) custom-call(s32[7]{0:T(128)} %slot_ref.1, s32[7,2,8,8]{3,2,1,0:T(8,128)} %mask_ref.1, bf16[7,2,512,512]{3,2,1,0:T(8,128)(2,1)} %left_ref.1, bf16[7,2,512,512]{3,2,1,0:T(8,128)(2,1)} %right_ref.1, bf16[2,512,512]{2,1,0:T(8,128)(2,1)} %ham_ref.1), custom_call_target="tpu_custom_call" | custom-call | bytes 33554432 | tf_op jit(solution)/shard_map/pallas_call | solution.py:118
  34.6 0.7 pad_maximum_fusion.coef_ref._
  35.2 0.0 collective-permute-done.refs_9_
  35.2 1.5 collective-permute-start.5
  36.8 25.3 %shard_map.94._ = f32[4,2,512,512]{3,2,1,0:T(8,128)} custom-call(f32[4,9]{1,0:T(4,128)} %pad_maximum_fusion.coef_ref._, f32[4,2,512,512]{3,2,1,0:T(8,128)} %base_ref.3, f32[4,9]{1,0:T(4,128)} %pad_maximum_fusion.coef_ref._, bf16[2,2,512,512]{3,2,1,0:T(8,128)(2,1)} %shard_map.91._.refs_0_.refs_3_.refs_6_, ...), custom_call_target="tpu_custom_call" | custom-call | flops 17179869184 | bytes 25165824 | tf_op jit(solution)/shard_map/pallas_call | solution.py:179
  62.0 0.0 collective-permute-done.1.refs_9_
  62.0 0.4 collective-permute-start.6
  62.4 25.4 %shard_map.95.base_ref = f32[4,2,512,512]{3,2,1,0:T(8,128)} custom-call(f32[4,9]{1,0:T(4,128)} %pad_maximum_fusion.coef_ref._, f32[4,2,512,512]{3,2,1,0:T(8,128)} %base_ref.3, f32[4,2,512,512]{3,2,1,0:T(8,128)} %shard_map.94._, bf16[2,2,512,512]{3,2,1,0:T(8,128)(2,1)} %get-tuple-element.19.refs_6_.refs_0_.refs_3_, ...), custom_call_target="tpu_custom_call", output_to_operand_aliasing={{}: (2, {})} | custom-call | flops 17179869184 | bytes 25165824 | tf_op jit(solution)/shard_map/pallas_call | solution.py:179
  87.8 0.0 copy-start.7
  87.8 0.1 collective-permute-done.2.refs_0_
  87.9 0.5 collective-permute-start.7
  88.3 11.2 %shard_map.96.base_ref = f32[4,2,512,512]{3,2,1,0:T(8,128)} custom-call(f32[4,9]{1,0:T(4,128)} %pad_maximum_fusion.coef_ref._, f32[4,2,512,512]{3,2,1,0:T(8,128)} %shard_map.95.base_ref, f32[4,9]{1,0:T(4,128)} %pad_maximum_fusion.coef_ref._, bf16[3,2,512,512]{3,2,1,0:T(8,128)(2,1)} %collective-permute-done.2.refs_0_, ...), custom_call_target="tpu_custom_call", output_to_operand_aliasing={{}: (1, {})} | custom-call | flops 6442450944 | bytes 17825792 | tf_op jit(solution)/shard_map/pallas_call | solution.py:179
  99.5 0.0 collective-permute-done.3.refs_0_
  99.5 0.0 copy-start.2
  99.5 0.0 copy-done.7
  99.5 1.6 collective-permute-start.10
  101.2 0.0 collective-permute-done.4.refs_3_
  101.2 2.5 %collective-permute-start.9 = (bf16[1,1,512,512]{3,2,1,0:T(8,128)(2,1)S(1)}, bf16[1,1,512,512]{3,2,1,0:T(8,128)(2,1)S(1)}, u32[]{:S(2)}, u32[]{:S(2)}) collective-permute-start(bf16[1,1,512,512]{3,2,1,0:T(8,128)(2,1)S(1)} %copy-done.7), channel_id=1, source_target_pairs={{0,16},{4,20},{8,24},{12,28},{16,0},{20,4},{24,8},{28,12},{1,17},{... | collective-permute-start | bytes 1572872 | tf_op jit(solution)/shard_map/ppermute | solution.py:291
  103.7 0.0 copy-done.2
  103.7 14.3 %shard_map.97.base_ref = f32[4,2,512,512]{3,2,1,0:T(8,128)} custom-call(f32[4,9]{1,0:T(4,128)} %pad_maximum_fusion.coef_ref._, f32[4,2,512,512]{3,2,1,0:T(8,128)} %shard_map.96.base_ref, f32[4,9]{1,0:T(4,128)} %pad_maximum_fusion.coef_ref._, bf16[2,2,512,512]{3,2,1,0:T(8,128)(2,1)} %copy-done.2, ...), custom_call_target="tpu_custom_call", output_to_operand_aliasing={{}: (1, {})} | custom-call | flops 8589934592 | bytes 16777216 | tf_op jit(solution)/shard_map/pallas_call | solution.py:179
  118.0 10.1 %collective-permute-done.5.refs_0_ = bf16[4,2,512,512]{3,2,1,0:T(8,128)(2,1)S(1)} collective-permute-done((bf16[4,2,512,512]{3,2,1,0:T(8,128)(2,1)}, bf16[4,2,512,512]{3,2,1,0:T(8,128)(2,1)S(1)}, u32[]{:S(2)}, u32[]{:S(2)}) %collective-permute-start.5) | collective-permute-done | bytes 4194336 | tf_op jit(solution)/shard_map/ppermute | solution.py:291
  128.1 0.0 copy-start.1
  128.1 0.0 copy-start.6
  128.1 0.5 collective-permute-start.8
  128.6 1.4 copy-done.1
  130.0 13.6 %shard_map.98.base_ref = f32[4,2,512,512]{3,2,1,0:T(8,128)} custom-call(f32[4,9]{1,0:T(4,128)} %pad_maximum_fusion.coef_ref._, f32[4,2,512,512]{3,2,1,0:T(8,128)} %shard_map.97.base_ref, f32[4,9]{1,0:T(4,128)} %pad_maximum_fusion.coef_ref._, bf16[4,2,512,512]{3,2,1,0:T(8,128)(2,1)} %copy-done.1, ...), custom_call_target="tpu_custom_call", output_to_operand_aliasing={{}: (1, {})} | custom-call | flops 8589934592 | bytes 23068672 | tf_op jit(solution)/shard_map/pallas_call | solution.py:179
  143.6 0.5 collective-permute-done.6.refs_0_
  144.2 0.0 copy-done.6
  144.2 0.0 collective-permute-start.11
  144.2 12.2 %collective-permute-done.7.refs_3_ = bf16[1,2,512,512]{3,2,1,0:T(8,128)(2,1)} collective-permute-done((bf16[1,2,512,512]{3,2,1,0:T(8,128)(2,1)}, bf16[1,2,512,512]{3,2,1,0:T(8,128)(2,1)}, u32[]{:S(2)}, u32[]{:S(2)}) %collective-permute-start.7) | collective-permute-done | bytes 1048608 | tf_op jit(solution)/shard_map/ppermute | solution.py:291
  156.4 0.0 collective-permute-start.12
  156.4 9.3 %shard_map.99.base_ref = f32[4,2,512,512]{3,2,1,0:T(8,128)} custom-call(f32[4,9]{1,0:T(4,128)} %pad_maximum_fusion.coef_ref._, f32[4,2,512,512]{3,2,1,0:T(8,128)} %shard_map.98.base_ref, f32[4,9]{1,0:T(4,128)} %pad_maximum_fusion.coef_ref._, bf16[1,2,512,512]{3,2,1,0:T(8,128)(2,1)} %collective-permute-done.6.refs_0_, ...), custom_call_target="tpu_custom_call", output_to_operand_aliasing={{}: (1, {})} | custom-call | flops 4294967296 | bytes 10485760 | tf_op jit(solution)/shard_map/pallas_call | solution.py:179
  165.7 0.0 copy-start
  165.7 0.0 collective-permute-done.8.refs_0_
  165.7 0.0 copy-start.3
  165.7 1.0 copy-done.3
  166.7 6.2 %shard_map.100.base_ref._ = f32[4,2,512,512]{3,2,1,0:T(8,128)} custom-call(f32[4,9]{1,0:T(4,128)} %pad_maximum_fusion.coef_ref._, f32[4,2,512,512]{3,2,1,0:T(8,128)} %shard_map.99.base_ref, f32[4,9]{1,0:T(4,128)} %pad_maximum_fusion.coef_ref._, bf16[1,2,512,512]{3,2,1,0:T(8,128)(2,1)} %copy-done.3, ...), custom_call_target="tpu_custom_call", output_to_operand_aliasing={{}: (1, {})} | custom-call | flops 2147483648 | bytes 7340032 | tf_op jit(solution)/shard_map/pallas_call | solution.py:179
  172.9 0.0 collective-permute-done.10.refs_1_
  172.9 0.0 collective-permute-done.9.refs_0_
  172.9 0.0 copy-done
  172.9 5.8 %shard_map.101 = (f32[2,512,512]{2,1,0:T(8,128)S(1)}, bf16[2,2,512,512]{3,2,1,0:T(8,128)(2,1)S(1)}, bf16[2,2,512,512]{3,2,1,0:T(8,128)(2,1)S(1)}) custom-call(f32[4,9]{1,0:T(4,128)S(1)} %copy-done, f32[4,2,512,512]{3,2,1,0:T(8,128)} %shard_map.100.base_ref._, bf16[8,2,512,512]{3,2,1,0:T(8,128)(2,1)} %get-tuple-element.17.refs_1_.refs_4_.refs_7_.refs_10_.left_ref, ...), custom_call_target="tpu_custom_call" | custom-call | flops 2147483648 | bytes 6291456 | tf_op jit(solution)/shard_map/pallas_call | solution.py:261
  178.7 10.1 %collective-permute-done.11.refs_0_ = bf16[1,1,512,512]{3,2,1,0:T(8,128)(2,1)S(1)} collective-permute-done((bf16[1,1,512,512]{3,2,1,0:T(8,128)(2,1)S(1)}, bf16[1,1,512,512]{3,2,1,0:T(8,128)(2,1)S(1)}, u32[]{:S(2)}, u32[]{:S(2)}) %collective-permute-start.11) | collective-permute-done | bytes 524320 | tf_op jit(solution)/shard_map/ppermute | solution.py:291
  188.8 0.1 collective-permute-done.12.refs_1_
  188.9 3.9 %shard_map.102 = f32[4,2,512,512]{3,2,1,0:T(8,128)} custom-call(f32[4,9]{1,0:T(4,128)S(1)} %copy-done, f32[4,2,512,512]{3,2,1,0:T(8,128)} %shard_map.100.base_ref._, f32[2,512,512]{2,1,0:T(8,128)S(1)} %get-tuple-element.25.total, bf16[2,2,512,512]{3,2,1,0:T(8,128)(2,1)S(1)} %get-tuple-element.26.left, ...), custom_call_target="tpu_custom_call", output_to_operand_aliasing={{}: (1, {})} | custom-call | flops 2147483648 | bytes 6291456 | tf_op jit(solution)/shard_map/pallas_call | solution.py:278
  (2 shorter events, 0.0 us)
Async XLA Ops:
  3.1 15.6 %copy-start.8 = (s32[7]{0:T(128)S(1)}, s32[7]{0:T(128)}, u32[]{:S(2)}) copy-start(s32[7]{0:T(128)} %param.15) | copy-start | bytes 88
  3.1 15.7 %copy-start.4 = (f32[7]{0:T(128)S(1)}, f32[7]{0:T(128)}, u32[]{:S(2)}) copy-start(f32[7]{0:T(128)} %_.1) | copy-start | bytes 88
  3.1 15.7 %copy-start.5 = (f32[7]{0:T(128)S(1)}, f32[7]{0:T(128)}, u32[]{:S(2)}) copy-start(f32[7]{0:T(128)} %param.17) | copy-start | bytes 88
  3.1 32.1 %collective-permute-start = (bf16[2,2,512,512]{3,2,1,0:T(8,128)(2,1)}, bf16[2,2,512,512]{3,2,1,0:T(8,128)(2,1)}, u32[]{:S(2)}, u32[]{:S(2)}) collective-permute-start(bf16[2,2,512,512]{3,2,1,0:T(8,128)(2,1)} %shard_map.91._.refs_0_.refs_3_.refs_6_), channel_id=1, source_target_pairs={{0,4},{4,0},{8,12},{12,8},{16,20},{20,16},{24,28},{28,24},{1,5},{5... | collective-permute-start | bytes 6291464 | tf_op jit(solution)/shard_map/ppermute | solution.py:291
  3.7 95.8 %collective-permute-start.3 = (bf16[2,2,512,512]{3,2,1,0:T(8,128)(2,1)}, bf16[2,2,512,512]{3,2,1,0:T(8,128)(2,1)S(1)}, u32[]{:S(2)}, u32[]{:S(2)}) collective-permute-start(bf16[2,2,512,512]{3,2,1,0:T(8,128)(2,1)} %shard_map.91._.refs_0_.refs_3_.refs_6_), channel_id=1, source_target_pairs={{0,16},{4,20},{8,24},{12,28},{16,0},{20,4},{24,8},{28,12},{1,17},{... | collective-permute-start | bytes 6291464 | tf_op jit(solution)/shard_map/ppermute | solution.py:291
  7.3 93.8 %collective-permute-start.4 = (bf16[2,2,512,512]{3,2,1,0:T(8,128)(2,1)}, bf16[2,2,512,512]{3,2,1,0:T(8,128)(2,1)}, u32[]{:S(2)}, u32[]{:S(2)}) collective-permute-start(bf16[2,2,512,512]{3,2,1,0:T(8,128)(2,1)} %shard_map.91._.refs_0_.refs_3_.refs_6_), channel_id=1, source_target_pairs={{0,8},{4,12},{8,0},{12,4},{16,24},{20,28},{24,16},{28,20},{1,9},{5... | collective-permute-start | bytes 6291464 | tf_op jit(solution)/shard_map/ppermute | solution.py:291
  17.0 45.1 %collective-permute-start.1 = (bf16[2,2,512,512]{3,2,1,0:T(8,128)(2,1)}, bf16[2,2,512,512]{3,2,1,0:T(8,128)(2,1)}, u32[]{:S(2)}, u32[]{:S(2)}) collective-permute-start(bf16[2,2,512,512]{3,2,1,0:T(8,128)(2,1)} %get-tuple-element.19.refs_6_.refs_0_.refs_3_), channel_id=1, source_target_pairs={{0,4},{4,0},{8,12},{12,8},{16,20},{20,16},{24,28},{28,24},{1,5},{5... | collective-permute-start | bytes 6291464 | tf_op jit(solution)/shard_map/ppermute | solution.py:291
  17.0 70.8 %collective-permute-start.2 = (bf16[3,2,512,512]{3,2,1,0:T(8,128)(2,1)}, bf16[3,2,512,512]{3,2,1,0:T(8,128)(2,1)}, u32[]{:S(2)}, u32[]{:S(2)}) collective-permute-start(bf16[3,2,512,512]{3,2,1,0:T(8,128)(2,1)} %get-tuple-element.20), channel_id=1, source_target_pairs={{0,1},{1,0},{2,3},{3,2},{4,5},{5,4},{6,7},{7,6},{8,9},{9,8},{10,11... | collective-permute-start | bytes 9437192 | tf_op jit(solution)/shard_map/ppermute | solution.py:291
  35.2 92.9 %collective-permute-start.5 = (bf16[4,2,512,512]{3,2,1,0:T(8,128)(2,1)}, bf16[4,2,512,512]{3,2,1,0:T(8,128)(2,1)S(1)}, u32[]{:S(2)}, u32[]{:S(2)}) collective-permute-start(bf16[4,2,512,512]{3,2,1,0:T(8,128)(2,1)} %get-tuple-element.21), channel_id=1, source_target_pairs={{0,2},{1,3},{2,0},{3,1},{4,6},{5,7},{6,4},{7,5},{8,10},{9,11},{10,... | collective-permute-start | bytes 12582920 | tf_op jit(solution)/shard_map/ppermute | solution.py:291
  62.0 82.1 %collective-permute-start.6 = (bf16[1,2,512,512]{3,2,1,0:T(8,128)(2,1)}, bf16[1,2,512,512]{3,2,1,0:T(8,128)(2,1)}, u32[]{:S(2)}, u32[]{:S(2)}) collective-permute-start(bf16[1,2,512,512]{3,2,1,0:T(8,128)(2,1)} %get-tuple-element.22), channel_id=1, source_target_pairs={{0,16},{4,20},{8,24},{12,28},{16,0},{20,4},{24,8},{28,12},{1,17},{... | collective-permute-start | bytes 3145736 | tf_op jit(solution)/shard_map/ppermute | solution.py:291
  87.8 11.7 %copy-start.7 = (bf16[1,1,512,512]{3,2,1,0:T(8,128)(2,1)S(1)}, bf16[1,1,512,512]{3,2,1,0:T(8,128)(2,1)}, u32[]{:S(2)}) copy-start(bf16[1,1,512,512]{3,2,1,0:T(8,128)(2,1)} %get-tuple-element.24) | copy-start | bytes 1572868
  87.9 68.5 %collective-permute-start.7 = (bf16[1,2,512,512]{3,2,1,0:T(8,128)(2,1)}, bf16[1,2,512,512]{3,2,1,0:T(8,128)(2,1)}, u32[]{:S(2)}, u32[]{:S(2)}) collective-permute-start(bf16[1,2,512,512]{3,2,1,0:T(8,128)(2,1)} %get-tuple-element.22), channel_id=1, source_target_pairs={{0,8},{4,12},{8,0},{12,4},{16,24},{20,28},{24,16},{28,20},{1,9},{5... | collective-permute-start | bytes 3145736 | tf_op jit(solution)/shard_map/ppermute | solution.py:291
  99.5 4.2 %copy-start.2 = (bf16[2,2,512,512]{3,2,1,0:T(8,128)(2,1)}, bf16[2,2,512,512]{3,2,1,0:T(8,128)(2,1)S(1)}, u32[]{:S(2)}) copy-start(bf16[2,2,512,512]{3,2,1,0:T(8,128)(2,1)S(1)} %collective-permute-done.3.refs_0_) | copy-start | bytes 6291460
  99.5 73.4 %collective-permute-start.10 = (bf16[1,1,512,512]{3,2,1,0:T(8,128)(2,1)S(1)}, bf16[1,1,512,512]{3,2,1,0:T(8,128)(2,1)S(1)}, u32[]{:S(2)}, u32[]{:S(2)}) collective-permute-start(bf16[1,1,512,512]{3,2,1,0:T(8,128)(2,1)S(1)} %copy-done.7), channel_id=1, source_target_pairs={{0,8},{4,12},{8,0},{12,4},{16,24},{20,28},{24,16},{28,20},{1,9},{5... | collective-permute-start | bytes 1572872 | tf_op jit(solution)/shard_map/ppermute | solution.py:291
  101.2 71.7 %collective-permute-start.9 = (bf16[1,1,512,512]{3,2,1,0:T(8,128)(2,1)S(1)}, bf16[1,1,512,512]{3,2,1,0:T(8,128)(2,1)S(1)}, u32[]{:S(2)}, u32[]{:S(2)}) collective-permute-start(bf16[1,1,512,512]{3,2,1,0:T(8,128)(2,1)S(1)} %copy-done.7), channel_id=1, source_target_pairs={{0,16},{4,20},{8,24},{12,28},{16,0},{20,4},{24,8},{28,12},{1,17},{... | collective-permute-start | bytes 1572872 | tf_op jit(solution)/shard_map/ppermute | solution.py:291
  128.1 1.9 %copy-start.1 = (bf16[4,2,512,512]{3,2,1,0:T(8,128)(2,1)}, bf16[4,2,512,512]{3,2,1,0:T(8,128)(2,1)S(1)}, u32[]{:S(2)}) copy-start(bf16[4,2,512,512]{3,2,1,0:T(8,128)(2,1)S(1)} %collective-permute-done.5.refs_0_) | copy-start | bytes 12582916
  128.1 16.1 %copy-start.6 = (bf16[1,1,512,512]{3,2,1,0:T(8,128)(2,1)S(1)}, bf16[1,1,512,512]{3,2,1,0:T(8,128)(2,1)}, u32[]{:S(2)}) copy-start(bf16[1,1,512,512]{3,2,1,0:T(8,128)(2,1)} %get-tuple-element.28) | copy-start | bytes 1572868
  128.1 37.6 %collective-permute-start.8 = (bf16[1,2,512,512]{3,2,1,0:T(8,128)(2,1)}, bf16[1,2,512,512]{3,2,1,0:T(8,128)(2,1)S(1)}, u32[]{:S(2)}, u32[]{:S(2)}) collective-permute-start(bf16[1,2,512,512]{3,2,1,0:T(8,128)(2,1)} %get-tuple-element.23), channel_id=1, source_target_pairs={{0,1},{1,0},{2,3},{3,2},{4,5},{5,4},{6,7},{7,6},{8,9},{9,8},{10,11... | collective-permute-start | bytes 3145736 | tf_op jit(solution)/shard_map/ppermute | solution.py:291
  144.2 44.6 %collective-permute-start.11 = (bf16[1,1,512,512]{3,2,1,0:T(8,128)(2,1)S(1)}, bf16[1,1,512,512]{3,2,1,0:T(8,128)(2,1)S(1)}, u32[]{:S(2)}, u32[]{:S(2)}) collective-permute-start(bf16[1,1,512,512]{3,2,1,0:T(8,128)(2,1)S(1)} %copy-done.6), channel_id=1, source_target_pairs={{0,16},{4,20},{8,24},{12,28},{16,0},{20,4},{24,8},{28,12},{1,17},{... | collective-permute-start | bytes 1572872 | tf_op jit(solution)/shard_map/ppermute | solution.py:291
  156.4 32.5 %collective-permute-start.12 = (bf16[1,1,512,512]{3,2,1,0:T(8,128)(2,1)S(1)}, bf16[1,1,512,512]{3,2,1,0:T(8,128)(2,1)S(1)}, u32[]{:S(2)}, u32[]{:S(2)}) collective-permute-start(bf16[1,1,512,512]{3,2,1,0:T(8,128)(2,1)S(1)} %copy-done.6), channel_id=1, source_target_pairs={{0,8},{4,12},{8,0},{12,4},{16,24},{20,28},{24,16},{28,20},{1,9},{5... | collective-permute-start | bytes 1572872 | tf_op jit(solution)/shard_map/ppermute | solution.py:291
  165.7 7.2 %copy-start = (f32[4,9]{1,0:T(4,128)S(1)}, f32[4,9]{1,0:T(4,128)}, u32[]{:S(2)}) copy-start(f32[4,9]{1,0:T(4,128)} %pad_maximum_fusion.coef_ref._) | copy-start | bytes 436
  165.7 1.0 copy-start.3

commit v2 on v1

--- a/solution.py
+++ b/solution.py
@@ -41,13 +41,50 @@
         reads[index, part].wait()
         kept = rounded[0].at[place]
         kept[...] = source[place].astype(jnp.bfloat16)
-        for (first, span, only), out_ref in zip(groups, outs):
-            if first <= index < first + span and only in (None, part):
-                target = out_ref.at[index - first, part if only is None else 0]
-                writes.append(pltpu.make_async_copy(kept, target, stores.at[len(writes)]))
-                writes[-1].start()
+        for (first, span, cut), out_ref in zip(groups, outs):
+            if not first <= index < first + span or cut and cut[0] != part:
+                continue
+            rows = pl.ds(cut[1], cut[2]) if cut else pl.ds(0, kept.shape[0])
+            target = out_ref.at[index - first, 0 if cut else part]
+            writes.append(pltpu.make_async_copy(kept.at[rows], target, stores.at[len(writes)]))
+            writes[-1].start()
     for write in writes:
         write.wait()
+
+
+def round_first_kernel(low, density_ref, out_ref, source, loads):
+    span, parts = out_ref.shape[:2]
+    pairs = [(index, part) for index in range(span) for part in range(parts)]
+    reads = [
+        pltpu.make_async_copy(
+            density_ref.at[low + index, part], source.at[index, part], loads.at[place]
+        )
+        for place, (index, part) in enumerate(pairs)
+    ]
+    for read in reads:
+        read.start()
+    for read, pair in zip(reads, pairs):
+        read.wait()
+        out_ref[pair] = source[pair].astype(jnp.bfloat16)
+
+
+def round_first(density, group):
+    n = density.shape[-1]
+    low, span, _ = group
+    return pl.pallas_call(
+        functools.partial(round_first_kernel, low),
+        in_specs=[pl.BlockSpec(memory_space=pl.ANY)],
+        out_specs=pl.BlockSpec(memory_space=pltpu.VMEM),
+        out_shape=pltpu.VMEM((span, 2, n, n), jnp.bfloat16),
+        scratch_shapes=[
+            pltpu.VMEM((span, 2, n, n), jnp.float32),
+            pltpu.SemaphoreType.DMA((2 * span,)),
+        ],
+        compiler_params=pltpu.CompilerParams(vmem_limit_bytes=VMEM_LIMIT),
+        cost_estimate=pl.CostEstimate(
+            flops=0, bytes_accessed=n * n * 12 * span, transcendentals=0
+        ),
+    )(density)
 
 
 def round_groups(density, groups, after):
@@ -55,16 +92,14 @@
     low = min(first for first, _, _ in groups)
     high = max(first + span for first, span, _ in groups)
     parts = 2 * (high - low)
-    writes = sum(span * (2 if part is None else 1) for _, span, part in groups)
+    shapes = [(span, 1, cut[2], n) if cut else (span, 2, n, n) for _, span, cut in groups]
+    writes = sum(shape[0] * shape[1] for shape in shapes)
     anywhere = pl.BlockSpec(memory_space=pl.ANY)
     return pl.pallas_call(
         functools.partial(round_kernel, groups, low, high),
         in_specs=[anywhere, anywhere],
         out_specs=[anywhere] * len(groups),
-        out_shape=[
-            jax.ShapeDtypeStruct((span, 2 if part is None else 1, n, n), jnp.bfloat16)
-            for _, span, part in groups
-        ],
+        out_shape=[jax.ShapeDtypeStruct(shape, jnp.bfloat16) for shape in shapes],
         scratch_shapes=[
             pltpu.VMEM((parts, n, n), jnp.float32),
             pltpu.SemaphoreType.DMA((parts,)),
@@ -141,22 +176,13 @@
         real, imag = rate * base_ref[0, 0], rate * base_ref[0, 1]
     else:
         real, imag = base_ref[0, 0], base_ref[0, 1]
-    for t, (mode, part) in enumerate(terms):
+    for t, mode in enumerate(terms):
         rho, left, right = refs[3 * t : 3 * t + 3]
         coef = coef_ref[index, mode]
         lr, li, rr, ri = left[0, 0], left[0, 1], right[0, 0], right[0, 1]
-        if part is None:
-            a, b = rho[0, 0], rho[0, 1]
-            real += coef * (dot(lr, a) - dot(li, b) + dot(a, rr) - dot(b, ri))
-            imag += coef * (dot(lr, b) + dot(li, a) + dot(a, ri) + dot(b, rr))
-        elif part == 0:
-            a = rho[0, 0]
-            real += coef * (dot(lr, a) + dot(a, rr))
-            imag += coef * (dot(li, a) + dot(a, ri))
-        else:
-            b = rho[0, 0]
-            real -= coef * (dot(li, b) + dot(b, ri))
-            imag += coef * (dot(lr, b) + dot(b, rr))
+        a, b = rho[0, 0], rho[0, 1]
+        real += coef * (dot(lr, a) - dot(li, b) + dot(a, rr) - dot(b, ri))
+        imag += coef * (dot(lr, b) + dot(li, a) + dot(a, ri) + dot(b, rr))
     out_ref[0, 0] = real
     out_ref[0, 1] = imag
 
@@ -168,46 +194,51 @@
     n = base.shape[-1]
     lefts, rights = operators
     specs, args = [], []
-    for mode, part, array, place in terms:
-        specs.append(
-            pl.BlockSpec((1, 2 if part is None else 1, n, n), lambda g, place=place: (place(g), 0, 0, 0))
-        )
+    for mode, array, place in terms:
+        specs.append(pl.BlockSpec((1, 2, n, n), lambda g, place=place: (place(g), 0, 0, 0)))
         operator = pl.BlockSpec((1, 2, n, n), lambda g, mode=mode: (mode, 0, 0, 0))
         specs += [operator, operator]
         args += [array, lefts, rights]
     block = pl.BlockSpec((1, 2, n, n), lambda g: (first + g, 0, 0, 0))
     return pl.pallas_call(
-        functools.partial(term_kernel, first, [t[:2] for t in terms], fresh),
+        functools.partial(term_kernel, first, [t[0] for t in terms], fresh),
         grid=(span,),
         in_specs=[SMEM, block, pl.BlockSpec(memory_space=pl.ANY)] + specs,
         out_specs=block,
         out_shape=jax.ShapeDtypeStruct(base.shape, jnp.float32),
         input_output_aliases=alias,
         **params(
-            16 * n**3 * span * sum(1 if t[1] is None else 0.5 for t in terms),
+            16 * n**3 * span * len(terms),
             n * n * span * (16 + 4 * len(terms)) + 8 * n * n * len(terms),
         ),
     )(coef, base, into, *args)
 
 
-def part_terms(index, out, terms, coef_ref, arrays, left, right):
-    change = None
-    for t, (mode, part) in enumerate(terms):
-        use = part if out == 0 else 1 - part
+def add_piece(index, modes, cut, out, rows, coef_ref, arrays, left, right, sum_in, sum_out):
+    part, first, size = cut
+    use = part if out == 0 else 1 - part
+    own = max(first, rows[0]), min(first + size, rows[1])
+    total = sum_in[out, rows[0] : rows[1]]
+    for t, mode in enumerate(modes):
         coef = coef_ref[index, mode]
-        if out == 0 and part == 1:
-            coef = -coef
-        value = arrays[t][0, 0]
-        term = coef * (dot(left[t, use], value) + dot(value, right[t, use]))
-        change = term if change is None else change + term
-    return change
-
-
-def stage_kernel(index, terms, coef_ref, base_ref, left_ref, right_ref, *refs):
-    count = len(terms)
+        coef = -coef if out == 0 and part == 1 else coef
+        total += coef * dot(left[t, use, rows[0] : rows[1], first : first + size], arrays[t][0, 0])
+    sum_out[out, rows[0] : rows[1]] = total
+    if own[0] < own[1]:
+        total = sum_out[out, own[0] : own[1]]
+        for t, mode in enumerate(modes):
+            coef = coef_ref[index, mode]
+            coef = -coef if out == 0 and part == 1 else coef
+            value = arrays[t][0, 0, own[0] - first : own[1] - first]
+            total += coef * dot(value, right[t, use])
+        sum_out[out, own[0] : own[1]] = total
+
+
+def first_piece_kernel(index, modes, cut, coef_ref, base_ref, left_ref, right_ref, *refs):
+    count = len(modes)
     arrays, (total, left, right, loads) = refs[:count], refs[count:]
     copies = [pltpu.make_async_copy(base_ref.at[index], total, loads.at[0])]
-    for t, (mode, _) in enumerate(terms):
+    for t, mode in enumerate(modes):
         for source, target in ((left_ref, left), (right_ref, right)):
             copies.append(
                 pltpu.make_async_copy(source.at[mode], target.at[t], loads.at[len(copies)])
@@ -216,20 +247,36 @@
         copy.start()
     for copy in copies:
         copy.wait()
+    rows = 0, total.shape[1]
     for out in range(2):
-        total[out] += part_terms(index, out, terms, coef_ref, arrays, left, right)
-
-
-def finish_kernel(index, terms, coef_ref, _, total, left, right, *refs):
-    count = len(terms)
+        add_piece(index, modes, cut, out, rows, coef_ref, arrays, left, right, total, total)
+
+
+def next_piece_kernel(index, modes, cut, coef_ref, total, left, right, *refs):
+    arrays, out_ref = refs[:-1], refs[-1]
+    rows = 0, total.shape[1]
+    for out in range(2):
+        add_piece(index, modes, cut, out, rows, coef_ref, arrays, left, right, total, out_ref)
+
+
+def last_piece_kernel(index, modes, cut, coef_ref, _, total, left, right, *refs):
+    count = len(modes)
     arrays, (out_ref, result, stores) = refs[:count], refs[count:]
+    n = total.shape[1]
+    bands = [(cut[1], cut[1] + cut[2]), (0, cut[1]), (cut[1] + cut[2], n)]
     writes = []
     for out in range(2):
-        result[out] = total[out] + part_terms(index, out, terms, coef_ref, arrays, left, right)
-        writes.append(
-            pltpu.make_async_copy(result.at[out], out_ref.at[index, out], stores.at[out])
-        )
-        writes[-1].start()
+        for rows in bands:
+            if rows[0] == rows[1]:
+                continue
+            add_piece(index, modes, cut, out, rows, coef_ref, arrays, left, right, total, result)
+            band = pl.ds(rows[0], rows[1] - rows[0])
+            writes.append(
+                pltpu.make_async_copy(
+                    result.at[out, band], out_ref.at[index, out, band], stores.at[len(writes)]
+                )
+            )
+            writes[-1].start()
     for write in writes:
         write.wait()
 
@@ -242,48 +289,61 @@
     return pltpu.with_memory_space_constraint(array, pltpu.HBM)
 
 
-def last_params(n, count):
-    return dict(
+ANYWHERE = pl.BlockSpec(memory_space=pl.ANY)
+WHOLE = pl.BlockSpec(memory_space=pltpu.VMEM)
+
+
+def piece_call(kernel, index, modes, cut, n, operands, arrays, out_shape, scratch, alias):
+    moved = n * n * (16 + 8 * len(modes))
+    out_specs = jax.tree.map(
+        lambda shape: ANYWHERE if isinstance(shape, jax.ShapeDtypeStruct) else WHOLE, out_shape
+    )
+    return pl.pallas_call(
+        functools.partial(kernel, index, modes, cut),
+        in_specs=[SMEM] + [spec for _, spec in operands[1:]] + [WHOLE] * len(arrays),
+        out_specs=out_specs,
+        out_shape=out_shape,
+        scratch_shapes=scratch,
+        input_output_aliases=alias,
         compiler_params=pltpu.CompilerParams(vmem_limit_bytes=LAST_VMEM_LIMIT),
         cost_estimate=pl.CostEstimate(
-            flops=8 * n**3 * count, bytes_accessed=n * n * (8 + 8 * count), transcendentals=0
-        ),
-    )
-
-
-ANYWHERE = pl.BlockSpec(memory_space=pl.ANY)
-WHOLE = pl.BlockSpec(memory_space=pltpu.VMEM)
-
-
-def stage_last(base, coef, operators, index, terms):
+            flops=8 * n * n * cut[2] * len(modes), bytes_accessed=moved, transcendentals=0
+        ),
+    )(*[array for array, _ in operands], *[in_vmem(array) for array in arrays])
+
+
+def first_piece(base, coef, operators, index, modes, cut, arrays):
+    n, count = base.shape[-1], len(modes)
+    operands = [(coef, SMEM)] + [(in_hbm(array), ANYWHERE) for array in (base, *operators)]
+    out_shape = [
+        pltpu.VMEM((2, n, n), jnp.float32),
+        pltpu.VMEM((count, 2, n, n), jnp.bfloat16),
+        pltpu.VMEM((count, 2, n, n), jnp.bfloat16),
+    ]
+    scratch = [pltpu.SemaphoreType.DMA((1 + 2 * count,))]
+    return piece_call(
+        first_piece_kernel, index, modes, cut, n, operands, arrays, out_shape, scratch, {}
+    )
+
+
+def next_piece(staged, coef, index, modes, cut, arrays):
+    n = staged[0].shape[-1]
+    operands = [(coef, SMEM)] + [(in_vmem(array), WHOLE) for array in staged]
+    out_shape = pltpu.VMEM((2, n, n), jnp.float32)
+    total = piece_call(
+        next_piece_kernel, index, modes, cut, n, operands, arrays, out_shape, [], {1: 0}
+    )
+    return [total] + list(staged[1:])
+
+
+def last_piece(base, staged, coef, index, modes, cut, arrays):
     n = base.shape[-1]
-    count = len(terms)
-    return pl.pallas_call(
-        functools.partial(stage_kernel, index, [t[:2] for t in terms]),
-        in_specs=[SMEM] + [ANYWHERE] * 3 + [WHOLE] * count,
-        out_specs=[WHOLE] * 3,
-        out_shape=[
-            pltpu.VMEM((2, n, n), jnp.float32),
-            pltpu.VMEM((count, 2, n, n), jnp.bfloat16),
-            pltpu.VMEM((count, 2, n, n), jnp.bfloat16),
-        ],
-        scratch_shapes=[pltpu.SemaphoreType.DMA((1 + 2 * count,))],
-        **last_params(n, count),
-    )(coef, *[in_hbm(array) for array in (base, *operators)], *[in_vmem(t[2]) for t in terms])
-
-
-def finish_last(base, coef, staged, index, terms):
-    n = base.shape[-1]
-    count = len(terms)
-    return pl.pallas_call(
-        functools.partial(finish_kernel, index, [t[:2] for t in terms]),
-        in_specs=[SMEM, ANYWHERE] + [WHOLE] * (3 + count),
-        out_specs=ANYWHERE,
-        out_shape=jax.ShapeDtypeStruct(base.shape, jnp.float32),
-        scratch_shapes=[pltpu.VMEM((2, n, n), jnp.float32), pltpu.SemaphoreType.DMA((2,))],
-        input_output_aliases={1: 0},
-        **last_params(n, count),
-    )(coef, base, *[in_vmem(part) for part in staged], *[in_vmem(t[2]) for t in terms])
+    operands = [(coef, SMEM), (base, ANYWHERE)] + [(in_vmem(array), WHOLE) for array in staged]
+    out_shape = jax.ShapeDtypeStruct(base.shape, jnp.float32)
+    scratch = [pltpu.VMEM((2, n, n), jnp.float32), pltpu.SemaphoreType.DMA((6,))]
+    return piece_call(
+        last_piece_kernel, index, modes, cut, n, operands, arrays, out_shape, scratch, {1: 0}
+    )
 
 
 def flip(value, axis, bit):
@@ -339,14 +399,19 @@
     plan += [(slow,) + piece + (None,) for piece in pieces[1:]]
     if last:
         plan.append((middle[:1], last, 1, None))
-    plan += [(slow, last, 1, part) for part in range(2)]
+    n = density.shape[-1]
+    cuts = [(0, 0, n), (1, 0, n // 2), (1, n // 2, n // 2)]
+    plan += [(slow, last, 1, cut) for cut in cuts]
 
     plan = [step for place, step in enumerate(plan) if step[0] or place < len(spans)]
 
     groups = list(dict.fromkeys([step[1:] for step in plan]))
     early = [step[1:] for step in plan if step[0] is slow][:1]
     late = [group for group in groups if group not in early]
-    rounded = dict(zip(early, round_groups(density, early, damping_rate)))
+    if early[0][2] is None:
+        rounded = {early[0]: round_first(density, early[0])}
+    else:
+        rounded = dict(zip(early, round_groups(density, early, damping_rate)))
     rounded.update(zip(late, round_groups(density, late, rounded[early[0]])))
 
     sent = [[flip(rounded[step[1:]], *axis_of(m)) for m in step[0]] for step in plan]
@@ -357,27 +422,29 @@
 
     def local_terms(span):
         own, other = rounded[span + (None,)], rounded[(half - span[0],) + span[1:] + (None,)]
-        terms = [(modes, None, own, lambda g: g)]
+        terms = [(modes, own, lambda g: g)]
         for mode in range(local_bits):
             step = 1 << mode
             if step < span[1]:
-                terms.append((mode, None, own, lambda g, step=step: g ^ step))
+                terms.append((mode, own, lambda g, step=step: g ^ step))
             else:
-                terms.append((mode, None, other, lambda g: g))
+                terms.append((mode, other, lambda g: g))
         return terms
 
     result, staged = None, None
-    for place, ((step_modes, first, span, part), arrays) in enumerate(zip(plan, sent)):
-        terms = [(m, part, array, lambda g: g) for m, array in zip(step_modes, arrays)]
+    for place, ((step_modes, first, span, cut), arrays) in enumerate(zip(plan, sent)):
+        terms = [(m, array, lambda g: g) for m, array in zip(step_modes, arrays)]
         if place < len(spans):
             terms = local_terms(spans[place]) + terms
             result = add_terms(density, result, coef, operators, first, span, terms)
-        elif part is None:
+        elif cut is None:
             result = add_terms(result, result, coef, operators, first, span, terms)
-        elif part == 0:
-            staged = stage_last(result, coef, operators, first, terms)
+        elif cut == cuts[0]:
+            staged = first_piece(result, coef, operators, first, step_modes, cut, arrays)
+        elif cut != cuts[-1]:
+            staged = next_piece(staged, coef, first, step_modes, cut, arrays)
         else:
-            result = finish_last(result, coef, staged, first, terms)
+            result = last_piece(result, staged, coef, first, step_modes, cut, arrays)
     return result
 
 

time: 193 us -> 191 us (0.990)
  waiting for transfers between devices: 33.1 us -> 30.1 us
    pallas_call x9 -> x11, Pallas kernels: 115 us -> 118 us  [the longest x7 105 us: add_terms(): pl.pallas_call(functools.partial(term_kernel, first, [t[0] for t in terms...]
    pallas_call x2 -> x1, Pallas kernels: 11.2 us -> 7.9 us  [round_groups(): pl.pallas_call(functools.partial(round_kernel, groups, low, high), in_spe...]
    ppermute x13 -> x15, waiting for transfers between devices: 33.1 us -> 30.1 us  [flip(): return lax.ppermute(value, axis, pairs)]
    ppermute x13 -> x15, starting transfers between devices: 14.5 us -> 15.6 us  [flip(): return lax.ppermute(value, axis, pairs)]
  transfers between devices with their start and end apart: 13 -> 15, of which waited for: 6 -> 5; matrix products, arithmetic and copies ran while one was open for 1% -> 1% of each run, Pallas kernels for 70% -> 72%
where the time goes in v2:
time: 191 us
  Pallas kernels  141 us (74%)
  waiting for transfers between devices  30.1 us (16%)
  starting transfers between devices  15.6 us (8%)
  local copies, waits for them, and re-layouts  2.09 us (1%)
    pallas_call x7, Pallas kernels, add_terms(): pl.pallas_call(functools.partial(term_kernel, first, [t[0] for t in terms...  105 us
    ppermute x15, waiting for transfers between devices, flip(): return lax.ppermute(value, axis, pairs)  30.1 us
    ppermute x15, starting transfers between devices, flip(): return lax.ppermute(value, axis, pairs)  15.6 us
    pallas_call x1, Pallas kernels, make_operators(): pl.pallas_call(operator_kernel, grid_spec=pltpu.PrefetchScalarGridSpec(nu...  15.4 us
    pallas_call x3, Pallas kernels, piece_call(): pl.pallas_call(functools.partial(kernel, index, modes, cut), in_specs=[SM...  10.7 us
    pallas_call x1, Pallas kernels, round_groups(): pl.pallas_call(functools.partial(round_kernel, groups, low, high), in_spe...  7.9 us
  transfers between devices with their start and end apart: 15, of which 5 were waited for; matrix products, arithmetic and copies ran while one was open for 1% of the time, Pallas kernels for 72%

profile of v2, /device:TPU:0, one launch (start us, length us, event | category | flops | bytes accessed | tf_op | source)
XLA Modules:
  0.0 190.8 jit_solution(7368526853260938561)
XLA Ops:
  0.0 2.3 %shard_map.91._.refs_0_.refs_3_.refs_6_ = bf16[2,2,512,512]{3,2,1,0:T(8,128)(2,1)S(1)} custom-call(f32[4,2,512,512]{3,2,1,0:T(8,128)} %base_ref.3), custom_call_target="tpu_custom_call" | custom-call | bytes 6291456 | tf_op jit(solution)/shard_map/pallas_call | solution.py:74
  2.3 0.0 copy-start
  2.3 0.0 copy-start.11
  2.3 0.0 copy-start.5
  2.3 0.0 copy-start.6
  2.3 0.5 collective-permute-start
  2.8 3.7 %collective-permute-start.3 = (bf16[2,2,512,512]{3,2,1,0:T(8,128)(2,1)S(1)}, bf16[2,2,512,512]{3,2,1,0:T(8,128)(2,1)}, u32[]{:S(2)}, u32[]{:S(2)}) collective-permute-start(bf16[2,2,512,512]{3,2,1,0:T(8,128)(2,1)S(1)} %shard_map.91._.refs_0_.refs_3_.refs_6_), channel_id=1, source_target_pairs={{0,16},{4,20},{8,24},{12,28},{16,0},{20,4},{24,8},{28,12},{1,17},{... | collective-permute-start | bytes 6291464 | tf_op jit(solution)/shard_map/ppermute | solution.py:351
  6.5 1.6 collective-permute-start.4
  8.1 0.0 copy-done
  8.1 7.9 %shard_map.93 = (bf16[2,2,512,512]{3,2,1,0:T(8,128)(2,1)}, bf16[3,2,512,512]{3,2,1,0:T(8,128)(2,1)}, bf16[4,2,512,512]{3,2,1,0:T(8,128)(2,1)}, bf16[1,2,512,512]...) custom-call(f32[4,2,512,512]{3,2,1,0:T(8,128)} %base_ref.3, ...), custom_call_target="tpu_custom_call" | custom-call | bytes 21495808 | tf_op jit(solution)/shard_map/pallas_call | solution.py:98
  16.0 0.1 collective-permute-start.1
  16.1 1.6 collective-permute-start.2
  17.6 0.1 shift-right-arithmetic_and_fusion
  17.7 0.0 copy-done.11
  17.7 0.2 reduce_window_sum.11
  17.9 0.0 copy-done.5
  17.9 0.0 copy-done.6
  17.9 0.2 fusion.5
  18.1 0.1 copy.18
  18.2 0.1 pad.1.clone
  18.2 15.4 %shard_map.92 = (bf16[8,2,512,512]{3,2,1,0:T(8,128)(2,1)}, bf16[8,2,512,512]{3,2,1,0:T(8,128)(2,1)}) custom-call(s32[7]{0:T(128)} %slot_ref.1, s32[7,2,8,8]{3,2,1,0:T(8,128)} %mask_ref.1, bf16[7,2,512,512]{3,2,1,0:T(8,128)(2,1)} %left_ref.1, bf16[7,2,512,512]{3,2,1,0:T(8,128)(2,1)} %right_ref.1, bf16[2,512,512]{2,1,0:T(8,128)(2,1)} %ham_ref.1), custom_call_target="tpu_custom_call" | custom-call | bytes 33554432 | tf_op jit(solution)/shard_map/pallas_call | solution.py:153
  33.6 0.7 pad_maximum_fusion.coef_ref._
  34.3 0.0 collective-permute-done.refs_9_
  34.3 1.5 collective-permute-start.5
  35.8 25.3 %shard_map.94._ = f32[4,2,512,512]{3,2,1,0:T(8,128)} custom-call(f32[4,9]{1,0:T(4,128)} %pad_maximum_fusion.coef_ref._, f32[4,2,512,512]{3,2,1,0:T(8,128)} %base_ref.3, f32[4,9]{1,0:T(4,128)} %pad_maximum_fusion.coef_ref._, bf16[2,2,512,512]{3,2,1,0:T(8,128)(2,1)} %copy-done, ...), custom_call_target="tpu_custom_call" | custom-call | flops 17179869184 | bytes 25165824 | tf_op jit(solution)/shard_map/pallas_call | solution.py:203
  61.1 0.0 collective-permute-done.1.refs_9_
  61.1 0.0 copy-done.8
  61.2 0.4 collective-permute-start.6
  61.6 25.4 %shard_map.95.base_ref = f32[4,2,512,512]{3,2,1,0:T(8,128)} custom-call(f32[4,9]{1,0:T(4,128)} %pad_maximum_fusion.coef_ref._, f32[4,2,512,512]{3,2,1,0:T(8,128)} %base_ref.3, f32[4,2,512,512]{3,2,1,0:T(8,128)} %shard_map.94._, bf16[2,2,512,512]{3,2,1,0:T(8,128)(2,1)} %get-tuple-element.20.refs_6_.refs_0_.refs_3_, ...), custom_call_target="tpu_custom_call", output_to_operand_aliasing={{}: (2, {})} | custom-call | flops 17179869184 | bytes 25165824 | tf_op jit(solution)/shard_map/pallas_call | solution.py:203
  86.9 0.0 collective-permute-done.2.refs_0_
  86.9 0.8 collective-permute-start.7
  87.8 11.2 %shard_map.96.base_ref = f32[4,2,512,512]{3,2,1,0:T(8,128)} custom-call(f32[4,9]{1,0:T(4,128)} %pad_maximum_fusion.coef_ref._, f32[4,2,512,512]{3,2,1,0:T(8,128)} %shard_map.95.base_ref, f32[4,9]{1,0:T(4,128)} %pad_maximum_fusion.coef_ref._, bf16[3,2,512,512]{3,2,1,0:T(8,128)(2,1)} %collective-permute-done.2.refs_0_, ...), custom_call_target="tpu_custom_call", output_to_operand_aliasing={{}: (1, {})} | custom-call | flops 6442450944 | bytes 17825792 | tf_op jit(solution)/shard_map/pallas_call | solution.py:203
  98.9 0.0 collective-permute-done.3.refs_0_
  98.9 1.3 collective-permute-start.10
  100.3 0.0 collective-permute-done.4.refs_3_
  100.3 2.5 %collective-permute-start.9 = (bf16[1,1,512,512]{3,2,1,0:T(8,128)(2,1)}, bf16[1,1,512,512]{3,2,1,0:T(8,128)(2,1)S(1)}, u32[]{:S(2)}, u32[]{:S(2)}) collective-permute-start(bf16[1,1,512,512]{3,2,1,0:T(8,128)(2,1)} %get-tuple-element.25), channel_id=1, source_target_pairs={{0,16},{4,20},{8,24},{12,28},{16,0},{20,4},{24,8},{28,12},{1,17},{... | collective-permute-start | bytes 1572872 | tf_op jit(solution)/shard_map/ppermute | solution.py:351
  102.8 14.3 %shard_map.97.base_ref = f32[4,2,512,512]{3,2,1,0:T(8,128)} custom-call(f32[4,9]{1,0:T(4,128)} %pad_maximum_fusion.coef_ref._, f32[4,2,512,512]{3,2,1,0:T(8,128)} %shard_map.96.base_ref, f32[4,9]{1,0:T(4,128)} %pad_maximum_fusion.coef_ref._, bf16[2,2,512,512]{3,2,1,0:T(8,128)(2,1)} %collective-permute-done.3.refs_0_, ...), custom_call_target="tpu_custom_call", output_to_operand_aliasing={{}: (1, {})} | custom-call | flops 8589934592 | bytes 16777216 | tf_op jit(solution)/shard_map/pallas_call | solution.py:203
  117.1 10.2 %collective-permute-done.5.refs_0_ = bf16[4,2,512,512]{3,2,1,0:T(8,128)(2,1)} collective-permute-done((bf16[4,2,512,512]{3,2,1,0:T(8,128)(2,1)}, bf16[4,2,512,512]{3,2,1,0:T(8,128)(2,1)}, u32[]{:S(2)}, u32[]{:S(2)}) %collective-permute-start.5) | collective-permute-done | bytes 4194336 | tf_op jit(solution)/shard_map/ppermute | solution.py:351
  127.2 0.0 copy-done.7
  127.2 0.5 collective-permute-start.8
  127.8 13.6 %shard_map.98.base_ref = f32[4,2,512,512]{3,2,1,0:T(8,128)} custom-call(f32[4,9]{1,0:T(4,128)} %pad_maximum_fusion.coef_ref._, f32[4,2,512,512]{3,2,1,0:T(8,128)} %shard_map.97.base_ref, f32[4,9]{1,0:T(4,128)} %pad_maximum_fusion.coef_ref._, bf16[4,2,512,512]{3,2,1,0:T(8,128)(2,1)} %collective-permute-done.5.refs_0_, ...), custom_call_target="tpu_custom_call", output_to_operand_aliasing={{}: (1, {})} | custom-call | flops 8589934592 | bytes 23068672 | tf_op jit(solution)/shard_map/pallas_call | solution.py:203
  141.4 1.6 collective-permute-done.6.refs_0_
  143.0 0.0 copy-done.10
  143.0 0.0 collective-permute-start.11
  143.0 12.2 %collective-permute-done.7.refs_3_ = bf16[1,2,512,512]{3,2,1,0:T(8,128)(2,1)S(1)} collective-permute-done((bf16[1,2,512,512]{3,2,1,0:T(8,128)(2,1)S(1)}, bf16[1,2,512,512]{3,2,1,0:T(8,128)(2,1)S(1)}, u32[]{:S(2)}, u32[]{:S(2)}) %collective-permute-start.7) | collective-permute-done | bytes 1048608 | tf_op jit(solution)/shard_map/ppermute | solution.py:351
  155.2 0.0 collective-permute-start.12
  155.2 0.0 copy-done.3
  155.2 1.0 copy-done.4
  156.2 9.3 %shard_map.99.base_ref = f32[4,2,512,512]{3,2,1,0:T(8,128)} custom-call(f32[4,9]{1,0:T(4,128)} %pad_maximum_fusion.coef_ref._, f32[4,2,512,512]{3,2,1,0:T(8,128)} %shard_map.98.base_ref, f32[4,9]{1,0:T(4,128)} %pad_maximum_fusion.coef_ref._, bf16[1,2,512,512]{3,2,1,0:T(8,128)(2,1)} %copy-done.3, ...), custom_call_target="tpu_custom_call", output_to_operand_aliasing={{}: (1, {})} | custom-call | flops 4294967296 | bytes 10485760 | tf_op jit(solution)/shard_map/pallas_call | solution.py:203
  165.6 0.0 collective-permute-done.8.refs_0_
  165.6 0.1 collective-permute-start.13
  165.6 0.9 copy-done.2
  166.6 6.2 %shard_map.100.base_ref._ = f32[4,2,512,512]{3,2,1,0:T(8,128)} custom-call(f32[4,9]{1,0:T(4,128)} %pad_maximum_fusion.coef_ref._, f32[4,2,512,512]{3,2,1,0:T(8,128)} %shard_map.99.base_ref, f32[4,9]{1,0:T(4,128)} %pad_maximum_fusion.coef_ref._, bf16[1,2,512,512]{3,2,1,0:T(8,128)(2,1)} %copy-done.2, ...), custom_call_target="tpu_custom_call", output_to_operand_aliasing={{}: (1, {})} | custom-call | flops 2147483648 | bytes 7340032 | tf_op jit(solution)/shard_map/pallas_call | solution.py:203
  172.7 0.0 collective-permute-done.10.refs_1_
  172.7 1.1 collective-permute-start.14
  173.8 0.0 collective-permute-done.9.refs_0_
  173.8 0.0 copy-done.1
  173.8 5.8 %shard_map.101 = (f32[2,512,512]{2,1,0:T(8,128)S(1)}, bf16[2,2,512,512]{3,2,1,0:T(8,128)(2,1)S(1)}, bf16[2,2,512,512]{3,2,1,0:T(8,128)(2,1)S(1)}) custom-call(f32[4,9]{1,0:T(4,128)S(1)} %copy-done.1, f32[4,2,512,512]{3,2,1,0:T(8,128)} %shard_map.100.base_ref._, bf16[8,2,512,512]{3,2,1,0:T(8,128)(2,1)} %get-tuple-element.18.refs_1_.refs_4_.refs_7_.refs_10_.left_ref, ...), custom_call_target="tpu_custom_call" | custom-call | flops 2147483648 | bytes 8388608 | tf_op jit(solution)/shard_map/pallas_call | solution.py:301
  179.6 0.0 collective-permute-done.11.refs_0_
  179.6 0.0 collective-permute-done.12.refs_1_
  179.6 2.1 %shard_map.102.total = f32[2,512,512]{2,1,0:T(8,128)S(1)} custom-call(f32[4,9]{1,0:T(4,128)S(1)} %copy-done.1, f32[2,512,512]{2,1,0:T(8,128)S(1)} %get-tuple-element.26.total, bf16[2,2,512,512]{3,2,1,0:T(8,128)(2,1)S(1)} %get-tuple-element.27.left, bf16[2,2,512,512]{3,2,1,0:T(8,128)(2,1)S(1)} %get-tuple-element.28.right, ...), custom_call_target="tpu_custom_call", output_to_operand_aliasing={{}: (1, {})} | custom-call | flops 1073741824 | bytes 8388608 | tf_op jit(solution)/shard_map/pallas_call | solution.py:301
  181.8 6.0 %collective-permute-done.13.refs_0_ = bf16[1,1,256,512]{3,2,1,0:T(8,128)(2,1)S(1)} collective-permute-done((bf16[1,1,256,512]{3,2,1,0:T(8,128)(2,1)S(1)}, bf16[1,1,256,512]{3,2,1,0:T(8,128)(2,1)S(1)}, u32[]{:S(2)}, u32[]{:S(2)}) %collective-permute-start.13) | collective-permute-done | bytes 262176 | tf_op jit(solution)/shard_map/ppermute | solution.py:351
  187.8 0.1 collective-permute-done.14.refs_1_
  187.8 2.7 %shard_map.103 = f32[4,2,512,512]{3,2,1,0:T(8,128)} custom-call(f32[4,9]{1,0:T(4,128)S(1)} %copy-done.1, f32[4,2,512,512]{3,2,1,0:T(8,128)} %shard_map.100.base_ref._, f32[2,512,512]{2,1,0:T(8,128)S(1)} %shard_map.102.total, bf16[2,2,512,512]{3,2,1,0:T(8,128)(2,1)S(1)} %get-tuple-element.27.left, ...), custom_call_target="tpu_custom_call", output_to_operand_aliasing={{}: (1, {})} | custom-call | flops 1073741824 | bytes 8388608 | tf_op jit(solution)/shard_map/pallas_call | solution.py:301
  (11 shorter events, 0.0 us)
Async XLA Ops:
  2.3 5.8 %copy-start = (bf16[2,2,512,512]{3,2,1,0:T(8,128)(2,1)}, bf16[2,2,512,512]{3,2,1,0:T(8,128)(2,1)S(1)}, u32[]{:S(2)}) copy-start(bf16[2,2,512,512]{3,2,1,0:T(8,128)(2,1)S(1)} %shard_map.91._.refs_0_.refs_3_.refs_6_) | copy-start | bytes 6291460
  2.3 15.4 %copy-start.11 = (s32[7]{0:T(128)S(1)}, s32[7]{0:T(128)}, u32[]{:S(2)}) copy-start(s32[7]{0:T(128)} %param.15) | copy-start | bytes 88
  2.3 15.6 %copy-start.5 = (f32[7]{0:T(128)S(1)}, f32[7]{0:T(128)}, u32[]{:S(2)}) copy-start(f32[7]{0:T(128)} %param.17) | copy-start | bytes 88
  2.3 15.6 %copy-start.6 = (f32[7]{0:T(128)S(1)}, f32[7]{0:T(128)}, u32[]{:S(2)}) copy-start(f32[7]{0:T(128)} %param.16) | copy-start | bytes 88
  2.3 32.0 %collective-permute-start = (bf16[2,2,512,512]{3,2,1,0:T(8,128)(2,1)S(1)}, bf16[2,2,512,512]{3,2,1,0:T(8,128)(2,1)}, u32[]{:S(2)}, u32[]{:S(2)}) collective-permute-start(bf16[2,2,512,512]{3,2,1,0:T(8,128)(2,1)S(1)} %shard_map.91._.refs_0_.refs_3_.refs_6_), channel_id=1, source_target_pairs={{0,4},{4,0},{8,12},{12,8},{16,20},{20,16},{24,28},{28,24},{1,5},{5... | collective-permute-start | bytes 6291464 | tf_op jit(solution)/shard_map/ppermute | solution.py:351
  2.8 96.1 %collective-permute-start.3 = (bf16[2,2,512,512]{3,2,1,0:T(8,128)(2,1)S(1)}, bf16[2,2,512,512]{3,2,1,0:T(8,128)(2,1)}, u32[]{:S(2)}, u32[]{:S(2)}) collective-permute-start(bf16[2,2,512,512]{3,2,1,0:T(8,128)(2,1)S(1)} %shard_map.91._.refs_0_.refs_3_.refs_6_), channel_id=1, source_target_pairs={{0,16},{4,20},{8,24},{12,28},{16,0},{20,4},{24,8},{28,12},{1,17},{... | collective-permute-start | bytes 6291464 | tf_op jit(solution)/shard_map/ppermute | solution.py:351
  6.5 93.8 %collective-permute-start.4 = (bf16[2,2,512,512]{3,2,1,0:T(8,128)(2,1)S(1)}, bf16[2,2,512,512]{3,2,1,0:T(8,128)(2,1)}, u32[]{:S(2)}, u32[]{:S(2)}) collective-permute-start(bf16[2,2,512,512]{3,2,1,0:T(8,128)(2,1)S(1)} %shard_map.91._.refs_0_.refs_3_.refs_6_), channel_id=1, source_target_pairs={{0,8},{4,12},{8,0},{12,4},{16,24},{20,28},{24,16},{28,20},{1,9},{5... | collective-permute-start | bytes 6291464 | tf_op jit(solution)/shard_map/ppermute | solution.py:351
  16.0 45.2 %collective-permute-start.1 = (bf16[2,2,512,512]{3,2,1,0:T(8,128)(2,1)}, bf16[2,2,512,512]{3,2,1,0:T(8,128)(2,1)}, u32[]{:S(2)}, u32[]{:S(2)}) collective-permute-start(bf16[2,2,512,512]{3,2,1,0:T(8,128)(2,1)} %get-tuple-element.20.refs_6_.refs_0_.refs_3_), channel_id=1, source_target_pairs={{0,4},{4,0},{8,12},{12,8},{16,20},{20,16},{24,28},{28,24},{1,5},{5... | collective-permute-start | bytes 6291464 | tf_op jit(solution)/shard_map/ppermute | solution.py:351
  16.1 70.9 %collective-permute-start.2 = (bf16[3,2,512,512]{3,2,1,0:T(8,128)(2,1)}, bf16[3,2,512,512]{3,2,1,0:T(8,128)(2,1)}, u32[]{:S(2)}, u32[]{:S(2)}) collective-permute-start(bf16[3,2,512,512]{3,2,1,0:T(8,128)(2,1)} %get-tuple-element.21), channel_id=1, source_target_pairs={{0,1},{1,0},{2,3},{3,2},{4,5},{5,4},{6,7},{7,6},{8,9},{9,8},{10,11... | collective-permute-start | bytes 9437192 | tf_op jit(solution)/shard_map/ppermute | solution.py:351
  34.3 93.0 %collective-permute-start.5 = (bf16[4,2,512,512]{3,2,1,0:T(8,128)(2,1)}, bf16[4,2,512,512]{3,2,1,0:T(8,128)(2,1)}, u32[]{:S(2)}, u32[]{:S(2)}) collective-permute-start(bf16[4,2,512,512]{3,2,1,0:T(8,128)(2,1)} %get-tuple-element.22), channel_id=1, source_target_pairs={{0,2},{1,3},{2,0},{3,1},{4,6},{5,7},{6,4},{7,5},{8,10},{9,11},{10,... | collective-permute-start | bytes 12582920 | tf_op jit(solution)/shard_map/ppermute | solution.py:351
  35.8 25.4 %copy-start.8 = (bf16[1,2,512,512]{3,2,1,0:T(8,128)(2,1)S(1)}, bf16[1,2,512,512]{3,2,1,0:T(8,128)(2,1)}, u32[]{:S(2)}) copy-start(bf16[1,2,512,512]{3,2,1,0:T(8,128)(2,1)} %get-tuple-element.23) | copy-start | bytes 3145732
  61.2 81.8 %collective-permute-start.6 = (bf16[1,2,512,512]{3,2,1,0:T(8,128)(2,1)S(1)}, bf16[1,2,512,512]{3,2,1,0:T(8,128)(2,1)S(1)}, u32[]{:S(2)}, u32[]{:S(2)}) collective-permute-start(bf16[1,2,512,512]{3,2,1,0:T(8,128)(2,1)S(1)} %copy-done.8), channel_id=1, source_target_pairs={{0,16},{4,20},{8,24},{12,28},{16,0},{20,4},{24,8},{28,12},{1,17},{... | collective-permute-start | bytes 3145736 | tf_op jit(solution)/shard_map/ppermute | solution.py:351
  86.9 68.3 %collective-permute-start.7 = (bf16[1,2,512,512]{3,2,1,0:T(8,128)(2,1)S(1)}, bf16[1,2,512,512]{3,2,1,0:T(8,128)(2,1)S(1)}, u32[]{:S(2)}, u32[]{:S(2)}) collective-permute-start(bf16[1,2,512,512]{3,2,1,0:T(8,128)(2,1)S(1)} %copy-done.8), channel_id=1, source_target_pairs={{0,8},{4,12},{8,0},{12,4},{16,24},{20,28},{24,16},{28,20},{1,9},{5... | collective-permute-start | bytes 3145736 | tf_op jit(solution)/shard_map/ppermute | solution.py:351
  98.9 28.3 %copy-start.7 = (bf16[1,2,512,512]{3,2,1,0:T(8,128)(2,1)S(1)}, bf16[1,2,512,512]{3,2,1,0:T(8,128)(2,1)}, u32[]{:S(2)}) copy-start(bf16[1,2,512,512]{3,2,1,0:T(8,128)(2,1)} %get-tuple-element.24) | copy-start | bytes 3145732
  98.9 73.8 %collective-permute-start.10 = (bf16[1,1,512,512]{3,2,1,0:T(8,128)(2,1)}, bf16[1,1,512,512]{3,2,1,0:T(8,128)(2,1)S(1)}, u32[]{:S(2)}, u32[]{:S(2)}) collective-permute-start(bf16[1,1,512,512]{3,2,1,0:T(8,128)(2,1)} %get-tuple-element.25), channel_id=1, source_target_pairs={{0,8},{4,12},{8,0},{12,4},{16,24},{20,28},{24,16},{28,20},{1,9},{5... | collective-permute-start | bytes 1572872 | tf_op jit(solution)/shard_map/ppermute | solution.py:351
  100.3 73.5 %collective-permute-start.9 = (bf16[1,1,512,512]{3,2,1,0:T(8,128)(2,1)}, bf16[1,1,512,512]{3,2,1,0:T(8,128)(2,1)S(1)}, u32[]{:S(2)}, u32[]{:S(2)}) collective-permute-start(bf16[1,1,512,512]{3,2,1,0:T(8,128)(2,1)} %get-tuple-element.25), channel_id=1, source_target_pairs={{0,16},{4,20},{8,24},{12,28},{16,0},{20,4},{24,8},{28,12},{1,17},{... | collective-permute-start | bytes 1572872 | tf_op jit(solution)/shard_map/ppermute | solution.py:351
  127.2 15.8 %copy-start.10 = (bf16[1,1,256,512]{3,2,1,0:T(8,128)(2,1)S(1)}, bf16[1,1,256,512]{3,2,1,0:T(8,128)(2,1)}, u32[]{:S(2)}) copy-start(bf16[1,1,256,512]{3,2,1,0:T(8,128)(2,1)} %get-tuple-element.29) | copy-start | bytes 786436
  127.2 38.3 %collective-permute-start.8 = (bf16[1,2,512,512]{3,2,1,0:T(8,128)(2,1)S(1)}, bf16[1,2,512,512]{3,2,1,0:T(8,128)(2,1)S(1)}, u32[]{:S(2)}, u32[]{:S(2)}) collective-permute-start(bf16[1,2,512,512]{3,2,1,0:T(8,128)(2,1)S(1)} %copy-done.7), channel_id=1, source_target_pairs={{0,1},{1,0},{2,3},{3,2},{4,5},{5,4},{6,7},{7,6},{8,9},{9,8},{10,11... | collective-permute-start | bytes 3145736 | tf_op jit(solution)/shard_map/ppermute | solution.py:351
  143.0 12.2 %copy-start.3 = (bf16[1,2,512,512]{3,2,1,0:T(8,128)(2,1)}, bf16[1,2,512,512]{3,2,1,0:T(8,128)(2,1)S(1)}, u32[]{:S(2)}) copy-start(bf16[1,2,512,512]{3,2,1,0:T(8,128)(2,1)S(1)} %collective-permute-done.6.refs_0_) | copy-start | bytes 3145732
  143.0 22.5 %copy-start.9 = (bf16[1,1,256,512]{3,2,1,0:T(8,128)(2,1)S(1)}, bf16[1,1,256,512]{3,2,1,0:T(8,128)(2,1)}, u32[]{:S(2)}) copy-start(bf16[1,1,256,512]{3,2,1,0:T(8,128)(2,1)} %get-tuple-element.30) | copy-start | bytes 786436
  143.0 36.6 %collective-permute-start.11 = (bf16[1,1,256,512]{3,2,1,0:T(8,128)(2,1)S(1)}, bf16[1,1,256,512]{3,2,1,0:T(8,128)(2,1)S(1)}, u32[]{:S(2)}, u32[]{:S(2)}) collective-permute-start(bf16[1,1,256,512]{3,2,1,0:T(8,128)(2,1)S(1)} %copy-done.10), channel_id=1, source_target_pairs={{0,16},{4,20},{8,24},{12,28},{16,0},{20,4},{24,8},{28,12},{1,17},{... | collective-permute-start | bytes 786440 | tf_op jit(solution)/shard_map/ppermute | solution.py:351
  155.2 1.0 copy-start.4
  155.2 24.4 %collective-permute-start.12 = (bf16[1,1,256,512]{3,2,1,0:T(8,128)(2,1)S(1)}, bf16[1,1,256,512]{3,2,1,0:T(8,128)(2,1)S(1)}, u32[]{:S(2)}, u32[]{:S(2)}) collective-permute-start(bf16[1,1,256,512]{3,2,1,0:T(8,128)(2,1)S(1)} %copy-done.10), channel_id=1, source_target_pairs={{0,8},{4,12},{8,0},{12,4},{16,24},{20,28},{24,16},{28,20},{1,9},{5... | collective-permute-start | bytes 786440 | tf_op jit(solution)/shard_map/ppermute | solution.py:351
  165.6 1.0 copy-start.2
  165.6 8.2 %copy-start.1 = (f32[4,9]{1,0:T(4,128)S(1)}, f32[4,9]{1,0:T(4,128)}, u32[]{:S(2)}) copy-start(f32[4,9]{1,0:T(4,128)} %pad_maximum_fusion.coef_ref._) | copy-start | bytes 436
  165.6 22.2 %collective-permute-start.13 = (bf16[1,1,256,512]{3,2,1,0:T(8,128)(2,1)S(1)}, bf16[1,1,256,512]{3,2,1,0:T(8,128)(2,1)S(1)}, u32[]{:S(2)}, u32[]{:S(2)}) collective-permute-start(bf16[1,1,256,512]{3,2,1,0:T(8,128)(2,1)S(1)} %copy-done.9), channel_id=1, source_target_pairs={{0,16},{4,20},{8,24},{12,28},{16,0},{20,4},{24,8},{28,12},{1,17},{... | collective-permute-start | bytes 786440 | tf_op jit(solution)/shard_map/ppermute | solution.py:351
  172.7 15.1 %collective-permute-start.14 = (bf16[1,1,256,512]{3,2,1,0:T(8,128)(2,1)S(1)}, bf16[1,1,256,512]{3,2,1,0:T(8,128)(2,1)S(1)}, u32[]{:S(2)}, u32[]{:S(2)}) collective-permute-start(bf16[1,1,256,512]{3,2,1,0:T(8,128)(2,1)S(1)} %copy-done.9), channel_id=1, source_target_pairs={{0,8},{4,12},{8,0},{12,4},{16,24},{20,28},{24,16},{28,20},{1,9},{5... | collective-permute-start | bytes 786440 | tf_op jit(solution)/shard_map/ppermute | solution.py:351

commit v3 on v2

--- a/solution.py
+++ b/solution.py
@@ -214,29 +214,29 @@
     )(coef, base, into, *args)
 
 
-def add_piece(index, modes, cut, out, rows, coef_ref, arrays, left, right, sum_in, sum_out):
+def bands_of(cut, n):
+    _, first, size = cut
+    bands = [(first, first + size), (0, first), (first + size, n)]
+    return [rows for rows in bands if rows[0] < rows[1]]
+
+
+def add_piece(modes, cut, out, rows, coefs, arrays, left, right, sum_in, sum_out):
     part, first, size = cut
     use = part if out == 0 else 1 - part
-    own = max(first, rows[0]), min(first + size, rows[1])
     total = sum_in[out, rows[0] : rows[1]]
-    for t, mode in enumerate(modes):
-        coef = coef_ref[index, mode]
-        coef = -coef if out == 0 and part == 1 else coef
-        total += coef * dot(left[t, use, rows[0] : rows[1], first : first + size], arrays[t][0, 0])
+    for t in range(len(modes)):
+        coef = -coefs[t] if out == 0 and part == 1 else coefs[t]
+        value = arrays[t][0, 0]
+        change = dot(left[t, use, rows[0] : rows[1], first : first + size], value)
+        if rows[0] == first:
+            change += dot(value, right[t, use])
+        total += coef * change
     sum_out[out, rows[0] : rows[1]] = total
-    if own[0] < own[1]:
-        total = sum_out[out, own[0] : own[1]]
-        for t, mode in enumerate(modes):
-            coef = coef_ref[index, mode]
-            coef = -coef if out == 0 and part == 1 else coef
-            value = arrays[t][0, 0, own[0] - first : own[1] - first]
-            total += coef * dot(value, right[t, use])
-        sum_out[out, own[0] : own[1]] = total
 
 
 def first_piece_kernel(index, modes, cut, coef_ref, base_ref, left_ref, right_ref, *refs):
     count = len(modes)
-    arrays, (total, left, right, loads) = refs[:count], refs[count:]
+    arrays, (total, left, right, scale, loads) = refs[:count], refs[count:]
     copies = [pltpu.make_async_copy(base_ref.at[index], total, loads.at[0])]
     for t, mode in enumerate(modes):
         for source, target in ((left_ref, left), (right_ref, right)):
@@ -245,31 +245,32 @@
             )
     for copy in copies:
         copy.start()
+    coefs = [coef_ref[index, mode] for mode in modes]
+    for t in range(count):
+        scale[t] = jnp.full(scale.shape[1:], coefs[t])
     for copy in copies:
         copy.wait()
-    rows = 0, total.shape[1]
     for out in range(2):
-        add_piece(index, modes, cut, out, rows, coef_ref, arrays, left, right, total, total)
-
-
-def next_piece_kernel(index, modes, cut, coef_ref, total, left, right, *refs):
+        for rows in bands_of(cut, total.shape[1]):
+            add_piece(modes, cut, out, rows, coefs, arrays, left, right, total, total)
+
+
+def next_piece_kernel(index, modes, cut, total, left, right, scale, *refs):
     arrays, out_ref = refs[:-1], refs[-1]
-    rows = 0, total.shape[1]
+    coefs = [scale[t, 0:1] for t in range(len(modes))]
     for out in range(2):
-        add_piece(index, modes, cut, out, rows, coef_ref, arrays, left, right, total, out_ref)
-
-
-def last_piece_kernel(index, modes, cut, coef_ref, _, total, left, right, *refs):
+        for rows in bands_of(cut, total.shape[1]):
+            add_piece(modes, cut, out, rows, coefs, arrays, left, right, total, out_ref)
+
+
+def last_piece_kernel(index, modes, cut, _, total, left, right, scale, *refs):
     count = len(modes)
     arrays, (out_ref, result, stores) = refs[:count], refs[count:]
-    n = total.shape[1]
-    bands = [(cut[1], cut[1] + cut[2]), (0, cut[1]), (cut[1] + cut[2], n)]
+    coefs = [scale[t, 0:1] for t in range(count)]
     writes = []
     for out in range(2):
-        for rows in bands:
-            if rows[0] == rows[1]:
-                continue
-            add_piece(index, modes, cut, out, rows, coef_ref, arrays, left, right, total, result)
+        for rows in bands_of(cut, total.shape[1]):
+            add_piece(modes, cut, out, rows, coefs, arrays, left, right, total, result)
             band = pl.ds(rows[0], rows[1] - rows[0])
             writes.append(
                 pltpu.make_async_copy(
@@ -300,7 +301,7 @@
     )
     return pl.pallas_call(
         functools.partial(kernel, index, modes, cut),
-        in_specs=[SMEM] + [spec for _, spec in operands[1:]] + [WHOLE] * len(arrays),
+        in_specs=[spec for _, spec in operands] + [WHOLE] * len(arrays),
         out_specs=out_specs,
         out_shape=out_shape,
         scratch_shapes=scratch,
@@ -319,6 +320,7 @@
         pltpu.VMEM((2, n, n), jnp.float32),
         pltpu.VMEM((count, 2, n, n), jnp.bfloat16),
         pltpu.VMEM((count, 2, n, n), jnp.bfloat16),
+        pltpu.VMEM((count, 8, n), jnp.float32),
     ]
     scratch = [pltpu.SemaphoreType.DMA((1 + 2 * count,))]
     return piece_call(
@@ -326,23 +328,23 @@
     )
 
 
-def next_piece(staged, coef, index, modes, cut, arrays):
+def next_piece(staged, index, modes, cut, arrays):
     n = staged[0].shape[-1]
-    operands = [(coef, SMEM)] + [(in_vmem(array), WHOLE) for array in staged]
+    operands = [(in_vmem(array), WHOLE) for array in staged]
     out_shape = pltpu.VMEM((2, n, n), jnp.float32)
     total = piece_call(
-        next_piece_kernel, index, modes, cut, n, operands, arrays, out_shape, [], {1: 0}
+        next_piece_kernel, index, modes, cut, n, operands, arrays, out_shape, [], {0: 0}
     )
     return [total] + list(staged[1:])
 
 
-def last_piece(base, staged, coef, index, modes, cut, arrays):
+def last_piece(base, staged, index, modes, cut, arrays):
     n = base.shape[-1]
-    operands = [(coef, SMEM), (base, ANYWHERE)] + [(in_vmem(array), WHOLE) for array in staged]
+    operands = [(base, ANYWHERE)] + [(in_vmem(array), WHOLE) for array in staged]
     out_shape = jax.ShapeDtypeStruct(base.shape, jnp.float32)
     scratch = [pltpu.VMEM((2, n, n), jnp.float32), pltpu.SemaphoreType.DMA((6,))]
     return piece_call(
-        last_piece_kernel, index, modes, cut, n, operands, arrays, out_shape, scratch, {1: 0}
+        last_piece_kernel, index, modes, cut, n, operands, arrays, out_shape, scratch, {0: 0}
     )
 
 
@@ -442,9 +444,9 @@
         elif cut == cuts[0]:
             staged = first_piece(result, coef, operators, first, step_modes, cut, arrays)
         elif cut != cuts[-1]:
-            staged = next_piece(staged, coef, first, step_modes, cut, arrays)
+            staged = next_piece(staged, first, step_modes, cut, arrays)
         else:
-            result = last_piece(result, staged, coef, first, step_modes, cut, arrays)
+            result = last_piece(result, staged, first, step_modes, cut, arrays)
     return result
 
 

time: 191 us -> 190 us (level)
  transfers between devices with their start and end apart: 15 -> 15, of which waited for: 5 -> 5; matrix products, arithmetic and copies ran while one was open for 1% -> 1% of each run, Pallas kernels for 72% -> 71%
where the time goes in v3:
time: 190 us
  Pallas kernels  140 us (74%)
  waiting for transfers between devices  30.9 us (16%)
  starting transfers between devices  15.6 us (8%)
  local copies, waits for them, and re-layouts  2.09 us (1%)
    pallas_call x7, Pallas kernels, add_terms(): pl.pallas_call(functools.partial(term_kernel, first, [t[0] for t in terms...  105 us
    ppermute x15, waiting for transfers between devices, flip(): return lax.ppermute(value, axis, pairs)  30.9 us
    ppermute x15, starting transfers between devices, flip(): return lax.ppermute(value, axis, pairs)  15.6 us
    pallas_call x1, Pallas kernels, make_operators(): pl.pallas_call(operator_kernel, grid_spec=pltpu.PrefetchScalarGridSpec(nu...  15.4 us
    pallas_call x3, Pallas kernels, piece_call(): pl.pallas_call(functools.partial(kernel, index, modes, cut), in_specs=[sp...  9.24 us
    pallas_call x1, Pallas kernels, round_groups(): pl.pallas_call(functools.partial(round_kernel, groups, low, high), in_spe...  7.9 us
  transfers between devices with their start and end apart: 15, of which 5 were waited for; matrix products, arithmetic and copies ran while one was open for 1% of the time, Pallas kernels for 71%

profile of v3, /device:TPU:0, one launch (start us, length us, event | category | flops | bytes accessed | tf_op | source)
XLA Modules:
  0.0 190.2 jit_solution(8363225919225223615)
XLA Ops:
  0.0 2.3 %shard_map.91._.refs_0_.refs_3_.refs_6_ = bf16[2,2,512,512]{3,2,1,0:T(8,128)(2,1)S(1)} custom-call(f32[4,2,512,512]{3,2,1,0:T(8,128)} %base_ref.3), custom_call_target="tpu_custom_call" | custom-call | bytes 6291456 | tf_op jit(solution)/shard_map/pallas_call | solution.py:74
  2.3 0.0 copy-start
  2.3 0.0 copy-start.11
  2.3 0.0 copy-start.5
  2.3 0.0 copy-start.6
  2.3 0.5 collective-permute-start
  2.8 3.7 %collective-permute-start.3 = (bf16[2,2,512,512]{3,2,1,0:T(8,128)(2,1)S(1)}, bf16[2,2,512,512]{3,2,1,0:T(8,128)(2,1)}, u32[]{:S(2)}, u32[]{:S(2)}) collective-permute-start(bf16[2,2,512,512]{3,2,1,0:T(8,128)(2,1)S(1)} %shard_map.91._.refs_0_.refs_3_.refs_6_), channel_id=1, source_target_pairs={{0,16},{4,20},{8,24},{12,28},{16,0},{20,4},{24,8},{28,12},{1,17},{... | collective-permute-start | bytes 6291464 | tf_op jit(solution)/shard_map/ppermute | solution.py:353
  6.5 1.6 collective-permute-start.4
  8.1 0.0 copy-done
  8.1 7.9 %shard_map.93 = (bf16[2,2,512,512]{3,2,1,0:T(8,128)(2,1)}, bf16[3,2,512,512]{3,2,1,0:T(8,128)(2,1)}, bf16[4,2,512,512]{3,2,1,0:T(8,128)(2,1)}, bf16[1,2,512,512]...) custom-call(f32[4,2,512,512]{3,2,1,0:T(8,128)} %base_ref.3, ...), custom_call_target="tpu_custom_call" | custom-call | bytes 21495808 | tf_op jit(solution)/shard_map/pallas_call | solution.py:98
  16.0 0.1 collective-permute-start.1
  16.1 1.6 collective-permute-start.2
  17.6 0.1 shift-right-arithmetic_and_fusion
  17.7 0.0 copy-done.11
  17.7 0.2 reduce_window_sum.11
  17.9 0.0 copy-done.5
  17.9 0.0 copy-done.6
  17.9 0.2 fusion.5
  18.1 0.1 copy.18
  18.2 0.1 pad.1.clone
  18.2 15.4 %shard_map.92 = (bf16[8,2,512,512]{3,2,1,0:T(8,128)(2,1)}, bf16[8,2,512,512]{3,2,1,0:T(8,128)(2,1)}) custom-call(s32[7]{0:T(128)} %slot_ref.1, s32[7,2,8,8]{3,2,1,0:T(8,128)} %mask_ref.1, bf16[7,2,512,512]{3,2,1,0:T(8,128)(2,1)} %left_ref.1, bf16[7,2,512,512]{3,2,1,0:T(8,128)(2,1)} %right_ref.1, bf16[2,512,512]{2,1,0:T(8,128)(2,1)} %ham_ref.1), custom_call_target="tpu_custom_call" | custom-call | bytes 33554432 | tf_op jit(solution)/shard_map/pallas_call | solution.py:153
  33.6 0.7 pad_maximum_fusion.coef_ref._
  34.3 0.0 collective-permute-done.refs_9_
  34.3 1.5 collective-permute-start.5
  35.8 25.3 %shard_map.94._ = f32[4,2,512,512]{3,2,1,0:T(8,128)} custom-call(f32[4,9]{1,0:T(4,128)} %pad_maximum_fusion.coef_ref._, f32[4,2,512,512]{3,2,1,0:T(8,128)} %base_ref.3, f32[4,9]{1,0:T(4,128)} %pad_maximum_fusion.coef_ref._, bf16[2,2,512,512]{3,2,1,0:T(8,128)(2,1)} %copy-done, ...), custom_call_target="tpu_custom_call" | custom-call | flops 17179869184 | bytes 25165824 | tf_op jit(solution)/shard_map/pallas_call | solution.py:203
  61.1 0.0 collective-permute-done.1.refs_9_
  61.1 0.0 copy-done.8
  61.2 0.4 collective-permute-start.6
  61.6 25.4 %shard_map.95.base_ref = f32[4,2,512,512]{3,2,1,0:T(8,128)} custom-call(f32[4,9]{1,0:T(4,128)} %pad_maximum_fusion.coef_ref._, f32[4,2,512,512]{3,2,1,0:T(8,128)} %base_ref.3, f32[4,2,512,512]{3,2,1,0:T(8,128)} %shard_map.94._, bf16[2,2,512,512]{3,2,1,0:T(8,128)(2,1)} %get-tuple-element.21.refs_6_.refs_0_.refs_3_, ...), custom_call_target="tpu_custom_call", output_to_operand_aliasing={{}: (2, {})} | custom-call | flops 17179869184 | bytes 25165824 | tf_op jit(solution)/shard_map/pallas_call | solution.py:203
  86.9 0.0 collective-permute-done.2.refs_0_
  86.9 0.8 collective-permute-start.7
  87.8 11.2 %shard_map.96.base_ref = f32[4,2,512,512]{3,2,1,0:T(8,128)} custom-call(f32[4,9]{1,0:T(4,128)} %pad_maximum_fusion.coef_ref._, f32[4,2,512,512]{3,2,1,0:T(8,128)} %shard_map.95.base_ref, f32[4,9]{1,0:T(4,128)} %pad_maximum_fusion.coef_ref._, bf16[3,2,512,512]{3,2,1,0:T(8,128)(2,1)} %collective-permute-done.2.refs_0_, ...), custom_call_target="tpu_custom_call", output_to_operand_aliasing={{}: (1, {})} | custom-call | flops 6442450944 | bytes 17825792 | tf_op jit(solution)/shard_map/pallas_call | solution.py:203
  98.9 0.0 collective-permute-done.3.refs_0_
  98.9 1.3 collective-permute-start.10
  100.3 0.0 collective-permute-done.4.refs_3_
  100.3 2.5 %collective-permute-start.9 = (bf16[1,1,512,512]{3,2,1,0:T(8,128)(2,1)}, bf16[1,1,512,512]{3,2,1,0:T(8,128)(2,1)S(1)}, u32[]{:S(2)}, u32[]{:S(2)}) collective-permute-start(bf16[1,1,512,512]{3,2,1,0:T(8,128)(2,1)} %get-tuple-element.26), channel_id=1, source_target_pairs={{0,16},{4,20},{8,24},{12,28},{16,0},{20,4},{24,8},{28,12},{1,17},{... | collective-permute-start | bytes 1572872 | tf_op jit(solution)/shard_map/ppermute | solution.py:353
  102.8 14.3 %shard_map.97.base_ref = f32[4,2,512,512]{3,2,1,0:T(8,128)} custom-call(f32[4,9]{1,0:T(4,128)} %pad_maximum_fusion.coef_ref._, f32[4,2,512,512]{3,2,1,0:T(8,128)} %shard_map.96.base_ref, f32[4,9]{1,0:T(4,128)} %pad_maximum_fusion.coef_ref._, bf16[2,2,512,512]{3,2,1,0:T(8,128)(2,1)} %collective-permute-done.3.refs_0_, ...), custom_call_target="tpu_custom_call", output_to_operand_aliasing={{}: (1, {})} | custom-call | flops 8589934592 | bytes 16777216 | tf_op jit(solution)/shard_map/pallas_call | solution.py:203
  117.1 10.2 %collective-permute-done.5.refs_0_ = bf16[4,2,512,512]{3,2,1,0:T(8,128)(2,1)} collective-permute-done((bf16[4,2,512,512]{3,2,1,0:T(8,128)(2,1)}, bf16[4,2,512,512]{3,2,1,0:T(8,128)(2,1)}, u32[]{:S(2)}, u32[]{:S(2)}) %collective-permute-start.5) | collective-permute-done | bytes 4194336 | tf_op jit(solution)/shard_map/ppermute | solution.py:353
  127.2 0.0 copy-done.7
  127.2 0.5 collective-permute-start.8
  127.8 13.6 %shard_map.98.base_ref = f32[4,2,512,512]{3,2,1,0:T(8,128)} custom-call(f32[4,9]{1,0:T(4,128)} %pad_maximum_fusion.coef_ref._, f32[4,2,512,512]{3,2,1,0:T(8,128)} %shard_map.97.base_ref, f32[4,9]{1,0:T(4,128)} %pad_maximum_fusion.coef_ref._, bf16[4,2,512,512]{3,2,1,0:T(8,128)(2,1)} %collective-permute-done.5.refs_0_, ...), custom_call_target="tpu_custom_call", output_to_operand_aliasing={{}: (1, {})} | custom-call | flops 8589934592 | bytes 23068672 | tf_op jit(solution)/shard_map/pallas_call | solution.py:203
  141.4 1.6 collective-permute-done.6.refs_0_
  143.0 0.0 copy-done.10
  143.0 0.0 collective-permute-start.11
  143.0 12.2 %collective-permute-done.7.refs_3_ = bf16[1,2,512,512]{3,2,1,0:T(8,128)(2,1)S(1)} collective-permute-done((bf16[1,2,512,512]{3,2,1,0:T(8,128)(2,1)S(1)}, bf16[1,2,512,512]{3,2,1,0:T(8,128)(2,1)S(1)}, u32[]{:S(2)}, u32[]{:S(2)}) %collective-permute-start.7) | collective-permute-done | bytes 1048608 | tf_op jit(solution)/shard_map/ppermute | solution.py:353
  155.2 0.0 collective-permute-start.12
  155.2 0.0 copy-done.3
  155.2 1.0 copy-done.4
  156.2 9.3 %shard_map.99.base_ref = f32[4,2,512,512]{3,2,1,0:T(8,128)} custom-call(f32[4,9]{1,0:T(4,128)} %pad_maximum_fusion.coef_ref._, f32[4,2,512,512]{3,2,1,0:T(8,128)} %shard_map.98.base_ref, f32[4,9]{1,0:T(4,128)} %pad_maximum_fusion.coef_ref._, bf16[1,2,512,512]{3,2,1,0:T(8,128)(2,1)} %copy-done.3, ...), custom_call_target="tpu_custom_call", output_to_operand_aliasing={{}: (1, {})} | custom-call | flops 4294967296 | bytes 10485760 | tf_op jit(solution)/shard_map/pallas_call | solution.py:203
  165.6 0.0 collective-permute-done.8.refs_0_
  165.6 0.1 collective-permute-start.13
  165.6 0.9 copy-done.2
  166.6 6.2 %shard_map.100.base_ref._ = f32[4,2,512,512]{3,2,1,0:T(8,128)} custom-call(f32[4,9]{1,0:T(4,128)} %pad_maximum_fusion.coef_ref._, f32[4,2,512,512]{3,2,1,0:T(8,128)} %shard_map.99.base_ref, f32[4,9]{1,0:T(4,128)} %pad_maximum_fusion.coef_ref._, bf16[1,2,512,512]{3,2,1,0:T(8,128)(2,1)} %copy-done.2, ...), custom_call_target="tpu_custom_call", output_to_operand_aliasing={{}: (1, {})} | custom-call | flops 2147483648 | bytes 7340032 | tf_op jit(solution)/shard_map/pallas_call | solution.py:203
  172.7 0.0 collective-permute-done.10.refs_1_
  172.7 1.1 collective-permute-start.14
  173.8 0.0 collective-permute-done.9.refs_0_
  173.8 0.0 copy-done.1
  173.8 5.8 %shard_map.101 = (f32[2,512,512]{2,1,0:T(8,128)S(1)}, bf16[2,2,512,512]{3,2,1,0:T(8,128)(2,1)S(1)}, bf16[2,2,512,512]{3,2,1,0:T(8,128)(2,1)S(1)}, f32[2,8,512]{2,1,0:T(8,128)S(1)}) custom-call(f32[4,9]{1,0:T(4,128)S(1)} %copy-done.1, f32[4,2,512,512]{3,2,1,0:T(8,128)} %shard_map.100.base_ref._, ...), custom_call_target="tpu_custom_call" | custom-call | flops 2147483648 | bytes 8388608 | tf_op jit(solution)/shard_map/pallas_call | solution.py:302
  179.6 0.0 collective-permute-done.11.refs_0_
  179.6 0.0 collective-permute-done.12.refs_1_
  179.6 1.3 shard_map.102.total
  180.9 6.9 %collective-permute-done.13.refs_0_ = bf16[1,1,256,512]{3,2,1,0:T(8,128)(2,1)S(1)} collective-permute-done((bf16[1,1,256,512]{3,2,1,0:T(8,128)(2,1)S(1)}, bf16[1,1,256,512]{3,2,1,0:T(8,128)(2,1)S(1)}, u32[]{:S(2)}, u32[]{:S(2)}) %collective-permute-start.13) | collective-permute-done | bytes 262176 | tf_op jit(solution)/shard_map/ppermute | solution.py:353
  187.8 0.1 collective-permute-done.14.refs_1_
  187.8 2.1 %shard_map.103 = f32[4,2,512,512]{3,2,1,0:T(8,128)} custom-call(f32[4,2,512,512]{3,2,1,0:T(8,128)} %shard_map.100.base_ref._, f32[2,512,512]{2,1,0:T(8,128)S(1)} %shard_map.102.total, bf16[2,2,512,512]{3,2,1,0:T(8,128)(2,1)S(1)} %get-tuple-element.28.left, bf16[2,2,512,512]{3,2,1,0:T(8,128)(2,1)S(1)} %get-tuple-element.29.right, ...), custom_call_target="tpu_custom_call", output_to_operand_aliasing={{}: (0, {})} | custom-call | flops 1073741824 | bytes 8388608 | tf_op jit(solution)/shard_map/pallas_call | solution.py:302
  (11 shorter events, 0.0 us)
Async XLA Ops:
  2.3 5.8 %copy-start = (bf16[2,2,512,512]{3,2,1,0:T(8,128)(2,1)}, bf16[2,2,512,512]{3,2,1,0:T(8,128)(2,1)S(1)}, u32[]{:S(2)}) copy-start(bf16[2,2,512,512]{3,2,1,0:T(8,128)(2,1)S(1)} %shard_map.91._.refs_0_.refs_3_.refs_6_) | copy-start | bytes 6291460
  2.3 15.4 %copy-start.11 = (s32[7]{0:T(128)S(1)}, s32[7]{0:T(128)}, u32[]{:S(2)}) copy-start(s32[7]{0:T(128)} %param.15) | copy-start | bytes 88
  2.3 15.6 %copy-start.5 = (f32[7]{0:T(128)S(1)}, f32[7]{0:T(128)}, u32[]{:S(2)}) copy-start(f32[7]{0:T(128)} %param.17) | copy-start | bytes 88
  2.3 15.6 %copy-start.6 = (f32[7]{0:T(128)S(1)}, f32[7]{0:T(128)}, u32[]{:S(2)}) copy-start(f32[7]{0:T(128)} %param.16) | copy-start | bytes 88
  2.3 32.0 %collective-permute-start = (bf16[2,2,512,512]{3,2,1,0:T(8,128)(2,1)S(1)}, bf16[2,2,512,512]{3,2,1,0:T(8,128)(2,1)}, u32[]{:S(2)}, u32[]{:S(2)}) collective-permute-start(bf16[2,2,512,512]{3,2,1,0:T(8,128)(2,1)S(1)} %shard_map.91._.refs_0_.refs_3_.refs_6_), channel_id=1, source_target_pairs={{0,4},{4,0},{8,12},{12,8},{16,20},{20,16},{24,28},{28,24},{1,5},{5... | collective-permute-start | bytes 6291464 | tf_op jit(solution)/shard_map/ppermute | solution.py:353
  2.8 96.1 %collective-permute-start.3 = (bf16[2,2,512,512]{3,2,1,0:T(8,128)(2,1)S(1)}, bf16[2,2,512,512]{3,2,1,0:T(8,128)(2,1)}, u32[]{:S(2)}, u32[]{:S(2)}) collective-permute-start(bf16[2,2,512,512]{3,2,1,0:T(8,128)(2,1)S(1)} %shard_map.91._.refs_0_.refs_3_.refs_6_), channel_id=1, source_target_pairs={{0,16},{4,20},{8,24},{12,28},{16,0},{20,4},{24,8},{28,12},{1,17},{... | collective-permute-start | bytes 6291464 | tf_op jit(solution)/shard_map/ppermute | solution.py:353
  6.5 93.8 %collective-permute-start.4 = (bf16[2,2,512,512]{3,2,1,0:T(8,128)(2,1)S(1)}, bf16[2,2,512,512]{3,2,1,0:T(8,128)(2,1)}, u32[]{:S(2)}, u32[]{:S(2)}) collective-permute-start(bf16[2,2,512,512]{3,2,1,0:T(8,128)(2,1)S(1)} %shard_map.91._.refs_0_.refs_3_.refs_6_), channel_id=1, source_target_pairs={{0,8},{4,12},{8,0},{12,4},{16,24},{20,28},{24,16},{28,20},{1,9},{5... | collective-permute-start | bytes 6291464 | tf_op jit(solution)/shard_map/ppermute | solution.py:353
  16.0 45.2 %collective-permute-start.1 = (bf16[2,2,512,512]{3,2,1,0:T(8,128)(2,1)}, bf16[2,2,512,512]{3,2,1,0:T(8,128)(2,1)}, u32[]{:S(2)}, u32[]{:S(2)}) collective-permute-start(bf16[2,2,512,512]{3,2,1,0:T(8,128)(2,1)} %get-tuple-element.21.refs_6_.refs_0_.refs_3_), channel_id=1, source_target_pairs={{0,4},{4,0},{8,12},{12,8},{16,20},{20,16},{24,28},{28,24},{1,5},{5... | collective-permute-start | bytes 6291464 | tf_op jit(solution)/shard_map/ppermute | solution.py:353
  16.1 70.9 %collective-permute-start.2 = (bf16[3,2,512,512]{3,2,1,0:T(8,128)(2,1)}, bf16[3,2,512,512]{3,2,1,0:T(8,128)(2,1)}, u32[]{:S(2)}, u32[]{:S(2)}) collective-permute-start(bf16[3,2,512,512]{3,2,1,0:T(8,128)(2,1)} %get-tuple-element.22), channel_id=1, source_target_pairs={{0,1},{1,0},{2,3},{3,2},{4,5},{5,4},{6,7},{7,6},{8,9},{9,8},{10,11... | collective-permute-start | bytes 9437192 | tf_op jit(solution)/shard_map/ppermute | solution.py:353
  34.3 93.0 %collective-permute-start.5 = (bf16[4,2,512,512]{3,2,1,0:T(8,128)(2,1)}, bf16[4,2,512,512]{3,2,1,0:T(8,128)(2,1)}, u32[]{:S(2)}, u32[]{:S(2)}) collective-permute-start(bf16[4,2,512,512]{3,2,1,0:T(8,128)(2,1)} %get-tuple-element.23), channel_id=1, source_target_pairs={{0,2},{1,3},{2,0},{3,1},{4,6},{5,7},{6,4},{7,5},{8,10},{9,11},{10,... | collective-permute-start | bytes 12582920 | tf_op jit(solution)/shard_map/ppermute | solution.py:353
  35.8 25.4 %copy-start.8 = (bf16[1,2,512,512]{3,2,1,0:T(8,128)(2,1)S(1)}, bf16[1,2,512,512]{3,2,1,0:T(8,128)(2,1)}, u32[]{:S(2)}) copy-start(bf16[1,2,512,512]{3,2,1,0:T(8,128)(2,1)} %get-tuple-element.24) | copy-start | bytes 3145732
  61.2 81.8 %collective-permute-start.6 = (bf16[1,2,512,512]{3,2,1,0:T(8,128)(2,1)S(1)}, bf16[1,2,512,512]{3,2,1,0:T(8,128)(2,1)S(1)}, u32[]{:S(2)}, u32[]{:S(2)}) collective-permute-start(bf16[1,2,512,512]{3,2,1,0:T(8,128)(2,1)S(1)} %copy-done.8), channel_id=1, source_target_pairs={{0,16},{4,20},{8,24},{12,28},{16,0},{20,4},{24,8},{28,12},{1,17},{... | collective-permute-start | bytes 3145736 | tf_op jit(solution)/shard_map/ppermute | solution.py:353
  86.9 68.3 %collective-permute-start.7 = (bf16[1,2,512,512]{3,2,1,0:T(8,128)(2,1)S(1)}, bf16[1,2,512,512]{3,2,1,0:T(8,128)(2,1)S(1)}, u32[]{:S(2)}, u32[]{:S(2)}) collective-permute-start(bf16[1,2,512,512]{3,2,1,0:T(8,128)(2,1)S(1)} %copy-done.8), channel_id=1, source_target_pairs={{0,8},{4,12},{8,0},{12,4},{16,24},{20,28},{24,16},{28,20},{1,9},{5... | collective-permute-start | bytes 3145736 | tf_op jit(solution)/shard_map/ppermute | solution.py:353
  98.9 28.3 %copy-start.7 = (bf16[1,2,512,512]{3,2,1,0:T(8,128)(2,1)S(1)}, bf16[1,2,512,512]{3,2,1,0:T(8,128)(2,1)}, u32[]{:S(2)}) copy-start(bf16[1,2,512,512]{3,2,1,0:T(8,128)(2,1)} %get-tuple-element.25) | copy-start | bytes 3145732
  98.9 73.8 %collective-permute-start.10 = (bf16[1,1,512,512]{3,2,1,0:T(8,128)(2,1)}, bf16[1,1,512,512]{3,2,1,0:T(8,128)(2,1)S(1)}, u32[]{:S(2)}, u32[]{:S(2)}) collective-permute-start(bf16[1,1,512,512]{3,2,1,0:T(8,128)(2,1)} %get-tuple-element.26), channel_id=1, source_target_pairs={{0,8},{4,12},{8,0},{12,4},{16,24},{20,28},{24,16},{28,20},{1,9},{5... | collective-permute-start | bytes 1572872 | tf_op jit(solution)/shard_map/ppermute | solution.py:353
  100.3 73.5 %collective-permute-start.9 = (bf16[1,1,512,512]{3,2,1,0:T(8,128)(2,1)}, bf16[1,1,512,512]{3,2,1,0:T(8,128)(2,1)S(1)}, u32[]{:S(2)}, u32[]{:S(2)}) collective-permute-start(bf16[1,1,512,512]{3,2,1,0:T(8,128)(2,1)} %get-tuple-element.26), channel_id=1, source_target_pairs={{0,16},{4,20},{8,24},{12,28},{16,0},{20,4},{24,8},{28,12},{1,17},{... | collective-permute-start | bytes 1572872 | tf_op jit(solution)/shard_map/ppermute | solution.py:353
  127.2 15.8 %copy-start.10 = (bf16[1,1,256,512]{3,2,1,0:T(8,128)(2,1)S(1)}, bf16[1,1,256,512]{3,2,1,0:T(8,128)(2,1)}, u32[]{:S(2)}) copy-start(bf16[1,1,256,512]{3,2,1,0:T(8,128)(2,1)} %get-tuple-element.31) | copy-start | bytes 786436
  127.2 38.3 %collective-permute-start.8 = (bf16[1,2,512,512]{3,2,1,0:T(8,128)(2,1)S(1)}, bf16[1,2,512,512]{3,2,1,0:T(8,128)(2,1)S(1)}, u32[]{:S(2)}, u32[]{:S(2)}) collective-permute-start(bf16[1,2,512,512]{3,2,1,0:T(8,128)(2,1)S(1)} %copy-done.7), channel_id=1, source_target_pairs={{0,1},{1,0},{2,3},{3,2},{4,5},{5,4},{6,7},{7,6},{8,9},{9,8},{10,11... | collective-permute-start | bytes 3145736 | tf_op jit(solution)/shard_map/ppermute | solution.py:353
  143.0 12.2 %copy-start.3 = (bf16[1,2,512,512]{3,2,1,0:T(8,128)(2,1)}, bf16[1,2,512,512]{3,2,1,0:T(8,128)(2,1)S(1)}, u32[]{:S(2)}) copy-start(bf16[1,2,512,512]{3,2,1,0:T(8,128)(2,1)S(1)} %collective-permute-done.6.refs_0_) | copy-start | bytes 3145732
  143.0 22.5 %copy-start.9 = (bf16[1,1,256,512]{3,2,1,0:T(8,128)(2,1)S(1)}, bf16[1,1,256,512]{3,2,1,0:T(8,128)(2,1)}, u32[]{:S(2)}) copy-start(bf16[1,1,256,512]{3,2,1,0:T(8,128)(2,1)} %get-tuple-element.32) | copy-start | bytes 786436
  143.0 36.5 %collective-permute-start.11 = (bf16[1,1,256,512]{3,2,1,0:T(8,128)(2,1)S(1)}, bf16[1,1,256,512]{3,2,1,0:T(8,128)(2,1)S(1)}, u32[]{:S(2)}, u32[]{:S(2)}) collective-permute-start(bf16[1,1,256,512]{3,2,1,0:T(8,128)(2,1)S(1)} %copy-done.10), channel_id=1, source_target_pairs={{0,16},{4,20},{8,24},{12,28},{16,0},{20,4},{24,8},{28,12},{1,17},{... | collective-permute-start | bytes 786440 | tf_op jit(solution)/shard_map/ppermute | solution.py:353
  155.2 1.0 copy-start.4
  155.2 24.3 %collective-permute-start.12 = (bf16[1,1,256,512]{3,2,1,0:T(8,128)(2,1)S(1)}, bf16[1,1,256,512]{3,2,1,0:T(8,128)(2,1)S(1)}, u32[]{:S(2)}, u32[]{:S(2)}) collective-permute-start(bf16[1,1,256,512]{3,2,1,0:T(8,128)(2,1)S(1)} %copy-done.10), channel_id=1, source_target_pairs={{0,8},{4,12},{8,0},{12,4},{16,24},{20,28},{24,16},{28,20},{1,9},{5... | collective-permute-start | bytes 786440 | tf_op jit(solution)/shard_map/ppermute | solution.py:353
  165.6 1.0 copy-start.2
  165.6 8.2 %copy-start.1 = (f32[4,9]{1,0:T(4,128)S(1)}, f32[4,9]{1,0:T(4,128)}, u32[]{:S(2)}) copy-start(f32[4,9]{1,0:T(4,128)} %pad_maximum_fusion.coef_ref._) | copy-start | bytes 436
  165.6 22.2 %collective-permute-start.13 = (bf16[1,1,256,512]{3,2,1,0:T(8,128)(2,1)S(1)}, bf16[1,1,256,512]{3,2,1,0:T(8,128)(2,1)S(1)}, u32[]{:S(2)}, u32[]{:S(2)}) collective-permute-start(bf16[1,1,256,512]{3,2,1,0:T(8,128)(2,1)S(1)} %copy-done.9), channel_id=1, source_target_pairs={{0,16},{4,20},{8,24},{12,28},{16,0},{20,4},{24,8},{28,12},{1,17},{... | collective-permute-start | bytes 786440 | tf_op jit(solution)/shard_map/ppermute | solution.py:353
  172.7 15.1 %collective-permute-start.14 = (bf16[1,1,256,512]{3,2,1,0:T(8,128)(2,1)S(1)}, bf16[1,1,256,512]{3,2,1,0:T(8,128)(2,1)S(1)}, u32[]{:S(2)}, u32[]{:S(2)}) collective-permute-start(bf16[1,1,256,512]{3,2,1,0:T(8,128)(2,1)S(1)} %copy-done.9), channel_id=1, source_target_pairs={{0,8},{4,12},{8,0},{12,4},{16,24},{20,28},{24,16},{28,20},{1,9},{5... | collective-permute-start | bytes 786440 | tf_op jit(solution)/shard_map/ppermute | solution.py:353

commit v4 on v3

--- a/solution.py
+++ b/solution.py
@@ -402,7 +402,7 @@
     if last:
         plan.append((middle[:1], last, 1, None))
     n = density.shape[-1]
-    cuts = [(0, 0, n), (1, 0, n // 2), (1, n // 2, n // 2)]
+    cuts = [(0, 0, n), (1, 0, 3 * n // 4), (1, 3 * n // 4, n // 4)]
     plan += [(slow, last, 1, cut) for cut in cuts]
 
     plan = [step for place, step in enumerate(plan) if step[0] or place < len(spans)]

time: 190 us -> 190 us (level)
  transfers between devices with their start and end apart: 15 -> 15, of which waited for: 5 -> 7; matrix products, arithmetic and copies ran while one was open for 1% -> 1% of each run, Pallas kernels for 71% -> 72%
where the time goes in v4:
time: 190 us
  Pallas kernels  141 us (74%)
  waiting for transfers between devices  30.1 us (16%)
  starting transfers between devices  15.6 us (8%)
  local copies, waits for them, and re-layouts  2.09 us (1%)
    pallas_call x7, Pallas kernels, add_terms(): pl.pallas_call(functools.partial(term_kernel, first, [t[0] for t in terms...  105 us
    ppermute x15, waiting for transfers between devices, flip(): return lax.ppermute(value, axis, pairs)  30.1 us
    ppermute x15, starting transfers between devices, flip(): return lax.ppermute(value, axis, pairs)  15.6 us
    pallas_call x1, Pallas kernels, make_operators(): pl.pallas_call(operator_kernel, grid_spec=pltpu.PrefetchScalarGridSpec(nu...  15.4 us
    pallas_call x3, Pallas kernels, piece_call(): pl.pallas_call(functools.partial(kernel, index, modes, cut), in_specs=[sp...  9.93 us
    pallas_call x1, Pallas kernels, round_groups(): pl.pallas_call(functools.partial(round_kernel, groups, low, high), in_spe...  7.9 us
  transfers between devices with their start and end apart: 15, of which 7 were waited for; matrix products, arithmetic and copies ran while one was open for 1% of the time, Pallas kernels for 72%

profile of v4, /device:TPU:0, one launch (start us, length us, event | category | flops | bytes accessed | tf_op | source)
XLA Modules:
  0.0 190.0 jit_solution(13301998402956007839)
XLA Ops:
  0.0 2.3 %shard_map.91._.refs_0_.refs_3_.refs_6_ = bf16[2,2,512,512]{3,2,1,0:T(8,128)(2,1)S(1)} custom-call(f32[4,2,512,512]{3,2,1,0:T(8,128)} %base_ref.3), custom_call_target="tpu_custom_call" | custom-call | bytes 6291456 | tf_op jit(solution)/shard_map/pallas_call | solution.py:74
  2.3 0.0 copy-start
  2.3 0.0 copy-start.11
  2.3 0.0 copy-start.5
  2.3 0.0 copy-start.6
  2.3 0.5 collective-permute-start
  2.8 3.7 %collective-permute-start.3 = (bf16[2,2,512,512]{3,2,1,0:T(8,128)(2,1)S(1)}, bf16[2,2,512,512]{3,2,1,0:T(8,128)(2,1)}, u32[]{:S(2)}, u32[]{:S(2)}) collective-permute-start(bf16[2,2,512,512]{3,2,1,0:T(8,128)(2,1)S(1)} %shard_map.91._.refs_0_.refs_3_.refs_6_), channel_id=1, source_target_pairs={{0,16},{4,20},{8,24},{12,28},{16,0},{20,4},{24,8},{28,12},{1,17},{... | collective-permute-start | bytes 6291464 | tf_op jit(solution)/shard_map/ppermute | solution.py:353
  6.5 1.6 collective-permute-start.4
  8.1 0.0 copy-done
  8.1 7.9 %shard_map.93 = (bf16[2,2,512,512]{3,2,1,0:T(8,128)(2,1)}, bf16[3,2,512,512]{3,2,1,0:T(8,128)(2,1)}, bf16[4,2,512,512]{3,2,1,0:T(8,128)(2,1)}, bf16[1,2,512,512]...) custom-call(f32[4,2,512,512]{3,2,1,0:T(8,128)} %base_ref.3, ...), custom_call_target="tpu_custom_call" | custom-call | bytes 21495808 | tf_op jit(solution)/shard_map/pallas_call | solution.py:98
  16.0 0.1 collective-permute-start.1
  16.1 1.6 collective-permute-start.2
  17.6 0.1 shift-right-arithmetic_and_fusion
  17.7 0.0 copy-done.11
  17.7 0.2 reduce_window_sum.11
  17.9 0.0 copy-done.5
  17.9 0.0 copy-done.6
  17.9 0.2 fusion.5
  18.1 0.1 copy.18
  18.2 0.1 pad.1.clone
  18.2 15.4 %shard_map.92 = (bf16[8,2,512,512]{3,2,1,0:T(8,128)(2,1)}, bf16[8,2,512,512]{3,2,1,0:T(8,128)(2,1)}) custom-call(s32[7]{0:T(128)} %slot_ref.1, s32[7,2,8,8]{3,2,1,0:T(8,128)} %mask_ref.1, bf16[7,2,512,512]{3,2,1,0:T(8,128)(2,1)} %left_ref.1, bf16[7,2,512,512]{3,2,1,0:T(8,128)(2,1)} %right_ref.1, bf16[2,512,512]{2,1,0:T(8,128)(2,1)} %ham_ref.1), custom_call_target="tpu_custom_call" | custom-call | bytes 33554432 | tf_op jit(solution)/shard_map/pallas_call | solution.py:153
  33.6 0.7 pad_maximum_fusion.coef_ref._
  34.3 0.0 collective-permute-done.refs_9_
  34.3 1.5 collective-permute-start.5
  35.8 25.3 %shard_map.94._ = f32[4,2,512,512]{3,2,1,0:T(8,128)} custom-call(f32[4,9]{1,0:T(4,128)} %pad_maximum_fusion.coef_ref._, f32[4,2,512,512]{3,2,1,0:T(8,128)} %base_ref.3, f32[4,9]{1,0:T(4,128)} %pad_maximum_fusion.coef_ref._, bf16[2,2,512,512]{3,2,1,0:T(8,128)(2,1)} %copy-done, ...), custom_call_target="tpu_custom_call" | custom-call | flops 17179869184 | bytes 25165824 | tf_op jit(solution)/shard_map/pallas_call | solution.py:203
  61.1 0.0 collective-permute-done.1.refs_9_
  61.1 0.0 copy-done.8
  61.2 0.4 collective-permute-start.6
  61.6 25.4 %shard_map.95.base_ref = f32[4,2,512,512]{3,2,1,0:T(8,128)} custom-call(f32[4,9]{1,0:T(4,128)} %pad_maximum_fusion.coef_ref._, f32[4,2,512,512]{3,2,1,0:T(8,128)} %base_ref.3, f32[4,2,512,512]{3,2,1,0:T(8,128)} %shard_map.94._, bf16[2,2,512,512]{3,2,1,0:T(8,128)(2,1)} %get-tuple-element.21.refs_6_.refs_0_.refs_3_, ...), custom_call_target="tpu_custom_call", output_to_operand_aliasing={{}: (2, {})} | custom-call | flops 17179869184 | bytes 25165824 | tf_op jit(solution)/shard_map/pallas_call | solution.py:203
  86.9 0.0 collective-permute-done.2.refs_0_
  86.9 0.8 collective-permute-start.7
  87.8 11.2 %shard_map.96.base_ref = f32[4,2,512,512]{3,2,1,0:T(8,128)} custom-call(f32[4,9]{1,0:T(4,128)} %pad_maximum_fusion.coef_ref._, f32[4,2,512,512]{3,2,1,0:T(8,128)} %shard_map.95.base_ref, f32[4,9]{1,0:T(4,128)} %pad_maximum_fusion.coef_ref._, bf16[3,2,512,512]{3,2,1,0:T(8,128)(2,1)} %collective-permute-done.2.refs_0_, ...), custom_call_target="tpu_custom_call", output_to_operand_aliasing={{}: (1, {})} | custom-call | flops 6442450944 | bytes 17825792 | tf_op jit(solution)/shard_map/pallas_call | solution.py:203
  98.9 0.0 collective-permute-done.3.refs_0_
  98.9 1.3 collective-permute-start.10
  100.3 0.0 collective-permute-done.4.refs_3_
  100.3 2.5 %collective-permute-start.9 = (bf16[1,1,512,512]{3,2,1,0:T(8,128)(2,1)}, bf16[1,1,512,512]{3,2,1,0:T(8,128)(2,1)S(1)}, u32[]{:S(2)}, u32[]{:S(2)}) collective-permute-start(bf16[1,1,512,512]{3,2,1,0:T(8,128)(2,1)} %get-tuple-element.26), channel_id=1, source_target_pairs={{0,16},{4,20},{8,24},{12,28},{16,0},{20,4},{24,8},{28,12},{1,17},{... | collective-permute-start | bytes 1572872 | tf_op jit(solution)/shard_map/ppermute | solution.py:353
  102.8 14.3 %shard_map.97.base_ref = f32[4,2,512,512]{3,2,1,0:T(8,128)} custom-call(f32[4,9]{1,0:T(4,128)} %pad_maximum_fusion.coef_ref._, f32[4,2,512,512]{3,2,1,0:T(8,128)} %shard_map.96.base_ref, f32[4,9]{1,0:T(4,128)} %pad_maximum_fusion.coef_ref._, bf16[2,2,512,512]{3,2,1,0:T(8,128)(2,1)} %collective-permute-done.3.refs_0_, ...), custom_call_target="tpu_custom_call", output_to_operand_aliasing={{}: (1, {})} | custom-call | flops 8589934592 | bytes 16777216 | tf_op jit(solution)/shard_map/pallas_call | solution.py:203
  117.1 10.2 %collective-permute-done.5.refs_0_ = bf16[4,2,512,512]{3,2,1,0:T(8,128)(2,1)} collective-permute-done((bf16[4,2,512,512]{3,2,1,0:T(8,128)(2,1)}, bf16[4,2,512,512]{3,2,1,0:T(8,128)(2,1)}, u32[]{:S(2)}, u32[]{:S(2)}) %collective-permute-start.5) | collective-permute-done | bytes 4194336 | tf_op jit(solution)/shard_map/ppermute | solution.py:353
  127.2 0.0 copy-done.7
  127.2 0.5 collective-permute-start.8
  127.8 13.6 %shard_map.98.base_ref = f32[4,2,512,512]{3,2,1,0:T(8,128)} custom-call(f32[4,9]{1,0:T(4,128)} %pad_maximum_fusion.coef_ref._, f32[4,2,512,512]{3,2,1,0:T(8,128)} %shard_map.97.base_ref, f32[4,9]{1,0:T(4,128)} %pad_maximum_fusion.coef_ref._, bf16[4,2,512,512]{3,2,1,0:T(8,128)(2,1)} %collective-permute-done.5.refs_0_, ...), custom_call_target="tpu_custom_call", output_to_operand_aliasing={{}: (1, {})} | custom-call | flops 8589934592 | bytes 23068672 | tf_op jit(solution)/shard_map/pallas_call | solution.py:203
  141.4 1.6 collective-permute-done.6.refs_0_
  143.0 0.0 copy-done.9
  143.0 0.0 collective-permute-start.11
  143.0 12.2 %collective-permute-done.7.refs_3_ = bf16[1,2,512,512]{3,2,1,0:T(8,128)(2,1)S(1)} collective-permute-done((bf16[1,2,512,512]{3,2,1,0:T(8,128)(2,1)S(1)}, bf16[1,2,512,512]{3,2,1,0:T(8,128)(2,1)S(1)}, u32[]{:S(2)}, u32[]{:S(2)}) %collective-permute-start.7) | collective-permute-done | bytes 1048608 | tf_op jit(solution)/shard_map/ppermute | solution.py:353
  155.2 0.0 collective-permute-start.12
  155.2 0.0 copy-done.3
  155.2 1.0 copy-done.4
  156.2 9.3 %shard_map.99.base_ref = f32[4,2,512,512]{3,2,1,0:T(8,128)} custom-call(f32[4,9]{1,0:T(4,128)} %pad_maximum_fusion.coef_ref._, f32[4,2,512,512]{3,2,1,0:T(8,128)} %shard_map.98.base_ref, f32[4,9]{1,0:T(4,128)} %pad_maximum_fusion.coef_ref._, bf16[1,2,512,512]{3,2,1,0:T(8,128)(2,1)} %copy-done.3, ...), custom_call_target="tpu_custom_call", output_to_operand_aliasing={{}: (1, {})} | custom-call | flops 4294967296 | bytes 10485760 | tf_op jit(solution)/shard_map/pallas_call | solution.py:203
  165.6 0.0 collective-permute-done.8.refs_0_
  165.6 0.1 collective-permute-start.13
  165.6 0.9 copy-done.2
  166.6 6.2 %shard_map.100.base_ref._ = f32[4,2,512,512]{3,2,1,0:T(8,128)} custom-call(f32[4,9]{1,0:T(4,128)} %pad_maximum_fusion.coef_ref._, f32[4,2,512,512]{3,2,1,0:T(8,128)} %shard_map.99.base_ref, f32[4,9]{1,0:T(4,128)} %pad_maximum_fusion.coef_ref._, bf16[1,2,512,512]{3,2,1,0:T(8,128)(2,1)} %copy-done.2, ...), custom_call_target="tpu_custom_call", output_to_operand_aliasing={{}: (1, {})} | custom-call | flops 2147483648 | bytes 7340032 | tf_op jit(solution)/shard_map/pallas_call | solution.py:203
  172.7 0.0 collective-permute-done.10.refs_1_
  172.7 1.1 collective-permute-start.14
  173.8 0.0 collective-permute-done.9.refs_0_
  173.8 0.0 copy-done.1
  173.8 5.8 %shard_map.101 = (f32[2,512,512]{2,1,0:T(8,128)S(1)}, bf16[2,2,512,512]{3,2,1,0:T(8,128)(2,1)S(1)}, bf16[2,2,512,512]{3,2,1,0:T(8,128)(2,1)S(1)}, f32[2,8,512]{2,1,0:T(8,128)S(1)}) custom-call(f32[4,9]{1,0:T(4,128)S(1)} %copy-done.1, f32[4,2,512,512]{3,2,1,0:T(8,128)} %shard_map.100.base_ref._, ...), custom_call_target="tpu_custom_call" | custom-call | flops 2147483648 | bytes 8388608 | tf_op jit(solution)/shard_map/pallas_call | solution.py:302
  179.6 2.8 %collective-permute-done.11.refs_0_ = bf16[1,1,384,512]{3,2,1,0:T(8,128)(2,1)S(1)} collective-permute-done((bf16[1,1,384,512]{3,2,1,0:T(8,128)(2,1)S(1)}, bf16[1,1,384,512]{3,2,1,0:T(8,128)(2,1)S(1)}, u32[]{:S(2)}, u32[]{:S(2)}) %collective-permute-start.11) | collective-permute-done | bytes 393248 | tf_op jit(solution)/shard_map/ppermute | solution.py:353
  182.4 0.9 collective-permute-done.12.refs_1_
  183.3 2.2 %shard_map.102.total = f32[2,512,512]{2,1,0:T(8,128)S(1)} custom-call(f32[2,512,512]{2,1,0:T(8,128)S(1)} %get-tuple-element.27.total, bf16[2,2,512,512]{3,2,1,0:T(8,128)(2,1)S(1)} %get-tuple-element.28.left, bf16[2,2,512,512]{3,2,1,0:T(8,128)(2,1)S(1)} %get-tuple-element.29.right, ...), custom_call_target="tpu_custom_call", output_to_operand_aliasing={{}: (0, {})} | custom-call | flops 1610612736 | bytes 8388608 | tf_op jit(solution)/shard_map/pallas_call | solution.py:302
  185.5 2.3 %collective-permute-done.13.refs_0_ = bf16[1,1,128,512]{3,2,1,0:T(8,128)(2,1)S(1)} collective-permute-done((bf16[1,1,128,512]{3,2,1,0:T(8,128)(2,1)S(1)}, bf16[1,1,128,512]{3,2,1,0:T(8,128)(2,1)S(1)}, u32[]{:S(2)}, u32[]{:S(2)}) %collective-permute-start.13) | collective-permute-done | bytes 131104 | tf_op jit(solution)/shard_map/ppermute | solution.py:353
  187.8 0.1 collective-permute-done.14.refs_1_
  187.8 1.9 %shard_map.103 = f32[4,2,512,512]{3,2,1,0:T(8,128)} custom-call(f32[4,2,512,512]{3,2,1,0:T(8,128)} %shard_map.100.base_ref._, f32[2,512,512]{2,1,0:T(8,128)S(1)} %shard_map.102.total, bf16[2,2,512,512]{3,2,1,0:T(8,128)(2,1)S(1)} %get-tuple-element.28.left, bf16[2,2,512,512]{3,2,1,0:T(8,128)(2,1)S(1)} %get-tuple-element.29.right, ...), custom_call_target="tpu_custom_call", output_to_operand_aliasing={{}: (0, {})} | custom-call | flops 536870912 | bytes 8388608 | tf_op jit(solution)/shard_map/pallas_call | solution.py:302
  (11 shorter events, 0.0 us)
Async XLA Ops:
  2.3 5.8 %copy-start = (bf16[2,2,512,512]{3,2,1,0:T(8,128)(2,1)}, bf16[2,2,512,512]{3,2,1,0:T(8,128)(2,1)S(1)}, u32[]{:S(2)}) copy-start(bf16[2,2,512,512]{3,2,1,0:T(8,128)(2,1)S(1)} %shard_map.91._.refs_0_.refs_3_.refs_6_) | copy-start | bytes 6291460
  2.3 15.4 %copy-start.11 = (s32[7]{0:T(128)S(1)}, s32[7]{0:T(128)}, u32[]{:S(2)}) copy-start(s32[7]{0:T(128)} %param.15) | copy-start | bytes 88
  2.3 15.6 %copy-start.5 = (f32[7]{0:T(128)S(1)}, f32[7]{0:T(128)}, u32[]{:S(2)}) copy-start(f32[7]{0:T(128)} %param.17) | copy-start | bytes 88
  2.3 15.6 %copy-start.6 = (f32[7]{0:T(128)S(1)}, f32[7]{0:T(128)}, u32[]{:S(2)}) copy-start(f32[7]{0:T(128)} %param.16) | copy-start | bytes 88
  2.3 32.0 %collective-permute-start = (bf16[2,2,512,512]{3,2,1,0:T(8,128)(2,1)S(1)}, bf16[2,2,512,512]{3,2,1,0:T(8,128)(2,1)}, u32[]{:S(2)}, u32[]{:S(2)}) collective-permute-start(bf16[2,2,512,512]{3,2,1,0:T(8,128)(2,1)S(1)} %shard_map.91._.refs_0_.refs_3_.refs_6_), channel_id=1, source_target_pairs={{0,4},{4,0},{8,12},{12,8},{16,20},{20,16},{24,28},{28,24},{1,5},{5... | collective-permute-start | bytes 6291464 | tf_op jit(solution)/shard_map/ppermute | solution.py:353
  2.8 96.1 %collective-permute-start.3 = (bf16[2,2,512,512]{3,2,1,0:T(8,128)(2,1)S(1)}, bf16[2,2,512,512]{3,2,1,0:T(8,128)(2,1)}, u32[]{:S(2)}, u32[]{:S(2)}) collective-permute-start(bf16[2,2,512,512]{3,2,1,0:T(8,128)(2,1)S(1)} %shard_map.91._.refs_0_.refs_3_.refs_6_), channel_id=1, source_target_pairs={{0,16},{4,20},{8,24},{12,28},{16,0},{20,4},{24,8},{28,12},{1,17},{... | collective-permute-start | bytes 6291464 | tf_op jit(solution)/shard_map/ppermute | solution.py:353
  6.5 93.8 %collective-permute-start.4 = (bf16[2,2,512,512]{3,2,1,0:T(8,128)(2,1)S(1)}, bf16[2,2,512,512]{3,2,1,0:T(8,128)(2,1)}, u32[]{:S(2)}, u32[]{:S(2)}) collective-permute-start(bf16[2,2,512,512]{3,2,1,0:T(8,128)(2,1)S(1)} %shard_map.91._.refs_0_.refs_3_.refs_6_), channel_id=1, source_target_pairs={{0,8},{4,12},{8,0},{12,4},{16,24},{20,28},{24,16},{28,20},{1,9},{5... | collective-permute-start | bytes 6291464 | tf_op jit(solution)/shard_map/ppermute | solution.py:353
  16.0 45.2 %collective-permute-start.1 = (bf16[2,2,512,512]{3,2,1,0:T(8,128)(2,1)}, bf16[2,2,512,512]{3,2,1,0:T(8,128)(2,1)}, u32[]{:S(2)}, u32[]{:S(2)}) collective-permute-start(bf16[2,2,512,512]{3,2,1,0:T(8,128)(2,1)} %get-tuple-element.21.refs_6_.refs_0_.refs_3_), channel_id=1, source_target_pairs={{0,4},{4,0},{8,12},{12,8},{16,20},{20,16},{24,28},{28,24},{1,5},{5... | collective-permute-start | bytes 6291464 | tf_op jit(solution)/shard_map/ppermute | solution.py:353
  16.1 70.9 %collective-permute-start.2 = (bf16[3,2,512,512]{3,2,1,0:T(8,128)(2,1)}, bf16[3,2,512,512]{3,2,1,0:T(8,128)(2,1)}, u32[]{:S(2)}, u32[]{:S(2)}) collective-permute-start(bf16[3,2,512,512]{3,2,1,0:T(8,128)(2,1)} %get-tuple-element.22), channel_id=1, source_target_pairs={{0,1},{1,0},{2,3},{3,2},{4,5},{5,4},{6,7},{7,6},{8,9},{9,8},{10,11... | collective-permute-start | bytes 9437192 | tf_op jit(solution)/shard_map/ppermute | solution.py:353
  34.3 93.0 %collective-permute-start.5 = (bf16[4,2,512,512]{3,2,1,0:T(8,128)(2,1)}, bf16[4,2,512,512]{3,2,1,0:T(8,128)(2,1)}, u32[]{:S(2)}, u32[]{:S(2)}) collective-permute-start(bf16[4,2,512,512]{3,2,1,0:T(8,128)(2,1)} %get-tuple-element.23), channel_id=1, source_target_pairs={{0,2},{1,3},{2,0},{3,1},{4,6},{5,7},{6,4},{7,5},{8,10},{9,11},{10,... | collective-permute-start | bytes 12582920 | tf_op jit(solution)/shard_map/ppermute | solution.py:353
  35.8 25.4 %copy-start.8 = (bf16[1,2,512,512]{3,2,1,0:T(8,128)(2,1)S(1)}, bf16[1,2,512,512]{3,2,1,0:T(8,128)(2,1)}, u32[]{:S(2)}) copy-start(bf16[1,2,512,512]{3,2,1,0:T(8,128)(2,1)} %get-tuple-element.24) | copy-start | bytes 3145732
  61.2 81.8 %collective-permute-start.6 = (bf16[1,2,512,512]{3,2,1,0:T(8,128)(2,1)S(1)}, bf16[1,2,512,512]{3,2,1,0:T(8,128)(2,1)S(1)}, u32[]{:S(2)}, u32[]{:S(2)}) collective-permute-start(bf16[1,2,512,512]{3,2,1,0:T(8,128)(2,1)S(1)} %copy-done.8), channel_id=1, source_target_pairs={{0,16},{4,20},{8,24},{12,28},{16,0},{20,4},{24,8},{28,12},{1,17},{... | collective-permute-start | bytes 3145736 | tf_op jit(solution)/shard_map/ppermute | solution.py:353
  86.9 68.3 %collective-permute-start.7 = (bf16[1,2,512,512]{3,2,1,0:T(8,128)(2,1)S(1)}, bf16[1,2,512,512]{3,2,1,0:T(8,128)(2,1)S(1)}, u32[]{:S(2)}, u32[]{:S(2)}) collective-permute-start(bf16[1,2,512,512]{3,2,1,0:T(8,128)(2,1)S(1)} %copy-done.8), channel_id=1, source_target_pairs={{0,8},{4,12},{8,0},{12,4},{16,24},{20,28},{24,16},{28,20},{1,9},{5... | collective-permute-start | bytes 3145736 | tf_op jit(solution)/shard_map/ppermute | solution.py:353
  98.9 28.3 %copy-start.7 = (bf16[1,2,512,512]{3,2,1,0:T(8,128)(2,1)S(1)}, bf16[1,2,512,512]{3,2,1,0:T(8,128)(2,1)}, u32[]{:S(2)}) copy-start(bf16[1,2,512,512]{3,2,1,0:T(8,128)(2,1)} %get-tuple-element.25) | copy-start | bytes 3145732
  98.9 73.8 %collective-permute-start.10 = (bf16[1,1,512,512]{3,2,1,0:T(8,128)(2,1)}, bf16[1,1,512,512]{3,2,1,0:T(8,128)(2,1)S(1)}, u32[]{:S(2)}, u32[]{:S(2)}) collective-permute-start(bf16[1,1,512,512]{3,2,1,0:T(8,128)(2,1)} %get-tuple-element.26), channel_id=1, source_target_pairs={{0,8},{4,12},{8,0},{12,4},{16,24},{20,28},{24,16},{28,20},{1,9},{5... | collective-permute-start | bytes 1572872 | tf_op jit(solution)/shard_map/ppermute | solution.py:353
  100.3 73.5 %collective-permute-start.9 = (bf16[1,1,512,512]{3,2,1,0:T(8,128)(2,1)}, bf16[1,1,512,512]{3,2,1,0:T(8,128)(2,1)S(1)}, u32[]{:S(2)}, u32[]{:S(2)}) collective-permute-start(bf16[1,1,512,512]{3,2,1,0:T(8,128)(2,1)} %get-tuple-element.26), channel_id=1, source_target_pairs={{0,16},{4,20},{8,24},{12,28},{16,0},{20,4},{24,8},{28,12},{1,17},{... | collective-permute-start | bytes 1572872 | tf_op jit(solution)/shard_map/ppermute | solution.py:353
  127.2 15.8 %copy-start.9 = (bf16[1,1,384,512]{3,2,1,0:T(8,128)(2,1)S(1)}, bf16[1,1,384,512]{3,2,1,0:T(8,128)(2,1)}, u32[]{:S(2)}) copy-start(bf16[1,1,384,512]{3,2,1,0:T(8,128)(2,1)} %get-tuple-element.31) | copy-start | bytes 1179652
  127.2 38.3 %collective-permute-start.8 = (bf16[1,2,512,512]{3,2,1,0:T(8,128)(2,1)S(1)}, bf16[1,2,512,512]{3,2,1,0:T(8,128)(2,1)S(1)}, u32[]{:S(2)}, u32[]{:S(2)}) collective-permute-start(bf16[1,2,512,512]{3,2,1,0:T(8,128)(2,1)S(1)} %copy-done.7), channel_id=1, source_target_pairs={{0,1},{1,0},{2,3},{3,2},{4,5},{5,4},{6,7},{7,6},{8,9},{9,8},{10,11... | collective-permute-start | bytes 3145736 | tf_op jit(solution)/shard_map/ppermute | solution.py:353
  143.0 12.2 %copy-start.3 = (bf16[1,2,512,512]{3,2,1,0:T(8,128)(2,1)}, bf16[1,2,512,512]{3,2,1,0:T(8,128)(2,1)S(1)}, u32[]{:S(2)}) copy-start(bf16[1,2,512,512]{3,2,1,0:T(8,128)(2,1)S(1)} %collective-permute-done.6.refs_0_) | copy-start | bytes 3145732
  143.0 22.5 %copy-start.10 = (bf16[1,1,128,512]{3,2,1,0:T(8,128)(2,1)S(1)}, bf16[1,1,128,512]{3,2,1,0:T(8,128)(2,1)}, u32[]{:S(2)}) copy-start(bf16[1,1,128,512]{3,2,1,0:T(8,128)(2,1)} %get-tuple-element.32) | copy-start | bytes 393220
  143.0 39.4 %collective-permute-start.11 = (bf16[1,1,384,512]{3,2,1,0:T(8,128)(2,1)S(1)}, bf16[1,1,384,512]{3,2,1,0:T(8,128)(2,1)S(1)}, u32[]{:S(2)}, u32[]{:S(2)}) collective-permute-start(bf16[1,1,384,512]{3,2,1,0:T(8,128)(2,1)S(1)} %copy-done.9), channel_id=1, source_target_pairs={{0,16},{4,20},{8,24},{12,28},{16,0},{20,4},{24,8},{28,12},{1,17},{... | collective-permute-start | bytes 1179656 | tf_op jit(solution)/shard_map/ppermute | solution.py:353
  155.2 1.0 copy-start.4
  155.2 28.0 %collective-permute-start.12 = (bf16[1,1,384,512]{3,2,1,0:T(8,128)(2,1)S(1)}, bf16[1,1,384,512]{3,2,1,0:T(8,128)(2,1)S(1)}, u32[]{:S(2)}, u32[]{:S(2)}) collective-permute-start(bf16[1,1,384,512]{3,2,1,0:T(8,128)(2,1)S(1)} %copy-done.9), channel_id=1, source_target_pairs={{0,8},{4,12},{8,0},{12,4},{16,24},{20,28},{24,16},{28,20},{1,9},{5... | collective-permute-start | bytes 1179656 | tf_op jit(solution)/shard_map/ppermute | solution.py:353
  165.6 1.0 copy-start.2
  165.6 8.2 %copy-start.1 = (f32[4,9]{1,0:T(4,128)S(1)}, f32[4,9]{1,0:T(4,128)}, u32[]{:S(2)}) copy-start(f32[4,9]{1,0:T(4,128)} %pad_maximum_fusion.coef_ref._) | copy-start | bytes 436
  165.6 22.2 %collective-permute-start.13 = (bf16[1,1,128,512]{3,2,1,0:T(8,128)(2,1)S(1)}, bf16[1,1,128,512]{3,2,1,0:T(8,128)(2,1)S(1)}, u32[]{:S(2)}, u32[]{:S(2)}) collective-permute-start(bf16[1,1,128,512]{3,2,1,0:T(8,128)(2,1)S(1)} %copy-done.10), channel_id=1, source_target_pairs={{0,16},{4,20},{8,24},{12,28},{16,0},{20,4},{24,8},{28,12},{1,17},{... | collective-permute-start | bytes 393224 | tf_op jit(solution)/shard_map/ppermute | solution.py:353
  172.7 15.1 %collective-permute-start.14 = (bf16[1,1,128,512]{3,2,1,0:T(8,128)(2,1)S(1)}, bf16[1,1,128,512]{3,2,1,0:T(8,128)(2,1)S(1)}, u32[]{:S(2)}, u32[]{:S(2)}) collective-permute-start(bf16[1,1,128,512]{3,2,1,0:T(8,128)(2,1)S(1)} %copy-done.10), channel_id=1, source_target_pairs={{0,8},{4,12},{8,0},{12,4},{16,24},{20,28},{24,16},{28,20},{1,9},{5... | collective-permute-start | bytes 393224 | tf_op jit(solution)/shard_map/ppermute | solution.py:353

commit v5 on v4

--- a/solution.py
+++ b/solution.py
@@ -216,7 +216,7 @@
 
 def bands_of(cut, n):
     _, first, size = cut
-    bands = [(first, first + size), (0, first), (first + size, n)]
+    bands = [(0, first), (first + size, n), (first, first + size)]
     return [rows for rows in bands if rows[0] < rows[1]]
 
 

time: 190 us -> 190 us (level)
  no operation moved by 1% of the time
where the time goes in v5:
time: 190 us
  Pallas kernels  141 us (74%)
  waiting for transfers between devices  30.1 us (16%)
  starting transfers between devices  15.6 us (8%)
  local copies, waits for them, and re-layouts  2.09 us (1%)
    pallas_call x7, Pallas kernels, add_terms(): pl.pallas_call(functools.partial(term_kernel, first, [t[0] for t in terms...  105 us
    ppermute x15, waiting for transfers between devices, flip(): return lax.ppermute(value, axis, pairs)  30.1 us
    ppermute x15, starting transfers between devices, flip(): return lax.ppermute(value, axis, pairs)  15.6 us
    pallas_call x1, Pallas kernels, make_operators(): pl.pallas_call(operator_kernel, grid_spec=pltpu.PrefetchScalarGridSpec(nu...  15.4 us
    pallas_call x3, Pallas kernels, piece_call(): pl.pallas_call(functools.partial(kernel, index, modes, cut), in_specs=[sp...  9.78 us
    pallas_call x1, Pallas kernels, round_groups(): pl.pallas_call(functools.partial(round_kernel, groups, low, high), in_spe...  7.9 us
  transfers between devices with their start and end apart: 15, of which 7 were waited for; matrix products, arithmetic and copies ran while one was open for 1% of the time, Pallas kernels for 72%

profile of v5, /device:TPU:0, one launch (start us, length us, event | category | flops | bytes accessed | tf_op | source)
XLA Modules:
  0.0 189.8 jit_solution(16682992558092967220)
XLA Ops:
  0.0 2.3 %shard_map.91._.refs_0_.refs_3_.refs_6_ = bf16[2,2,512,512]{3,2,1,0:T(8,128)(2,1)S(1)} custom-call(f32[4,2,512,512]{3,2,1,0:T(8,128)} %base_ref.3), custom_call_target="tpu_custom_call" | custom-call | bytes 6291456 | tf_op jit(solution)/shard_map/pallas_call | solution.py:74
  2.3 0.0 copy-start
  2.3 0.0 copy-start.11
  2.3 0.0 copy-start.5
  2.3 0.0 copy-start.6
  2.3 0.5 collective-permute-start
  2.8 3.7 %collective-permute-start.3 = (bf16[2,2,512,512]{3,2,1,0:T(8,128)(2,1)S(1)}, bf16[2,2,512,512]{3,2,1,0:T(8,128)(2,1)}, u32[]{:S(2)}, u32[]{:S(2)}) collective-permute-start(bf16[2,2,512,512]{3,2,1,0:T(8,128)(2,1)S(1)} %shard_map.91._.refs_0_.refs_3_.refs_6_), channel_id=1, source_target_pairs={{0,16},{4,20},{8,24},{12,28},{16,0},{20,4},{24,8},{28,12},{1,17},{... | collective-permute-start | bytes 6291464 | tf_op jit(solution)/shard_map/ppermute | solution.py:353
  6.5 1.6 collective-permute-start.4
  8.1 0.0 copy-done
  8.1 7.9 %shard_map.93 = (bf16[2,2,512,512]{3,2,1,0:T(8,128)(2,1)}, bf16[3,2,512,512]{3,2,1,0:T(8,128)(2,1)}, bf16[4,2,512,512]{3,2,1,0:T(8,128)(2,1)}, bf16[1,2,512,512]...) custom-call(f32[4,2,512,512]{3,2,1,0:T(8,128)} %base_ref.3, ...), custom_call_target="tpu_custom_call" | custom-call | bytes 21495808 | tf_op jit(solution)/shard_map/pallas_call | solution.py:98
  16.0 0.1 collective-permute-start.1
  16.1 1.6 collective-permute-start.2
  17.6 0.1 shift-right-arithmetic_and_fusion
  17.7 0.0 copy-done.11
  17.7 0.2 reduce_window_sum.11
  17.9 0.0 copy-done.5
  17.9 0.0 copy-done.6
  17.9 0.2 fusion.5
  18.1 0.1 copy.18
  18.2 0.1 pad.1.clone
  18.2 15.4 %shard_map.92 = (bf16[8,2,512,512]{3,2,1,0:T(8,128)(2,1)}, bf16[8,2,512,512]{3,2,1,0:T(8,128)(2,1)}) custom-call(s32[7]{0:T(128)} %slot_ref.1, s32[7,2,8,8]{3,2,1,0:T(8,128)} %mask_ref.1, bf16[7,2,512,512]{3,2,1,0:T(8,128)(2,1)} %left_ref.1, bf16[7,2,512,512]{3,2,1,0:T(8,128)(2,1)} %right_ref.1, bf16[2,512,512]{2,1,0:T(8,128)(2,1)} %ham_ref.1), custom_call_target="tpu_custom_call" | custom-call | bytes 33554432 | tf_op jit(solution)/shard_map/pallas_call | solution.py:153
  33.6 0.7 pad_maximum_fusion.coef_ref._
  34.3 0.0 collective-permute-done.refs_9_
  34.3 1.5 collective-permute-start.5
  35.8 25.3 %shard_map.94._ = f32[4,2,512,512]{3,2,1,0:T(8,128)} custom-call(f32[4,9]{1,0:T(4,128)} %pad_maximum_fusion.coef_ref._, f32[4,2,512,512]{3,2,1,0:T(8,128)} %base_ref.3, f32[4,9]{1,0:T(4,128)} %pad_maximum_fusion.coef_ref._, bf16[2,2,512,512]{3,2,1,0:T(8,128)(2,1)} %copy-done, ...), custom_call_target="tpu_custom_call" | custom-call | flops 17179869184 | bytes 25165824 | tf_op jit(solution)/shard_map/pallas_call | solution.py:203
  61.1 0.0 collective-permute-done.1.refs_9_
  61.1 0.0 copy-done.8
  61.2 0.4 collective-permute-start.6
  61.6 25.4 %shard_map.95.base_ref = f32[4,2,512,512]{3,2,1,0:T(8,128)} custom-call(f32[4,9]{1,0:T(4,128)} %pad_maximum_fusion.coef_ref._, f32[4,2,512,512]{3,2,1,0:T(8,128)} %base_ref.3, f32[4,2,512,512]{3,2,1,0:T(8,128)} %shard_map.94._, bf16[2,2,512,512]{3,2,1,0:T(8,128)(2,1)} %get-tuple-element.21.refs_6_.refs_0_.refs_3_, ...), custom_call_target="tpu_custom_call", output_to_operand_aliasing={{}: (2, {})} | custom-call | flops 17179869184 | bytes 25165824 | tf_op jit(solution)/shard_map/pallas_call | solution.py:203
  86.9 0.0 collective-permute-done.2.refs_0_
  86.9 0.8 collective-permute-start.7
  87.8 11.2 %shard_map.96.base_ref = f32[4,2,512,512]{3,2,1,0:T(8,128)} custom-call(f32[4,9]{1,0:T(4,128)} %pad_maximum_fusion.coef_ref._, f32[4,2,512,512]{3,2,1,0:T(8,128)} %shard_map.95.base_ref, f32[4,9]{1,0:T(4,128)} %pad_maximum_fusion.coef_ref._, bf16[3,2,512,512]{3,2,1,0:T(8,128)(2,1)} %collective-permute-done.2.refs_0_, ...), custom_call_target="tpu_custom_call", output_to_operand_aliasing={{}: (1, {})} | custom-call | flops 6442450944 | bytes 17825792 | tf_op jit(solution)/shard_map/pallas_call | solution.py:203
  98.9 0.0 collective-permute-done.3.refs_0_
  98.9 1.3 collective-permute-start.10
  100.3 0.0 collective-permute-done.4.refs_3_
  100.3 2.5 %collective-permute-start.9 = (bf16[1,1,512,512]{3,2,1,0:T(8,128)(2,1)}, bf16[1,1,512,512]{3,2,1,0:T(8,128)(2,1)S(1)}, u32[]{:S(2)}, u32[]{:S(2)}) collective-permute-start(bf16[1,1,512,512]{3,2,1,0:T(8,128)(2,1)} %get-tuple-element.26), channel_id=1, source_target_pairs={{0,16},{4,20},{8,24},{12,28},{16,0},{20,4},{24,8},{28,12},{1,17},{... | collective-permute-start | bytes 1572872 | tf_op jit(solution)/shard_map/ppermute | solution.py:353
  102.8 14.3 %shard_map.97.base_ref = f32[4,2,512,512]{3,2,1,0:T(8,128)} custom-call(f32[4,9]{1,0:T(4,128)} %pad_maximum_fusion.coef_ref._, f32[4,2,512,512]{3,2,1,0:T(8,128)} %shard_map.96.base_ref, f32[4,9]{1,0:T(4,128)} %pad_maximum_fusion.coef_ref._, bf16[2,2,512,512]{3,2,1,0:T(8,128)(2,1)} %collective-permute-done.3.refs_0_, ...), custom_call_target="tpu_custom_call", output_to_operand_aliasing={{}: (1, {})} | custom-call | flops 8589934592 | bytes 16777216 | tf_op jit(solution)/shard_map/pallas_call | solution.py:203
  117.1 10.2 %collective-permute-done.5.refs_0_ = bf16[4,2,512,512]{3,2,1,0:T(8,128)(2,1)} collective-permute-done((bf16[4,2,512,512]{3,2,1,0:T(8,128)(2,1)}, bf16[4,2,512,512]{3,2,1,0:T(8,128)(2,1)}, u32[]{:S(2)}, u32[]{:S(2)}) %collective-permute-start.5) | collective-permute-done | bytes 4194336 | tf_op jit(solution)/shard_map/ppermute | solution.py:353
  127.2 0.0 copy-done.7
  127.2 0.5 collective-permute-start.8
  127.8 13.6 %shard_map.98.base_ref = f32[4,2,512,512]{3,2,1,0:T(8,128)} custom-call(f32[4,9]{1,0:T(4,128)} %pad_maximum_fusion.coef_ref._, f32[4,2,512,512]{3,2,1,0:T(8,128)} %shard_map.97.base_ref, f32[4,9]{1,0:T(4,128)} %pad_maximum_fusion.coef_ref._, bf16[4,2,512,512]{3,2,1,0:T(8,128)(2,1)} %collective-permute-done.5.refs_0_, ...), custom_call_target="tpu_custom_call", output_to_operand_aliasing={{}: (1, {})} | custom-call | flops 8589934592 | bytes 23068672 | tf_op jit(solution)/shard_map/pallas_call | solution.py:203
  141.4 1.6 collective-permute-done.6.refs_0_
  143.0 0.0 copy-done.9
  143.0 0.0 collective-permute-start.11
  143.0 12.2 %collective-permute-done.7.refs_3_ = bf16[1,2,512,512]{3,2,1,0:T(8,128)(2,1)S(1)} collective-permute-done((bf16[1,2,512,512]{3,2,1,0:T(8,128)(2,1)S(1)}, bf16[1,2,512,512]{3,2,1,0:T(8,128)(2,1)S(1)}, u32[]{:S(2)}, u32[]{:S(2)}) %collective-permute-start.7) | collective-permute-done | bytes 1048608 | tf_op jit(solution)/shard_map/ppermute | solution.py:353
  155.2 0.0 collective-permute-start.12
  155.2 0.0 copy-done.3
  155.2 1.0 copy-done.4
  156.2 9.3 %shard_map.99.base_ref = f32[4,2,512,512]{3,2,1,0:T(8,128)} custom-call(f32[4,9]{1,0:T(4,128)} %pad_maximum_fusion.coef_ref._, f32[4,2,512,512]{3,2,1,0:T(8,128)} %shard_map.98.base_ref, f32[4,9]{1,0:T(4,128)} %pad_maximum_fusion.coef_ref._, bf16[1,2,512,512]{3,2,1,0:T(8,128)(2,1)} %copy-done.3, ...), custom_call_target="tpu_custom_call", output_to_operand_aliasing={{}: (1, {})} | custom-call | flops 4294967296 | bytes 10485760 | tf_op jit(solution)/shard_map/pallas_call | solution.py:203
  165.6 0.0 collective-permute-done.8.refs_0_
  165.6 0.1 collective-permute-start.13
  165.6 0.9 copy-done.2
  166.6 6.2 %shard_map.100.base_ref._ = f32[4,2,512,512]{3,2,1,0:T(8,128)} custom-call(f32[4,9]{1,0:T(4,128)} %pad_maximum_fusion.coef_ref._, f32[4,2,512,512]{3,2,1,0:T(8,128)} %shard_map.99.base_ref, f32[4,9]{1,0:T(4,128)} %pad_maximum_fusion.coef_ref._, bf16[1,2,512,512]{3,2,1,0:T(8,128)(2,1)} %copy-done.2, ...), custom_call_target="tpu_custom_call", output_to_operand_aliasing={{}: (1, {})} | custom-call | flops 2147483648 | bytes 7340032 | tf_op jit(solution)/shard_map/pallas_call | solution.py:203
  172.7 0.0 collective-permute-done.10.refs_1_
  172.7 1.1 collective-permute-start.14
  173.8 0.0 collective-permute-done.9.refs_0_
  173.8 0.0 copy-done.1
  173.8 5.8 %shard_map.101 = (f32[2,512,512]{2,1,0:T(8,128)S(1)}, bf16[2,2,512,512]{3,2,1,0:T(8,128)(2,1)S(1)}, bf16[2,2,512,512]{3,2,1,0:T(8,128)(2,1)S(1)}, f32[2,8,512]{2,1,0:T(8,128)S(1)}) custom-call(f32[4,9]{1,0:T(4,128)S(1)} %copy-done.1, f32[4,2,512,512]{3,2,1,0:T(8,128)} %shard_map.100.base_ref._, ...), custom_call_target="tpu_custom_call" | custom-call | flops 2147483648 | bytes 8388608 | tf_op jit(solution)/shard_map/pallas_call | solution.py:302
  179.6 2.8 %collective-permute-done.11.refs_0_ = bf16[1,1,384,512]{3,2,1,0:T(8,128)(2,1)S(1)} collective-permute-done((bf16[1,1,384,512]{3,2,1,0:T(8,128)(2,1)S(1)}, bf16[1,1,384,512]{3,2,1,0:T(8,128)(2,1)S(1)}, u32[]{:S(2)}, u32[]{:S(2)}) %collective-permute-start.11) | collective-permute-done | bytes 393248 | tf_op jit(solution)/shard_map/ppermute | solution.py:353
  182.4 0.9 collective-permute-done.12.refs_1_
  183.3 2.2 %shard_map.102.total = f32[2,512,512]{2,1,0:T(8,128)S(1)} custom-call(f32[2,512,512]{2,1,0:T(8,128)S(1)} %get-tuple-element.27.total, bf16[2,2,512,512]{3,2,1,0:T(8,128)(2,1)S(1)} %get-tuple-element.28.left, bf16[2,2,512,512]{3,2,1,0:T(8,128)(2,1)S(1)} %get-tuple-element.29.right, ...), custom_call_target="tpu_custom_call", output_to_operand_aliasing={{}: (0, {})} | custom-call | flops 1610612736 | bytes 8388608 | tf_op jit(solution)/shard_map/pallas_call | solution.py:302
  185.5 2.3 %collective-permute-done.13.refs_0_ = bf16[1,1,128,512]{3,2,1,0:T(8,128)(2,1)S(1)} collective-permute-done((bf16[1,1,128,512]{3,2,1,0:T(8,128)(2,1)S(1)}, bf16[1,1,128,512]{3,2,1,0:T(8,128)(2,1)S(1)}, u32[]{:S(2)}, u32[]{:S(2)}) %collective-permute-start.13) | collective-permute-done | bytes 131104 | tf_op jit(solution)/shard_map/ppermute | solution.py:353
  187.8 0.1 collective-permute-done.14.refs_1_
  187.8 1.8 shard_map.103
  (11 shorter events, 0.0 us)
Async XLA Ops:
  2.3 5.8 %copy-start = (bf16[2,2,512,512]{3,2,1,0:T(8,128)(2,1)}, bf16[2,2,512,512]{3,2,1,0:T(8,128)(2,1)S(1)}, u32[]{:S(2)}) copy-start(bf16[2,2,512,512]{3,2,1,0:T(8,128)(2,1)S(1)} %shard_map.91._.refs_0_.refs_3_.refs_6_) | copy-start | bytes 6291460
  2.3 15.4 %copy-start.11 = (s32[7]{0:T(128)S(1)}, s32[7]{0:T(128)}, u32[]{:S(2)}) copy-start(s32[7]{0:T(128)} %param.15) | copy-start | bytes 88
  2.3 15.6 %copy-start.5 = (f32[7]{0:T(128)S(1)}, f32[7]{0:T(128)}, u32[]{:S(2)}) copy-start(f32[7]{0:T(128)} %param.17) | copy-start | bytes 88
  2.3 15.6 %copy-start.6 = (f32[7]{0:T(128)S(1)}, f32[7]{0:T(128)}, u32[]{:S(2)}) copy-start(f32[7]{0:T(128)} %param.16) | copy-start | bytes 88
  2.3 32.0 %collective-permute-start = (bf16[2,2,512,512]{3,2,1,0:T(8,128)(2,1)S(1)}, bf16[2,2,512,512]{3,2,1,0:T(8,128)(2,1)}, u32[]{:S(2)}, u32[]{:S(2)}) collective-permute-start(bf16[2,2,512,512]{3,2,1,0:T(8,128)(2,1)S(1)} %shard_map.91._.refs_0_.refs_3_.refs_6_), channel_id=1, source_target_pairs={{0,4},{4,0},{8,12},{12,8},{16,20},{20,16},{24,28},{28,24},{1,5},{5... | collective-permute-start | bytes 6291464 | tf_op jit(solution)/shard_map/ppermute | solution.py:353
  2.8 96.1 %collective-permute-start.3 = (bf16[2,2,512,512]{3,2,1,0:T(8,128)(2,1)S(1)}, bf16[2,2,512,512]{3,2,1,0:T(8,128)(2,1)}, u32[]{:S(2)}, u32[]{:S(2)}) collective-permute-start(bf16[2,2,512,512]{3,2,1,0:T(8,128)(2,1)S(1)} %shard_map.91._.refs_0_.refs_3_.refs_6_), channel_id=1, source_target_pairs={{0,16},{4,20},{8,24},{12,28},{16,0},{20,4},{24,8},{28,12},{1,17},{... | collective-permute-start | bytes 6291464 | tf_op jit(solution)/shard_map/ppermute | solution.py:353
  6.5 93.8 %collective-permute-start.4 = (bf16[2,2,512,512]{3,2,1,0:T(8,128)(2,1)S(1)}, bf16[2,2,512,512]{3,2,1,0:T(8,128)(2,1)}, u32[]{:S(2)}, u32[]{:S(2)}) collective-permute-start(bf16[2,2,512,512]{3,2,1,0:T(8,128)(2,1)S(1)} %shard_map.91._.refs_0_.refs_3_.refs_6_), channel_id=1, source_target_pairs={{0,8},{4,12},{8,0},{12,4},{16,24},{20,28},{24,16},{28,20},{1,9},{5... | collective-permute-start | bytes 6291464 | tf_op jit(solution)/shard_map/ppermute | solution.py:353
  16.0 45.2 %collective-permute-start.1 = (bf16[2,2,512,512]{3,2,1,0:T(8,128)(2,1)}, bf16[2,2,512,512]{3,2,1,0:T(8,128)(2,1)}, u32[]{:S(2)}, u32[]{:S(2)}) collective-permute-start(bf16[2,2,512,512]{3,2,1,0:T(8,128)(2,1)} %get-tuple-element.21.refs_6_.refs_0_.refs_3_), channel_id=1, source_target_pairs={{0,4},{4,0},{8,12},{12,8},{16,20},{20,16},{24,28},{28,24},{1,5},{5... | collective-permute-start | bytes 6291464 | tf_op jit(solution)/shard_map/ppermute | solution.py:353
  16.1 70.9 %collective-permute-start.2 = (bf16[3,2,512,512]{3,2,1,0:T(8,128)(2,1)}, bf16[3,2,512,512]{3,2,1,0:T(8,128)(2,1)}, u32[]{:S(2)}, u32[]{:S(2)}) collective-permute-start(bf16[3,2,512,512]{3,2,1,0:T(8,128)(2,1)} %get-tuple-element.22), channel_id=1, source_target_pairs={{0,1},{1,0},{2,3},{3,2},{4,5},{5,4},{6,7},{7,6},{8,9},{9,8},{10,11... | collective-permute-start | bytes 9437192 | tf_op jit(solution)/shard_map/ppermute | solution.py:353
  34.3 93.0 %collective-permute-start.5 = (bf16[4,2,512,512]{3,2,1,0:T(8,128)(2,1)}, bf16[4,2,512,512]{3,2,1,0:T(8,128)(2,1)}, u32[]{:S(2)}, u32[]{:S(2)}) collective-permute-start(bf16[4,2,512,512]{3,2,1,0:T(8,128)(2,1)} %get-tuple-element.23), channel_id=1, source_target_pairs={{0,2},{1,3},{2,0},{3,1},{4,6},{5,7},{6,4},{7,5},{8,10},{9,11},{10,... | collective-permute-start | bytes 12582920 | tf_op jit(solution)/shard_map/ppermute | solution.py:353
  35.8 25.4 %copy-start.8 = (bf16[1,2,512,512]{3,2,1,0:T(8,128)(2,1)S(1)}, bf16[1,2,512,512]{3,2,1,0:T(8,128)(2,1)}, u32[]{:S(2)}) copy-start(bf16[1,2,512,512]{3,2,1,0:T(8,128)(2,1)} %get-tuple-element.24) | copy-start | bytes 3145732
  61.2 81.8 %collective-permute-start.6 = (bf16[1,2,512,512]{3,2,1,0:T(8,128)(2,1)S(1)}, bf16[1,2,512,512]{3,2,1,0:T(8,128)(2,1)S(1)}, u32[]{:S(2)}, u32[]{:S(2)}) collective-permute-start(bf16[1,2,512,512]{3,2,1,0:T(8,128)(2,1)S(1)} %copy-done.8), channel_id=1, source_target_pairs={{0,16},{4,20},{8,24},{12,28},{16,0},{20,4},{24,8},{28,12},{1,17},{... | collective-permute-start | bytes 3145736 | tf_op jit(solution)/shard_map/ppermute | solution.py:353
  86.9 68.3 %collective-permute-start.7 = (bf16[1,2,512,512]{3,2,1,0:T(8,128)(2,1)S(1)}, bf16[1,2,512,512]{3,2,1,0:T(8,128)(2,1)S(1)}, u32[]{:S(2)}, u32[]{:S(2)}) collective-permute-start(bf16[1,2,512,512]{3,2,1,0:T(8,128)(2,1)S(1)} %copy-done.8), channel_id=1, source_target_pairs={{0,8},{4,12},{8,0},{12,4},{16,24},{20,28},{24,16},{28,20},{1,9},{5... | collective-permute-start | bytes 3145736 | tf_op jit(solution)/shard_map/ppermute | solution.py:353
  98.9 28.3 %copy-start.7 = (bf16[1,2,512,512]{3,2,1,0:T(8,128)(2,1)S(1)}, bf16[1,2,512,512]{3,2,1,0:T(8,128)(2,1)}, u32[]{:S(2)}) copy-start(bf16[1,2,512,512]{3,2,1,0:T(8,128)(2,1)} %get-tuple-element.25) | copy-start | bytes 3145732
  98.9 73.8 %collective-permute-start.10 = (bf16[1,1,512,512]{3,2,1,0:T(8,128)(2,1)}, bf16[1,1,512,512]{3,2,1,0:T(8,128)(2,1)S(1)}, u32[]{:S(2)}, u32[]{:S(2)}) collective-permute-start(bf16[1,1,512,512]{3,2,1,0:T(8,128)(2,1)} %get-tuple-element.26), channel_id=1, source_target_pairs={{0,8},{4,12},{8,0},{12,4},{16,24},{20,28},{24,16},{28,20},{1,9},{5... | collective-permute-start | bytes 1572872 | tf_op jit(solution)/shard_map/ppermute | solution.py:353
  100.3 73.5 %collective-permute-start.9 = (bf16[1,1,512,512]{3,2,1,0:T(8,128)(2,1)}, bf16[1,1,512,512]{3,2,1,0:T(8,128)(2,1)S(1)}, u32[]{:S(2)}, u32[]{:S(2)}) collective-permute-start(bf16[1,1,512,512]{3,2,1,0:T(8,128)(2,1)} %get-tuple-element.26), channel_id=1, source_target_pairs={{0,16},{4,20},{8,24},{12,28},{16,0},{20,4},{24,8},{28,12},{1,17},{... | collective-permute-start | bytes 1572872 | tf_op jit(solution)/shard_map/ppermute | solution.py:353
  127.2 15.8 %copy-start.9 = (bf16[1,1,384,512]{3,2,1,0:T(8,128)(2,1)S(1)}, bf16[1,1,384,512]{3,2,1,0:T(8,128)(2,1)}, u32[]{:S(2)}) copy-start(bf16[1,1,384,512]{3,2,1,0:T(8,128)(2,1)} %get-tuple-element.31) | copy-start | bytes 1179652
  127.2 38.3 %collective-permute-start.8 = (bf16[1,2,512,512]{3,2,1,0:T(8,128)(2,1)S(1)}, bf16[1,2,512,512]{3,2,1,0:T(8,128)(2,1)S(1)}, u32[]{:S(2)}, u32[]{:S(2)}) collective-permute-start(bf16[1,2,512,512]{3,2,1,0:T(8,128)(2,1)S(1)} %copy-done.7), channel_id=1, source_target_pairs={{0,1},{1,0},{2,3},{3,2},{4,5},{5,4},{6,7},{7,6},{8,9},{9,8},{10,11... | collective-permute-start | bytes 3145736 | tf_op jit(solution)/shard_map/ppermute | solution.py:353
  143.0 12.2 %copy-start.3 = (bf16[1,2,512,512]{3,2,1,0:T(8,128)(2,1)}, bf16[1,2,512,512]{3,2,1,0:T(8,128)(2,1)S(1)}, u32[]{:S(2)}) copy-start(bf16[1,2,512,512]{3,2,1,0:T(8,128)(2,1)S(1)} %collective-permute-done.6.refs_0_) | copy-start | bytes 3145732
  143.0 22.5 %copy-start.10 = (bf16[1,1,128,512]{3,2,1,0:T(8,128)(2,1)S(1)}, bf16[1,1,128,512]{3,2,1,0:T(8,128)(2,1)}, u32[]{:S(2)}) copy-start(bf16[1,1,128,512]{3,2,1,0:T(8,128)(2,1)} %get-tuple-element.32) | copy-start | bytes 393220
  143.0 39.4 %collective-permute-start.11 = (bf16[1,1,384,512]{3,2,1,0:T(8,128)(2,1)S(1)}, bf16[1,1,384,512]{3,2,1,0:T(8,128)(2,1)S(1)}, u32[]{:S(2)}, u32[]{:S(2)}) collective-permute-start(bf16[1,1,384,512]{3,2,1,0:T(8,128)(2,1)S(1)} %copy-done.9), channel_id=1, source_target_pairs={{0,16},{4,20},{8,24},{12,28},{16,0},{20,4},{24,8},{28,12},{1,17},{... | collective-permute-start | bytes 1179656 | tf_op jit(solution)/shard_map/ppermute | solution.py:353
  155.2 1.0 copy-start.4
  155.2 28.0 %collective-permute-start.12 = (bf16[1,1,384,512]{3,2,1,0:T(8,128)(2,1)S(1)}, bf16[1,1,384,512]{3,2,1,0:T(8,128)(2,1)S(1)}, u32[]{:S(2)}, u32[]{:S(2)}) collective-permute-start(bf16[1,1,384,512]{3,2,1,0:T(8,128)(2,1)S(1)} %copy-done.9), channel_id=1, source_target_pairs={{0,8},{4,12},{8,0},{12,4},{16,24},{20,28},{24,16},{28,20},{1,9},{5... | collective-permute-start | bytes 1179656 | tf_op jit(solution)/shard_map/ppermute | solution.py:353
  165.6 1.0 copy-start.2
  165.6 8.2 %copy-start.1 = (f32[4,9]{1,0:T(4,128)S(1)}, f32[4,9]{1,0:T(4,128)}, u32[]{:S(2)}) copy-start(f32[4,9]{1,0:T(4,128)} %pad_maximum_fusion.coef_ref._) | copy-start | bytes 436
  165.6 22.2 %collective-permute-start.13 = (bf16[1,1,128,512]{3,2,1,0:T(8,128)(2,1)S(1)}, bf16[1,1,128,512]{3,2,1,0:T(8,128)(2,1)S(1)}, u32[]{:S(2)}, u32[]{:S(2)}) collective-permute-start(bf16[1,1,128,512]{3,2,1,0:T(8,128)(2,1)S(1)} %copy-done.10), channel_id=1, source_target_pairs={{0,16},{4,20},{8,24},{12,28},{16,0},{20,4},{24,8},{28,12},{1,17},{... | collective-permute-start | bytes 393224 | tf_op jit(solution)/shard_map/ppermute | solution.py:353
  172.7 15.1 %collective-permute-start.14 = (bf16[1,1,128,512]{3,2,1,0:T(8,128)(2,1)S(1)}, bf16[1,1,128,512]{3,2,1,0:T(8,128)(2,1)S(1)}, u32[]{:S(2)}, u32[]{:S(2)}) collective-permute-start(bf16[1,1,128,512]{3,2,1,0:T(8,128)(2,1)S(1)} %copy-done.10), channel_id=1, source_target_pairs={{0,8},{4,12},{8,0},{12,4},{16,24},{20,28},{24,16},{28,20},{1,9},{5... | collective-permute-start | bytes 393224 | tf_op jit(solution)/shard_map/ppermute | solution.py:353
